TPU v7x, 256 devices: a whole 4x4x8 slice. The times are simulated.
256 devices in a mesh: ctx: 16 (over x, z_lo, core), head: 16 (over z_hi, y).
Axes of the slice: x: 4, y: 4, z: 8 (z_hi: 4, z_lo: 2; z = z_hi * 2 + z_lo), core: 2. Of those that a mesh axis runs over, the one named last changes fastest.
Arguments:
- queries: bfloat16 [16384, 8192], P(('ctx', 'head')), may hold values from -13.5 to 13.5
- span_keys: bfloat16 [16384, 1024], P(('ctx', 'head')), may hold values from -13.5 to 13.5
- span_values: bfloat16 [16384, 1024], P(('ctx', 'head')), may hold values from -4 to 4
- cache_keys: bfloat16 [16384, 1024], P('ctx'), may hold values from -4 to 4
- cache_values: bfloat16 [16384, 1024], P('ctx'), may hold values from -4 to 4
- verticals: int32 [64, 16, 1], P('head'), may hold values from 0 to 15
- slashes: int32 [64, 3], P('head'), may hold values from 1 to 255
Outputs:
- attended: bfloat16 [16384, 8192], P(('ctx', 'head'))
All inputs are finite; a program needn't handle non-finite values.
Results may differ from a plain program's by a relative error of at most 0.009.
Values may be sent and summed in bfloat16 or wider, within the bound.
No kernel may reach another device: no remote copies, remote signals or barrier semaphores. Data moves between devices by JAX's collectives and lax.ppermute only.
A program may use at most 128 MiB of HBM per device.

v0:
```python
import jax
import jax.numpy as jnp
from jax import lax
from jax.sharding import PartitionSpec as P

H = 64
KVH = 8
DH = 128
BLK = 128


masked_score = -1e30


def block_place(target, cache_blocks, shard_cache, shard_span):
    bounded_index = jnp.maximum(target, 0)
    span_part = jnp.maximum(bounded_index - cache_blocks, 0)
    in_cache = bounded_index < cache_blocks
    shard_of = jnp.where(in_cache, bounded_index // shard_cache, span_part // shard_span)
    inside_range = jnp.where(
        in_cache, bounded_index % shard_cache, shard_cache + span_part % shard_span
    )
    return (shard_of, inside_range)


def block_absolute(shard_of, inside_range, cache_blocks, shard_cache, shard_span):
    return jnp.where(
        inside_range < shard_cache,
        shard_of * shard_cache + inside_range,
        cache_blocks + shard_of * shard_span + inside_range - shard_cache,
    )


def keep_first(absolute, usable):
    position = jnp.arange(absolute.shape[-1], dtype=jnp.int32)
    earlier = position[None, :] < position[:, None]
    repeated = (absolute[..., :, None] == absolute[..., None, :]) & usable[..., None, :] & earlier
    return usable & jnp.logical_not(jnp.any(repeated, axis=-1))


def attend(partial_value, flat_queries, blocks, picked, absolute, usable, row_blocks):
    running_max, running_sum, summed = partial_value
    chosen = jnp.take(blocks, picked, axis=0)
    key_rows = chosen[:, :, :, 0, :]
    value_rows = chosen[:, :, :, 1, :]
    inside_range = jnp.arange(BLK, dtype=jnp.int32)
    key_pos = absolute[:, :, None] * BLK + inside_range
    query_pos = row_blocks[:, None] * BLK + inside_range
    allowed = usable[:, None, :, None] & (key_pos[:, None, :, :] <= query_pos[:, :, None, None])
    logit_matrix = jnp.einsum(
        "rqd,rckd->rqck", flat_queries, key_rows, preferred_element_type=jnp.float32
    ) * DH ** (-0.5)
    logit_matrix = jnp.where(allowed, logit_matrix, masked_score)
    new_max = jnp.maximum(running_max, jnp.max(logit_matrix, axis=(2, 3)))
    weights = jnp.where(allowed, jnp.exp(logit_matrix - new_max[:, :, None, None]), 0.0)
    rescale = jnp.exp(running_max - new_max)
    running_sum = running_sum * rescale + jnp.sum(weights, axis=(2, 3))
    summed = summed * rescale[:, :, None] + jnp.einsum(
        "rqck,rckd->rqd",
        weights.astype(jnp.bfloat16),
        value_rows,
        preferred_element_type=jnp.float32,
    )
    return (new_max, running_sum, summed)


def per_device(queries, span_keys, span_values, cache_keys, cache_values, verticals, slashes):
    head_count = lax.axis_size("head")
    cycle_count = lax.axis_size("ctx")
    head_index = lax.axis_index("head")
    cycle_index = lax.axis_index("ctx")
    local_heads = H // head_count
    group_size = head_count // KVH
    span_rows = queries.shape[0]
    slab_rows = span_rows * head_count
    keys_spread = jnp.repeat(span_keys.reshape(span_rows, KVH, DH), group_size, axis=1)
    values_spread = jnp.repeat(span_values.reshape(span_rows, KVH, DH), group_size, axis=1)
    outgoing = jnp.concatenate(
        [queries.reshape(span_rows, head_count, local_heads * DH), keys_spread, values_spread],
        axis=2,
    ).reshape(span_rows, head_count * (local_heads + 2) * DH)
    arrived = lax.all_to_all(outgoing, "head", split_axis=1, concat_axis=0, tiled=True)
    slab_queries = arrived[:, : local_heads * DH].reshape(slab_rows, local_heads, DH)
    slab_keys = arrived[:, local_heads * DH : (local_heads + 1) * DH]
    slab_values = arrived[:, (local_heads + 1) * DH :]
    kv_start = head_index // group_size * DH
    own_keys = lax.dynamic_slice_in_dim(cache_keys, kv_start, DH, 1)
    own_values = lax.dynamic_slice_in_dim(cache_values, kv_start, DH, 1)
    held_cache = jnp.stack([own_keys, own_values], axis=1)
    payload = jnp.concatenate([held_cache, jnp.stack([slab_keys, slab_values], axis=1)], axis=0)
    shard_cache = cache_keys.shape[0] // BLK
    shard_span = slab_rows // BLK
    cache_blocks = shard_cache * cycle_count
    shard_blocks = shard_cache + shard_span
    query_blocks = cache_blocks + cycle_index * shard_span + jnp.arange(shard_span, dtype=jnp.int32)
    offsets = jnp.concatenate([jnp.zeros((local_heads, 1), jnp.int32), slashes], axis=1)
    targets = query_blocks[None, :, None] - offsets[:, None, :]
    slash_shard, slash_within = block_place(targets, cache_blocks, shard_cache, shard_span)
    slash_usable = targets >= 0
    row_count = local_heads * shard_span
    flat_queries = (
        slab_queries.reshape(shard_span, BLK, local_heads, DH)
        .transpose(2, 0, 1, 3)
        .reshape(row_count, BLK, DH)
    )
    row_blocks = jnp.broadcast_to(query_blocks[None, :], (local_heads, shard_span)).reshape(
        row_count
    )
    initial = (
        jnp.full((row_count, BLK), masked_score, jnp.float32),
        jnp.zeros((row_count, BLK), jnp.float32),
        jnp.zeros((row_count, BLK, DH), jnp.float32),
    )
    gathered = lax.all_gather(payload, "ctx", axis=0, tiled=True)
    blocks = gathered.reshape(cycle_count * shard_blocks, BLK, 2, DH)
    shard_ids = jnp.arange(cycle_count, dtype=jnp.int32)[None, :, None]
    vertical_abs = block_absolute(
        shard_ids, verticals, cache_blocks, shard_cache, shard_span
    ).reshape(local_heads, 1, -1)
    vertical_pick = (shard_ids * shard_blocks + verticals).reshape(local_heads, 1, -1)
    listed = (local_heads, shard_span, vertical_pick.shape[2])
    picked = jnp.concatenate(
        [jnp.broadcast_to(vertical_pick, listed), slash_shard * shard_blocks + slash_within], axis=2
    )
    absolute = jnp.concatenate([jnp.broadcast_to(vertical_abs, listed), targets], axis=2)
    usable = jnp.concatenate([jnp.ones(listed, bool), slash_usable], axis=2)
    usable = keep_first(absolute, usable)
    head_initial = jax.tree.map(
        lambda leaf: leaf.reshape((local_heads, shard_span) + leaf.shape[1:]), initial
    )

    def per_head(element):
        start_value, head_queries, head_picked, head_absolute, head_usable, head_rows = element
        return attend(
            start_value, head_queries, blocks, head_picked, head_absolute, head_usable, head_rows
        )

    per_head_result = lax.map(
        per_head,
        (
            head_initial,
            flat_queries.reshape(local_heads, shard_span, BLK, DH),
            picked,
            absolute,
            usable,
            row_blocks.reshape(local_heads, shard_span),
        ),
    )
    partial_value = jax.tree.map(
        lambda leaf: leaf.reshape((row_count,) + leaf.shape[2:]), per_head_result
    )
    running_max, running_sum, summed = partial_value
    result = (summed / running_sum[:, :, None]).astype(jnp.bfloat16)
    result = (
        result.reshape(local_heads, shard_span, BLK, DH)
        .transpose(1, 2, 0, 3)
        .reshape(slab_rows, local_heads * DH)
    )
    return lax.all_to_all(result, "head", split_axis=0, concat_axis=1, tiled=True)


def solution(mesh):
    return jax.shard_map(
        per_device,
        mesh=mesh,
        in_specs=(
            P(("ctx", "head"), None),
            P(("ctx", "head"), None),
            P(("ctx", "head"), None),
            P("ctx", None),
            P("ctx", None),
            P("head", None, None),
            P("head", None),
        ),
        out_specs=P(("ctx", "head"), None),
        check_vma=False,
    )
```

profile of v0, /device:TPU:32, one launch (start us, length us, event | category | flops | bytes accessed | tf_op | source)
XLA Modules:
  0.0 489.2 jit_solution(13415739974619607048)
XLA Ops:
  6.5 0.9 copy-done
  7.5 0.9 copy_bitcast_fusion.3
  8.4 1.3 copy.60
  9.8 1.3 pad_maximum_fusion
  11.1 10.3 %all-to-all-start = ((bf16[64,16,768]{2,0,1:T(8,128)(2,1)}), bf16[64,16,768]{2,0,1:T(8,128)(2,1)S(1)}, u32[]{:S(2)}, u32[]{:S(2)}) async-start(bf16[64,16,768]{2,0,1:T(8,128)(2,1)} %pad_maximum_fusion), calls=%async_computation | async-start | bytes 3145728 | tf_op jit(solution)/shard_map/all_to_all | solution.py:82
  21.5 1.1 dynamic-slice_bitcast_fusion.1
  22.6 39.3 %all-to-all-done = bf16[64,16,768]{2,0,1:T(8,128)(2,1)S(1)} async-done(((bf16[64,16,768]{2,0,1:T(8,128)(2,1)}), bf16[64,16,768]{2,0,1:T(8,128)(2,1)S(1)}, u32[]{:S(2)}, u32[]{:S(2)}) %all-to-all-start) | async-done | bytes 1572896 | tf_op jit(solution)/shard_map/all_to_all | solution.py:82
  62.0 1.0 maximum_maximum_fusion
  63.1 0.1 fusion.28
  63.2 0.1 copy.33
  63.5 0.1 copy.34
  63.6 0.1 copy.59
  63.8 1.6 and_reduce_fusion
  65.4 0.1 copy.41
  65.8 0.3 reshape.216
  66.1 0.2 copy.61
  66.3 87.7 %all-gather.2.cloned.1.call-done = bf16[32768,2,128]{2,0,1:T(8,128)(2,1)} async-done(((bf16[2048,2,128]{2,0,1:T(8,128)(2,1)}), bf16[32768,2,128]{2,0,1:T(8,128)(2,1)}) %all-gather.2.cloned.1.call-update) | async-done | bytes 16777232 | tf_op jit(solution)/shard_map/all_gather | solution.py:114
  154.0 31.1 %copy.43 = bf16[256,128,2,128]{3,2,1,0:T(2,128)(2,1)} copy(bf16[256,128,2,128]{3,1,0,2:T(8,128)(2,1)} %bitcast.118) | data formatting | bytes 33554432 | tf_op jit(solution)/shard_map/while | solution.py:138
  185.1 259.3 %while.12 = (s32[]{:T(128)}, f32[4,8,128]{2,1,0:T(8,128)S(1)}, f32[4,8,128,128]{3,2,1,0:T(8,128)S(1)}, pred[4,8,20]{2,1,0:T(8,128)(4,1)S(1)}, s32[4,8,20]{2,1,0:...) while((s32[]{:T(128)}, f32[4,8,128]{2,1,0:T(8,128)S(1)}, ...), condition=%wide.region_4.5_spmd, body=%wide.region_1.4_spmd.sunk | while | flops 1397387776 | bytes 106079496 | solution.py:138
  185.4 30.1 %gather_fusion = bf16[160,128,2,128]{3,2,1,0:T(2,128)(2,1)} fusion(bf16[256,128,2,128]{3,2,1,0:T(2,128)(2,1)} %get-tuple-element.205, s32[1024]{0:T(1024)S(1)} %pad_clamp_fusion.2), kind=kCustom, calls=%fused_computation.clone.1 | custom fusion | bytes 20972160 | tf_op jit(solution)/shard_map/while/body/eval_jaxpr/jit(_take)/gather | solution.py:43
  215.5 10.8 %copy.63 = bf16[160,128,2,128]{3,1,0,2:T(8,128)(2,1)} copy(bf16[160,128,2,128]{3,2,1,0:T(2,128)(2,1)} %gather_fusion) | data formatting | bytes 20971520 | tf_op jit(solution)/shard_map/while/body/eval_jaxpr/jit(_take)/gather | solution.py:43
  226.3 5.8 %broadcast_select_fusion.2 = bf16[8,20,128,2,128]{4,2,1,0,3:T(8,128)(2,1)S(1)} fusion(bf16[8,20,128,2,128]{4,2,1,0,3:T(8,128)(2,1)} %bitcast.117, pred[8,20]{1,0:T(8,128)(4,1)S(1)} %compare_and_fusion.3), kind=kLoop, calls=%fused_computation.3.clone.1 | loop fusion | flops 5242880 | bytes 20971680 | tf_op jit(solution)/shard_map/while/body/eval_jaxpr/jit(_take)/select_n | solution.py:43
  232.1 4.0 fusion.44
  236.2 5.8 %fusion.45 = f32[8,128]{1,0:T(8,128)S(1)} fusion(f32[8,128]{1,0:T(8,128)S(1)} %get-tuple-element.174, f32[8,128,20,128]{1,3,2,0:T(8,128)S(1)} %get-tuple-element.175, s32[8,128]{1,0:T(8,128)S(1)} %iota_add_fusion.5, s32[8,20,128]{2,1,0:T(8,128)S(1)} %iota_add_fusion.6, pred[8,20]{1,0:T(8,128)(4,1)S(1)} %dynamic-slice_bitcast_fusion.4), kind=kLoop, calls=%fused_computation.11.clone.1 | loop fusion | flops 18349056 | bytes 10580128 | tf_op jit(solution)/shard_map/while/body/eval_jaxpr/reduce_sum | solution.py:57
  242.0 7.9 %fusion.46 = f32[4,8,128,128]{3,2,1,0:T(8,128)S(1)} fusion(f32[4,8,128,128]{3,2,1,0:T(8,128)S(1)} %get-tuple-element.189, s32[]{:T(128)S(6)} %copy.69, bf16[8,20,128,2,128]{4,2,1,0,3:T(8,128)(2,1)S(1)} %broadcast_select_fusion.2, f32[8,128]{1,0:T(8,128)S(1)} %get-tuple-element.174, f32[8,128,20,128]{1,3,2,0:T(8,128)S(1)} %get-tuple-element.175, ...), kind=kOutput, calls=%fused_computation.15.clone.1 | convolution fusion | flops 689569792 | bytes 16364548 | tf_op jit(solution)/shard_map/while/body/eval_jaxpr/rqck,rckd->rqd/dot_general | solution.py:58
  250.3 30.1 %gather_fusion = bf16[160,128,2,128]{3,2,1,0:T(2,128)(2,1)} fusion(bf16[256,128,2,128]{3,2,1,0:T(2,128)(2,1)} %get-tuple-element.205, s32[1024]{0:T(1024)S(1)} %pad_clamp_fusion.2), kind=kCustom, calls=%fused_computation.clone.1 | custom fusion | bytes 20972160 | tf_op jit(solution)/shard_map/while/body/eval_jaxpr/jit(_take)/gather | solution.py:43
  280.4 10.8 %copy.63 = bf16[160,128,2,128]{3,1,0,2:T(8,128)(2,1)} copy(bf16[160,128,2,128]{3,2,1,0:T(2,128)(2,1)} %gather_fusion) | data formatting | bytes 20971520 | tf_op jit(solution)/shard_map/while/body/eval_jaxpr/jit(_take)/gather | solution.py:43
  291.2 5.8 %broadcast_select_fusion.2 = bf16[8,20,128,2,128]{4,2,1,0,3:T(8,128)(2,1)S(1)} fusion(bf16[8,20,128,2,128]{4,2,1,0,3:T(8,128)(2,1)} %bitcast.117, pred[8,20]{1,0:T(8,128)(4,1)S(1)} %compare_and_fusion.3), kind=kLoop, calls=%fused_computation.3.clone.1 | loop fusion | flops 5242880 | bytes 20971680 | tf_op jit(solution)/shard_map/while/body/eval_jaxpr/jit(_take)/select_n | solution.py:43
  297.0 4.0 fusion.44
  301.0 5.8 %fusion.45 = f32[8,128]{1,0:T(8,128)S(1)} fusion(f32[8,128]{1,0:T(8,128)S(1)} %get-tuple-element.174, f32[8,128,20,128]{1,3,2,0:T(8,128)S(1)} %get-tuple-element.175, s32[8,128]{1,0:T(8,128)S(1)} %iota_add_fusion.5, s32[8,20,128]{2,1,0:T(8,128)S(1)} %iota_add_fusion.6, pred[8,20]{1,0:T(8,128)(4,1)S(1)} %dynamic-slice_bitcast_fusion.4), kind=kLoop, calls=%fused_computation.11.clone.1 | loop fusion | flops 18349056 | bytes 10580128 | tf_op jit(solution)/shard_map/while/body/eval_jaxpr/reduce_sum | solution.py:57
  306.8 7.9 %fusion.46 = f32[4,8,128,128]{3,2,1,0:T(8,128)S(1)} fusion(f32[4,8,128,128]{3,2,1,0:T(8,128)S(1)} %get-tuple-element.189, s32[]{:T(128)S(6)} %copy.69, bf16[8,20,128,2,128]{4,2,1,0,3:T(8,128)(2,1)S(1)} %broadcast_select_fusion.2, f32[8,128]{1,0:T(8,128)S(1)} %get-tuple-element.174, f32[8,128,20,128]{1,3,2,0:T(8,128)S(1)} %get-tuple-element.175, ...), kind=kOutput, calls=%fused_computation.15.clone.1 | convolution fusion | flops 689569792 | bytes 16364548 | tf_op jit(solution)/shard_map/while/body/eval_jaxpr/rqck,rckd->rqd/dot_general | solution.py:58
  315.1 30.1 %gather_fusion = bf16[160,128,2,128]{3,2,1,0:T(2,128)(2,1)} fusion(bf16[256,128,2,128]{3,2,1,0:T(2,128)(2,1)} %get-tuple-element.205, s32[1024]{0:T(1024)S(1)} %pad_clamp_fusion.2), kind=kCustom, calls=%fused_computation.clone.1 | custom fusion | bytes 20972160 | tf_op jit(solution)/shard_map/while/body/eval_jaxpr/jit(_take)/gather | solution.py:43
  345.2 10.8 %copy.63 = bf16[160,128,2,128]{3,1,0,2:T(8,128)(2,1)} copy(bf16[160,128,2,128]{3,2,1,0:T(2,128)(2,1)} %gather_fusion) | data formatting | bytes 20971520 | tf_op jit(solution)/shard_map/while/body/eval_jaxpr/jit(_take)/gather | solution.py:43
  356.0 5.8 %broadcast_select_fusion.2 = bf16[8,20,128,2,128]{4,2,1,0,3:T(8,128)(2,1)S(1)} fusion(bf16[8,20,128,2,128]{4,2,1,0,3:T(8,128)(2,1)} %bitcast.117, pred[8,20]{1,0:T(8,128)(4,1)S(1)} %compare_and_fusion.3), kind=kLoop, calls=%fused_computation.3.clone.1 | loop fusion | flops 5242880 | bytes 20971680 | tf_op jit(solution)/shard_map/while/body/eval_jaxpr/jit(_take)/select_n | solution.py:43
  361.8 4.0 fusion.44
  365.8 5.8 %fusion.45 = f32[8,128]{1,0:T(8,128)S(1)} fusion(f32[8,128]{1,0:T(8,128)S(1)} %get-tuple-element.174, f32[8,128,20,128]{1,3,2,0:T(8,128)S(1)} %get-tuple-element.175, s32[8,128]{1,0:T(8,128)S(1)} %iota_add_fusion.5, s32[8,20,128]{2,1,0:T(8,128)S(1)} %iota_add_fusion.6, pred[8,20]{1,0:T(8,128)(4,1)S(1)} %dynamic-slice_bitcast_fusion.4), kind=kLoop, calls=%fused_computation.11.clone.1 | loop fusion | flops 18349056 | bytes 10580128 | tf_op jit(solution)/shard_map/while/body/eval_jaxpr/reduce_sum | solution.py:57
  371.7 7.9 %fusion.46 = f32[4,8,128,128]{3,2,1,0:T(8,128)S(1)} fusion(f32[4,8,128,128]{3,2,1,0:T(8,128)S(1)} %get-tuple-element.189, s32[]{:T(128)S(6)} %copy.69, bf16[8,20,128,2,128]{4,2,1,0,3:T(8,128)(2,1)S(1)} %broadcast_select_fusion.2, f32[8,128]{1,0:T(8,128)S(1)} %get-tuple-element.174, f32[8,128,20,128]{1,3,2,0:T(8,128)S(1)} %get-tuple-element.175, ...), kind=kOutput, calls=%fused_computation.15.clone.1 | convolution fusion | flops 689569792 | bytes 16364548 | tf_op jit(solution)/shard_map/while/body/eval_jaxpr/rqck,rckd->rqd/dot_general | solution.py:58
  379.9 30.1 %gather_fusion = bf16[160,128,2,128]{3,2,1,0:T(2,128)(2,1)} fusion(bf16[256,128,2,128]{3,2,1,0:T(2,128)(2,1)} %get-tuple-element.205, s32[1024]{0:T(1024)S(1)} %pad_clamp_fusion.2), kind=kCustom, calls=%fused_computation.clone.1 | custom fusion | bytes 20972160 | tf_op jit(solution)/shard_map/while/body/eval_jaxpr/jit(_take)/gather | solution.py:43
  410.0 10.8 %copy.63 = bf16[160,128,2,128]{3,1,0,2:T(8,128)(2,1)} copy(bf16[160,128,2,128]{3,2,1,0:T(2,128)(2,1)} %gather_fusion) | data formatting | bytes 20971520 | tf_op jit(solution)/shard_map/while/body/eval_jaxpr/jit(_take)/gather | solution.py:43
  420.8 5.8 %broadcast_select_fusion.2 = bf16[8,20,128,2,128]{4,2,1,0,3:T(8,128)(2,1)S(1)} fusion(bf16[8,20,128,2,128]{4,2,1,0,3:T(8,128)(2,1)} %bitcast.117, pred[8,20]{1,0:T(8,128)(4,1)S(1)} %compare_and_fusion.3), kind=kLoop, calls=%fused_computation.3.clone.1 | loop fusion | flops 5242880 | bytes 20971680 | tf_op jit(solution)/shard_map/while/body/eval_jaxpr/jit(_take)/select_n | solution.py:43
  426.6 4.0 fusion.44
  430.7 5.8 %fusion.45 = f32[8,128]{1,0:T(8,128)S(1)} fusion(f32[8,128]{1,0:T(8,128)S(1)} %get-tuple-element.174, f32[8,128,20,128]{1,3,2,0:T(8,128)S(1)} %get-tuple-element.175, s32[8,128]{1,0:T(8,128)S(1)} %iota_add_fusion.5, s32[8,20,128]{2,1,0:T(8,128)S(1)} %iota_add_fusion.6, pred[8,20]{1,0:T(8,128)(4,1)S(1)} %dynamic-slice_bitcast_fusion.4), kind=kLoop, calls=%fused_computation.11.clone.1 | loop fusion | flops 18349056 | bytes 10580128 | tf_op jit(solution)/shard_map/while/body/eval_jaxpr/reduce_sum | solution.py:57
  436.5 7.9 %fusion.46 = f32[4,8,128,128]{3,2,1,0:T(8,128)S(1)} fusion(f32[4,8,128,128]{3,2,1,0:T(8,128)S(1)} %get-tuple-element.189, s32[]{:T(128)S(6)} %copy.69, bf16[8,20,128,2,128]{4,2,1,0,3:T(8,128)(2,1)S(1)} %broadcast_select_fusion.2, f32[8,128]{1,0:T(8,128)S(1)} %get-tuple-element.174, f32[8,128,20,128]{1,3,2,0:T(8,128)S(1)} %get-tuple-element.175, ...), kind=kOutput, calls=%fused_computation.15.clone.1 | convolution fusion | flops 689569792 | bytes 16364548 | tf_op jit(solution)/shard_map/while/body/eval_jaxpr/rqck,rckd->rqd/dot_general | solution.py:58
  444.5 0.7 fusion.25
  445.2 0.8 copy.44
  446.0 0.4 all_to_all.29
  446.5 34.8 %all_to_all.35 = bf16[16,64,512]{2,1,0:T(8,128)(2,1)S(1)} all-to-all(bf16[16,64,512]{2,1,0:T(8,128)(2,1)S(1)} %all_to_all.29), channel_id=1, replica_groups=mesh['ctx'=16,'head'=16] {'head'}, dimensions={0} | all-to-all | bytes 2097152 | tf_op jit(solution)/shard_map/all_to_all | solution.py:159
  481.3 1.1 copy.54
  (77 shorter events, 2.1 us)
Async XLA Ops:
  6.5 0.9 copy-start
  6.5 56.5 %copy-start.3 = (s32[4,3]{1,0:T(4,128)S(1)}, s32[4,3]{1,0:T(4,128)}, u32[]{:S(2)}) copy-start(s32[4,3]{1,0:T(4,128)} %param.15) | copy-start | bytes 148
  7.4 55.9 %copy-start.4 = (s32[4,16,1]{1,2,0:T(1,128)S(1)}, s32[4,16,1]{1,2,0:T(1,128)}, u32[]{:S(2)}) copy-start(s32[4,16,1]{1,2,0:T(1,128)} %param.14) | copy-start | bytes 772
  11.1 50.8 %all-to-all-start = ((bf16[64,16,768]{2,0,1:T(8,128)(2,1)}), bf16[64,16,768]{2,0,1:T(8,128)(2,1)S(1)}, u32[]{:S(2)}, u32[]{:S(2)}) async-start(bf16[64,16,768]{2,0,1:T(8,128)(2,1)} %pad_maximum_fusion), calls=%async_computation | async-start | bytes 3145728 | tf_op jit(solution)/shard_map/all_to_all | solution.py:82
  21.5 132.6 %all-gather.2.cloned.1.call-start = ((), (), s32[]{:S(2)}) async-start(), calls=%async_computation.2 | async-start | bytes 17825792 | tf_op jit(solution)/shard_map/all_gather | solution.py:114
  154.0 31.1 %copy-start.2 = (f32[4,8,128,128]{3,2,1,0:T(8,128)S(1)}, f32[4,8,128,128]{3,2,1,0:T(8,128)}, u32[]{:S(2)}) copy-start(f32[4,8,128,128]{3,2,1,0:T(8,128)} %custom-call.3) | copy-start | bytes 6291460
  444.4 37.9 %copy-start.1 = (bf16[64,1024]{1,0:T(8,128)(2,1)S(1)}, bf16[64,1024]{1,0:T(8,128)(2,1)}, u32[]{:S(2)}) copy-start(bf16[64,1024]{1,0:T(8,128)(2,1)} %param.11) | copy-start | bytes 393220
Sparse Core Ops, SparseCore 0:
  63.2 90.8 all-gather.1
where the time goes:
time: 494 us; the launch traced here: 489 us
  local copies, waits for them, and re-layouts  203 us (41%)
  waiting for transfers between devices  127 us (26%)
  other arithmetic  52.1 us (11%)
  matrix products  47.9 us (10%)
  blocking collectives  34.8 us (7%)
  between operations  13.6 us (3%)
  starting transfers between devices  10.3 us (2%)
    gather x8, local copies, waits for them, and re-layouts, attend(): chosen = jnp.take(blocks, picked, axis=0)  164 us
    all_gather x1, waiting for transfers between devices, per_device(): gathered = lax.all_gather(payload, 'ctx', axis=0, tiled=True)  87.7 us
    all_to_all x1, waiting for transfers between devices, per_device(): lax.all_to_all(outgoing, 'head', split_axis=1, concat_axis=0, tiled=True)  39.3 us
    all_to_all x1, blocking collectives, per_device(): lax.all_to_all(result, 'head', split_axis=0, concat_axis=1, tiled=True)  34.8 us
    dot_general x4, matrix products, attend(): jnp.einsum('rqck,rckd->rqd', weights.astype(jnp.bfloat16), value_rows, pr...  31.7 us
    while x2, local copies, waits for them, and re-layouts, per_device(): lax.map(per_head, (head_initial, flat_queries.reshape(local_heads, shard_...  31.2 us
    select_n x8, other arithmetic, attend(): chosen = jnp.take(blocks, picked, axis=0)  23.2 us
    reduce_sum x4, other arithmetic, attend(): running_sum = running_sum * rescale + jnp.sum(weights, axis=(2, 3))  23.2 us
  transfers between devices with their start and end apart: 2, of which 2 were waited for; matrix products, arithmetic and copies ran while one was open for 1% of the time, Pallas kernels for 0%

commit v1 on v0

v1 whole, which is shorter than its diff:
```python
import functools

import jax
import jax.numpy as jnp
import numpy as np
from jax import lax
from jax.experimental import pallas as pl
from jax.experimental.pallas import tpu as pltpu
from jax.sharding import Mesh
from jax.sharding import PartitionSpec as P

H = 64
KVH = 8
DH = 128
BLK = 128
GROUP = H // KVH
HALF = 64
NLIST = 20
GRP = 4
masked_score = -1e30
SCALE = DH ** (-0.5) * 1.4426950408889634


def shift(value, axis, size, step):
    return lax.ppermute(value, axis, [(i, (i + step) % size) for i in range(size)])


def ring_direct(value, axis):
    return [value, shift(value, axis, 4, 1), shift(value, axis, 4, -1), shift(value, axis, 4, 2)]


ORIGINS = (0, -1, 1, 2)
PLANES = (0, 2, 4, 6, 1, 3, 5, 7)


HBM = pl.BlockSpec(memory_space=pl.ANY)
SMEM = pl.BlockSpec(memory_space=pltpu.SMEM)
VMEM = pl.BlockSpec(memory_space=pltpu.VMEM)


def shaped(shape, dtype=jnp.bfloat16):
    return jax.ShapeDtypeStruct(shape, dtype)


def payload_kernel(place, cache_keys, cache_values, span_keys, span_values, own, other, span, sems):
    start = pl.multiple_of(place[1] * 256, 256)
    plane, near = place[3], place[4]
    copies = []
    for i, cache in enumerate((cache_keys, cache_values)):
        for j, (target, column) in enumerate(((own, plane), (other, near))):
            lanes = pl.ds(pl.multiple_of(column * DH, DH), DH)
            copies.append(
                pltpu.make_async_copy(cache.at[pl.ds(start, 256), lanes], target.at[i], sems.at[2 * i + j])
            )
    for copy in copies:
        copy.start()
    for i, source in enumerate((span_keys, span_values)):
        for slot, p in enumerate(PLANES):
            span[slot, i] = source[:, p * DH : (p + 1) * DH]
    for copy in copies:
        copy.wait()


def payload(place, cache_keys, cache_values, span_keys, span_values):
    return pl.pallas_call(
        payload_kernel,
        out_shape=[shaped((2, 256, DH)), shaped((2, 256, DH)), shaped((8, 2, HALF, DH))],
        in_specs=[SMEM, HBM, HBM, VMEM, VMEM],
        out_specs=[VMEM, VMEM, VMEM],
        scratch_shapes=[pltpu.SemaphoreType.DMA((4,))],
        name="payload",
    )(place, cache_keys, cache_values, span_keys, span_values)


def merge_kernel(extra, place, own, swapped, *refs):
    zl = place[5]
    for i, target in enumerate(refs[extra:]):
        target[zl] = own[i]
        target[1 - zl] = swapped[i]


def merge(place, own, swapped, after=()):
    return pl.pallas_call(
        functools.partial(merge_kernel, len(after)),
        out_shape=[shaped((2, 256, DH))] * 2,
        in_specs=[SMEM, VMEM, VMEM] + [HBM] * len(after),
        out_specs=[VMEM, VMEM],
        name="merge",
    )(place, own, swapped, *after)


def stack_kernel(*refs):
    for i, source in enumerate(refs[:8]):
        refs[8 + i // 4][i % 4] = source[...]


def stack(keys, values):
    shape = (4,) + keys[0].shape
    return pl.pallas_call(
        stack_kernel,
        out_shape=[shaped(shape)] * 2,
        in_specs=[VMEM] * 8,
        out_specs=[VMEM, VMEM],
        name="stack",
    )(*keys, *values)


def plane_kernel(extra, source, *refs):
    target = refs[extra]
    width = GROUP * DH
    for slot, plane in enumerate(PLANES):
        target[slot] = source[:, plane * width : (plane + 1) * width]


def by_plane(queries, after=()):
    return pl.pallas_call(
        functools.partial(plane_kernel, len(after)),
        out_shape=shaped((8, HALF, GROUP * DH)),
        in_specs=[VMEM] + [HBM] * len(after),
        out_specs=VMEM,
        name="by_plane",
    )(queries, *after)


def second_stage(plan, arrays, slots, is_value):
    x_first = not is_value
    pieces = ring_direct(slots, "y" if x_first else "x")
    for array, origin in zip(pieces, ORIGINS):
        for other in range(2):
            plan.append((is_value, x_first, origin, other))
            arrays.append((shift(array, "k", 2, 1) if other else array).reshape(4, 2, 2, BLK, DH))
    return pieces


def attention_kernel(plan, place, picks, biases, q_ref, span_ref, *refs):
    pieces = refs[: len(plan)]
    out_ref, kbuf, vbuf, sems = refs[len(plan) :]
    my_x, my_y, my_k = place[0], place[1], place[2]
    copies = []

    def copy(source, target):
        copies.append(pltpu.make_async_copy(source, target, sems.at[len(copies)]))

    for piece, (is_value, x_first, origin, other) in zip(pieces, plan):
        buffer = vbuf if is_value else kbuf
        for slot, near in enumerate(ORIGINS):
            dx, dy = (near, origin) if x_first else (origin, near)
            from_x = lax.rem(my_x + (dx + 4), 4)
            from_y = lax.rem(my_y + (dy + 4), 4)
            from_k = 1 - my_k if other else my_k
            copy(piece.at[slot], buffer.at[0, from_x, :, from_k, from_y])
    for x in range(4):
        for k in range(2):
            for y in range(4):
                slot = (x * 2 + k) * 4 + y
                for is_value, buffer in enumerate((kbuf, vbuf)):
                    copy(
                        span_ref.at[pl.ds(2 * slot, 2), :, is_value],
                        buffer.at[1, x, :, k, :, y // 2, pl.ds(y % 2 * HALF, HALF), :],
                    )
    for entry in copies:
        entry.start()
    for entry in copies:
        entry.wait()

    keys = kbuf.reshape(256, BLK, DH)
    values = vbuf.reshape(256, BLK, DH)
    half = lax.rem(my_y, 2) * HALF
    rows = lax.broadcasted_iota(jnp.int32, (HALF, BLK), 0) + half
    cols = lax.broadcasted_iota(jnp.int32, (HALF, BLK), 1)
    triangle = cols <= rows
    dims = (((1,), (1,)), ((), ()))

    def step(item, carry):
        head = lax.div(item, 8 // GRP)
        part = lax.rem(item, 8 // GRP)
        lane = pl.ds(pl.multiple_of(head * DH, DH), DH)
        base = [(head * 8 + part * GRP + r) * NLIST for r in range(GRP)]
        q = [q_ref[part * GRP + r, :, lane] for r in range(GRP)]
        q_all = jnp.concatenate(q, axis=0)
        scores = [[] for _ in range(GRP)]

        def pick(ref, start, e):
            return jnp.concatenate([ref[picks[start + e]], ref[picks[start + e + 1]]], axis=0)

        def put(r, e, s):
            for d in range(2):
                block = s[:, d * BLK : (d + 1) * BLK]
                if e + d == 0:
                    block = jnp.where(triangle, block, masked_score)
                else:
                    block = block + biases[base[r] + e + d]
                scores[r].append(block)

        for e in range(0, 4, 2):
            for r in range(GRP):
                s = lax.dot_general(q[r], pick(keys, base[r], e), dims, preferred_element_type=jnp.float32)
                put(r, e, s)
        for e in range(4, NLIST, 2):
            s = lax.dot_general(q_all, pick(keys, base[0], e), dims, preferred_element_type=jnp.float32)
            for r in range(GRP):
                put(r, e, s[r * HALF : (r + 1) * HALF])
        weights = []
        inverse = []
        for r in range(GRP):
            top = functools.reduce(jnp.maximum, scores[r])
            top = jnp.max(top, axis=1, keepdims=True) * SCALE
            w = [jnp.exp2(s * SCALE - top) for s in scores[r]]
            total = jnp.sum(functools.reduce(jnp.add, w), axis=1, keepdims=True)
            inverse.append(1.0 / total)
            weights.append([a.astype(jnp.bfloat16) for a in w])
        summed = []
        for r in range(GRP):
            acc = jnp.zeros((HALF, DH), jnp.float32)
            for e in range(0, 4, 2):
                pair = jnp.concatenate(weights[r][e : e + 2], axis=1)
                acc = acc + jnp.dot(pair, pick(values, base[r], e), preferred_element_type=jnp.float32)
            summed.append(acc)
        acc = jnp.concatenate(summed, axis=0)
        for e in range(4, NLIST, 2):
            pair = jnp.concatenate(
                [jnp.concatenate(weights[r][e : e + 2], axis=1) for r in range(GRP)], axis=0
            )
            acc = acc + jnp.dot(pair, pick(values, base[0], e), preferred_element_type=jnp.float32)
        for r in range(GRP):
            result = acc[r * HALF : (r + 1) * HALF] * inverse[r]
            out_ref[part * GRP + r, :, lane] = result.astype(jnp.bfloat16)
        return carry

    lax.fori_loop(0, GROUP * 8 // GRP, step, 0)


def head_table(table, my_y, zl):
    around = jnp.stack(ring_direct(table, "y"))
    origins = (my_y + jnp.array([0, 3, 1, 2], jnp.int32)) % 4

    def of(wanted):
        return jnp.sum(jnp.where((origins == wanted)[:, None, None], around, 0), axis=0)

    return jnp.concatenate([of(2 * zl), of(2 * zl + 1)], axis=0)


def listed_blocks(table, my_x, my_y, my_k):
    verticals, slashes = table[:, :16], table[:, 16:]
    shard = jnp.arange(16, dtype=jnp.int32)
    vertical = shard * 8 + verticals + jnp.where(verticals >= 8, 120, 0)
    zl = jnp.arange(8, dtype=jnp.int32) // 4
    zh = jnp.arange(8, dtype=jnp.int32) % 4
    own = 128 + (my_x * 4 + zl * 2 + my_k) * 8 + zh * 2 + my_y // 2
    target = own[None, :, None] - slashes[:, None, :]
    before = jnp.arange(3)[None, :] < jnp.arange(3)[:, None]
    repeated = jnp.any((slashes[:, :, None] == slashes[:, None, :]) & before, axis=-1)
    listed = jnp.any(target[..., None] == vertical[:, None, None, :], axis=-1)
    slash_ok = (target >= 0) & jnp.logical_not(repeated[:, None, :]) & jnp.logical_not(listed)
    vertical_ok = vertical[:, None, :] < own[None, :, None]
    shape = (GROUP, 8, 1)
    picks = jnp.concatenate(
        [
            jnp.broadcast_to(own[None, :, None], shape),
            jnp.maximum(target, 0),
            jnp.broadcast_to(vertical[:, None, :], (GROUP, 8, 16)),
        ],
        axis=2,
    )
    usable = jnp.concatenate([jnp.ones(shape, bool), slash_ok, vertical_ok], axis=2)
    biases = jnp.where(usable, 0.0, masked_score).astype(jnp.float32)
    return picks.reshape(-1), biases.reshape(-1)


def per_device(queries, span_keys, span_values, cache_keys, cache_values, verticals, slashes):
    my_x, my_y, my_k = lax.axis_index("x"), lax.axis_index("y"), lax.axis_index("k")
    zh, zl = lax.axis_index("zh"), lax.axis_index("zl")
    plane = zh * 2 + zl
    zaxes = ("zl", "zh")

    table = jnp.concatenate([verticals[:, :, 0], slashes], axis=1)
    table = head_table(table, my_y, zl)

    place = jnp.stack([my_x, my_y, my_k, plane, plane + 1 - 2 * zl, zl]).astype(jnp.int32)
    own, other, span = payload(place, cache_keys, cache_values, span_keys, span_values)
    swapped = shift(other, "zl", 2, 1)
    span = lax.all_to_all(span, zaxes, split_axis=0, concat_axis=0, tiled=True)

    span = lax.all_gather(span, ("x", "k", "y"), axis=0, tiled=True)
    span = span.reshape(64, 4, 2, HALF, DH)

    plan = []
    arrays = []
    cache_k, cache_v = merge(place, own, swapped, (table,))
    cache_k, cache_v = stack(ring_direct(cache_k, "x"), ring_direct(cache_v, "y"))
    second_stage(plan, arrays, cache_k, False)
    second_stage(plan, arrays, cache_v, True)
    slab_queries = lax.all_to_all(
        by_plane(queries, (cache_k,)), zaxes, split_axis=0, concat_axis=0, tiled=True
    )

    picks, biases = listed_blocks(table, my_x, my_y, my_k)
    buffer = (2, 4, 2, 2, 4, 2, BLK, DH)
    attended = pl.pallas_call(
        functools.partial(attention_kernel, tuple(plan)),
        out_shape=jax.ShapeDtypeStruct((8, HALF, GROUP * DH), jnp.bfloat16),
        in_specs=[SMEM, SMEM, SMEM, VMEM] + [HBM] * (1 + len(arrays)),
        out_specs=VMEM,
        scratch_shapes=[
            pltpu.VMEM(buffer, jnp.bfloat16),
            pltpu.VMEM(buffer, jnp.bfloat16),
            pltpu.SemaphoreType.DMA((4 * len(arrays) + 64,)),
        ],
        compiler_params=pltpu.CompilerParams(vmem_limit_bytes=50 * 1024 * 1024),
        cost_estimate=pl.CostEstimate(
            flops=2 * 2 * 64 * 64 * 2560 * 128, bytes_accessed=18 << 20, transcendentals=10 << 20
        ),
        name="attention",
    )(place, picks, biases, slab_queries, span, *arrays)
    result = lax.all_to_all(attended, zaxes, split_axis=0, concat_axis=0, tiled=True)
    return jnp.concatenate([result[PLANES.index(p)] for p in range(8)], axis=1)


def solution(mesh):
    axes = ("x", "zl", "k", "zh", "y")
    fine = Mesh(np.asarray(mesh.devices).reshape(4, 2, 2, 4, 4), axes)
    rows = P(axes, None)
    return jax.shard_map(
        per_device,
        mesh=fine,
        in_specs=(
            rows,
            rows,
            rows,
            P(("x", "zl", "k"), None),
            P(("x", "zl", "k"), None),
            P(("zh", "y"), None, None),
            P(("zh", "y"), None),
        ),
        out_specs=rows,
        check_vma=False,
    )
```

time: 494 us -> 191 us (0.39)
  local copies, waits for them, and re-layouts: 203 us -> 4.32 us
  waiting for transfers between devices: 127 us -> 44.6 us
  other arithmetic: 52.1 us -> 1.88 us
  matrix products: 47.9 us -> 0 us
  Pallas kernels: 0 us -> 43.3 us
  blocking collectives: 34.8 us -> 53.9 us
  starting transfers between devices: 10.3 us -> 29.3 us
    gather x8 -> x0, local copies, waits for them, and re-layouts: 164 us -> none  [attend(): chosen = jnp.take(blocks, picked, axis=0)]
    all_gather x1, waiting for transfers between devices: 87.7 us -> 0.01 us  [per_device(): span = lax.all_gather(span, ('x', 'k', 'y'), axis=0, tiled=True)]
    dot_general x8 -> x0, matrix products: 47.9 us -> none  [the longest x4 31.7 us: attend(): jnp.einsum('rqck,rckd->rqd', weights.astype(jnp.bfloat16), value_rows, pr...]
    ppermute x0 -> x24, waiting for transfers between devices: none -> 44.6 us  [shift(): lax.ppermute(value, axis, [(i, (i + step) % size) for i in range(size)])]
    pallas_call x0 -> x5, Pallas kernels: none -> 43.3 us  [the longest x1 34.1 us: per_device(): pl.pallas_call(functools.partial(attention_kernel, tuple(plan)), out_shap...]
    all_to_all x1, waiting for transfers between devices: 39.3 us -> 0.01 us  [per_device(): lax.all_to_all(by_plane(queries, (cache_k,)), zaxes, split_axis=0, concat...]
    while x2 -> x0, local copies, waits for them, and re-layouts: 31.2 us -> none  [per_device(): lax.map(per_head, (head_initial, flat_queries.reshape(local_heads, shard_...]
    ppermute x0 -> x24, starting transfers between devices: none -> 24.8 us  [shift(): lax.ppermute(value, axis, [(i, (i + step) % size) for i in range(size)])]
  transfers between devices with their start and end apart: 2 -> 26, of which waited for: 2 -> 13; matrix products, arithmetic and copies ran while one was open for 1% -> 1% of each run, Pallas kernels for 0% -> 3%
where the time goes in v1:
time: 191 us
  blocking collectives  53.9 us (28%)
  waiting for transfers between devices  44.6 us (23%)
  Pallas kernels  43.3 us (23%)
  starting transfers between devices  29.3 us (15%)
  between operations  13.6 us (7%)
  local copies, waits for them, and re-layouts  4.32 us (2%)
    ppermute x24, waiting for transfers between devices, shift(): lax.ppermute(value, axis, [(i, (i + step) % size) for i in range(size)])  44.6 us
    all_to_all x1, blocking collectives, per_device(): lax.all_to_all(attended, zaxes, split_axis=0, concat_axis=0, tiled=True)  34.8 us
    pallas_call x1, Pallas kernels, per_device(): pl.pallas_call(functools.partial(attention_kernel, tuple(plan)), out_shap...  34.1 us
    ppermute x24, starting transfers between devices, shift(): lax.ppermute(value, axis, [(i, (i + step) % size) for i in range(size)])  24.8 us
    all_to_all x1, blocking collectives, per_device(): span = lax.all_to_all(span, zaxes, split_axis=0, concat_axis=0, tiled=True)  19.1 us
    all_to_all x1, starting transfers between devices, per_device(): lax.all_to_all(by_plane(queries, (cache_k,)), zaxes, split_axis=0, concat...  4.47 us
  transfers between devices with their start and end apart: 26, of which 13 were waited for; matrix products, arithmetic and copies ran while one was open for 1% of the time, Pallas kernels for 3%

profile of v1, /device:TPU:32, one launch (start us, length us, event | category | flops | bytes accessed | tf_op | source)
XLA Modules:
  0.0 190.9 jit_solution(16706333488885949941)
XLA Ops:
  6.5 0.6 stack.43.place
  7.1 2.8 %payload.1 = (bf16[2,256,128]{2,1,0:T(8,128)(2,1)}, bf16[2,256,128]{2,1,0:T(8,128)(2,1)}, bf16[8,2,64,128]{3,2,1,0:T(8,128)(2,1)}) custom-call(s32[6]{0:T(128)} %stack.43.place, bf16[1024,1024]{1,0:T(8,128)(2,1)} %cache_keys.1, bf16[1024,1024]{1,0:T(8,128)(2,1)} %cache_values.1, bf16[64,1024]{1,0:T(8,128)(2,1)} %span_keys.1, bf16[64,1024]{1,0:T(8,128)(2,1)} %span_values.1), custom_call_target="tpu_custom_call" | custom-call | tf_op jit(solution)/shard_map/payload/pallas_call | solution.py:65
  9.9 19.1 %all_to_all.15 = bf16[8,2,64,128]{3,2,1,0:T(8,128)(2,1)} all-to-all(bf16[8,2,64,128]{3,2,1,0:T(8,128)(2,1)} %get-tuple-element.17), channel_id=1, replica_groups=mesh['x'=4,'zl'=2,'k'=2,'zh'=4,'y'=4] {'zl','zh'}, dimensions={0} | all-to-all | bytes 524288 | tf_op jit(solution)/shard_map/all_to_all | solution.py:282
  29.1 3.2 %collective-permute-start.2 = (s32[4,19]{1,0:T(4,128)S(1)}, s32[4,19]{1,0:T(4,128)S(1)}, u32[]{:S(2)}, u32[]{:S(2)}) collective-permute-start(s32[4,19]{1,0:T(4,128)S(1)} %pad_add_fusion.3), channel_id=1, source_target_pairs={{0,2},{1,3},{2,0},{3,1},{4,6},{5,7},{6,4},{7,5},{8,10},{9,11},{10,... | collective-permute-start | bytes 920 | tf_op jit(solution)/shard_map/ppermute | solution.py:25
  32.3 0.7 collective-permute-start
  33.0 2.6 %collective-permute-start.1 = (s32[4,19]{1,0:T(4,128)S(1)}, s32[4,19]{1,0:T(4,128)S(1)}, u32[]{:S(2)}, u32[]{:S(2)}) collective-permute-start(s32[4,19]{1,0:T(4,128)S(1)} %pad_add_fusion.3), channel_id=1, source_target_pairs={{0,3},{1,0},{2,1},{3,2},{4,7},{5,4},{6,5},{7,6},{8,11},{9,8},{10,9... | collective-permute-start | bytes 920 | tf_op jit(solution)/shard_map/ppermute | solution.py:25
  35.6 1.5 collective-permute-done
  37.2 0.6 pad_add_fusion.2.refs_0_
  37.8 2.9 %collective-permute-done.3.swapped = bf16[2,256,128]{2,1,0:T(8,128)(2,1)S(1)} collective-permute-done((bf16[2,256,128]{2,1,0:T(8,128)(2,1)}, bf16[2,256,128]{2,1,0:T(8,128)(2,1)S(1)}, u32[]{:S(2)}, u32[]{:S(2)}) %collective-permute-start.3) | collective-permute-done | bytes 131104 | tf_op jit(solution)/shard_map/ppermute | solution.py:25
  40.8 0.7 copy-done.2
  41.4 1.7 merge.1
  43.1 1.5 collective-permute-start.4
  44.6 1.7 collective-permute-start.5
  46.4 1.8 collective-permute-start.6
  48.2 3.2 %collective-permute-start.8 = (bf16[2,256,128]{2,1,0:T(8,128)(2,1)}, bf16[2,256,128]{2,1,0:T(8,128)(2,1)S(1)}, u32[]{:S(2)}, u32[]{:S(2)}) collective-permute-start(bf16[2,256,128]{2,1,0:T(8,128)(2,1)} %get-tuple-element.15.refs_4_), channel_id=1, source_target_pairs={{0,3},{1,0},{2,1},{3,2},{4,7},{5,4},{6,5},{7,6},{8,11},{9,8},{10,9... | collective-permute-start | bytes 393224 | tf_op jit(solution)/shard_map/ppermute | solution.py:25
  51.4 0.3 collective-permute-start.9
  51.7 2.0 %collective-permute-done.6.refs_3_ = bf16[2,256,128]{2,1,0:T(8,128)(2,1)S(1)} collective-permute-done((bf16[2,256,128]{2,1,0:T(8,128)(2,1)}, bf16[2,256,128]{2,1,0:T(8,128)(2,1)S(1)}, u32[]{:S(2)}, u32[]{:S(2)}) %collective-permute-start.6) | collective-permute-done | bytes 131104 | tf_op jit(solution)/shard_map/ppermute | solution.py:25
  53.8 1.4 collective-permute-done.7.refs_5_
  55.2 2.9 %collective-permute-done.9.refs_7_ = bf16[2,256,128]{2,1,0:T(8,128)(2,1)S(1)} collective-permute-done((bf16[2,256,128]{2,1,0:T(8,128)(2,1)}, bf16[2,256,128]{2,1,0:T(8,128)(2,1)S(1)}, u32[]{:S(2)}, u32[]{:S(2)}) %collective-permute-start.9) | collective-permute-done | bytes 131104 | tf_op jit(solution)/shard_map/ppermute | solution.py:25
  58.2 0.6 copy-done.8
  58.8 2.3 %stack.49 = (bf16[4,2,256,128]{3,2,1,0:T(8,128)(2,1)}, bf16[4,2,256,128]{3,2,1,0:T(8,128)(2,1)}) custom-call(bf16[2,256,128]{2,1,0:T(8,128)(2,1)} %get-tuple-element.14.refs_0_, bf16[2,256,128]{2,1,0:T(8,128)(2,1)} %copy-done.3, bf16[2,256,128]{2,1,0:T(8,128)(2,1)} %copy-done.4, bf16[2,256,128]{2,1,0:T(8,128)(2,1)} %copy-done.5, ...), custom_call_target="tpu_custom_call" | custom-call | tf_op jit(solution)/shard_map/stack/pallas_call | solution.py:99
  61.1 2.3 %by_plane.1 = bf16[8,64,1024]{2,1,0:T(8,128)(2,1)} custom-call(bf16[64,8192]{1,0:T(8,128)(2,1)} %source.1, bf16[4,2,256,128]{3,2,1,0:T(8,128)(2,1)} %get-tuple-element.16.refs_0_), custom_call_target="tpu_custom_call" | custom-call | tf_op jit(solution)/shard_map/by_plane/pallas_call | solution.py:116
  63.4 4.5 %all-to-all-start = ((bf16[8,64,1024]{2,1,0:T(8,128)(2,1)}), bf16[8,64,1024]{2,1,0:T(8,128)(2,1)}, u32[]{:S(2)}, u32[]{:S(2)}) async-start(bf16[8,64,1024]{2,1,0:T(8,128)(2,1)} %by_plane.1), calls=%async_computation | async-start | bytes 2097152 | tf_op jit(solution)/shard_map/all_to_all | solution.py:293
  67.9 1.0 collective-permute-start.11
  69.0 2.3 %collective-permute-start.13 = (bf16[4,2,256,128]{3,2,1,0:T(8,128)(2,1)S(1)}, bf16[4,2,256,128]{3,2,1,0:T(8,128)(2,1)S(1)}, u32[]{:S(2)}, u32[]{:S(2)}) collective-permute-start(bf16[4,2,256,128]{3,2,1,0:T(8,128)(2,1)S(1)} %copy-done), channel_id=1, source_target_pairs={{0,3},{1,0},{2,1},{3,2},{4,7},{5,4},{6,5},{7,6},{8,11},{9,8},{10,9... | collective-permute-start | bytes 1572872 | tf_op jit(solution)/shard_map/ppermute | solution.py:25
  71.3 0.6 collective-permute-start.18
  72.2 2.7 %collective-permute-start.20 = (bf16[4,2,256,128]{3,2,1,0:T(8,128)(2,1)}, bf16[4,2,256,128]{3,2,1,0:T(8,128)(2,1)}, u32[]{:S(2)}, u32[]{:S(2)}) collective-permute-start(bf16[4,2,256,128]{3,2,1,0:T(8,128)(2,1)} %get-tuple-element.18), channel_id=1, source_target_pairs={{0,192},{64,0},{128,64},{192,128},{1,193},{65,1},{129,65},{193,129... | collective-permute-start | bytes 1572872 | tf_op jit(solution)/shard_map/ppermute | solution.py:25
  74.9 22.0 %collective-permute-done.11 = bf16[4,2,256,128]{3,2,1,0:T(8,128)(2,1)S(1)} collective-permute-done((bf16[4,2,256,128]{3,2,1,0:T(8,128)(2,1)S(1)}, bf16[4,2,256,128]{3,2,1,0:T(8,128)(2,1)S(1)}, u32[]{:S(2)}, u32[]{:S(2)}) %collective-permute-start.11) | collective-permute-done | bytes 524320 | tf_op jit(solution)/shard_map/ppermute | solution.py:25
  96.9 1.5 collective-permute-start.22
  98.5 7.8 %collective-permute-done.15 = bf16[4,2,256,128]{3,2,1,0:T(8,128)(2,1)S(1)} collective-permute-done((bf16[4,2,256,128]{3,2,1,0:T(8,128)(2,1)S(1)}, bf16[4,2,256,128]{3,2,1,0:T(8,128)(2,1)S(1)}, u32[]{:S(2)}, u32[]{:S(2)}) %collective-permute-start.15) | collective-permute-done | bytes 524320 | tf_op jit(solution)/shard_map/ppermute | solution.py:25
  106.2 0.5 collective-permute-start.12
  106.7 0.6 compare_reduce_fusion
  107.4 0.1 copy.20
  107.6 0.3 collective-permute-done.22
  107.9 0.2 collective-permute-start.16
  108.1 0.3 collective-permute-start.19
  108.4 0.7 collective-permute-done.17
  109.1 0.1 collective-permute-start.21
  109.3 0.4 collective-permute-start.23
  109.9 0.1 copy.15
  110.3 0.3 collective-permute-done.14
  110.7 1.5 collective-permute-done.16
  112.2 0.4 collective-permute-done.21
  112.6 0.7 collective-permute-done.23
  113.4 34.1 %attention.1 = bf16[8,64,1024]{2,1,0:T(8,128)(2,1)} custom-call(s32[6]{0:T(128)S(1)} %copy-done.1, s32[1280]{0:T(1024)S(1)} %reshape.92.picks, f32[1280]{0:T(1024)S(1)} %select_n.55.biases, bf16[8,64,1024]{2,1,0:T(8,128)(2,1)} %all-to-all-done.q_ref, bf16[64,4,2,64,128]{4,3,2,1,0:T(8,128)(2,1)} %bitcast.72, bf16[4,2,2,128,128]{4,3,2,1,0:T(8,128)(2,1)S(1)} %bitcast.61, ...), custom_call_target="tpu_custom_call" | custom-call | flops 5368709120 | bytes 18874368 | tf_op jit(solution)/shard_map/attention/pallas_call | solution.py:299
  147.5 34.8 %all_to_all.16 = bf16[8,64,1024]{2,1,0:T(8,128)(2,1)S(1)} all-to-all(bf16[8,64,1024]{2,1,0:T(8,128)(2,1)} %attention.1), channel_id=1, replica_groups=mesh['x'=4,'zl'=2,'k'=2,'zh'=4,'y'=4] {'zl','zh'}, dimensions={0} | all-to-all | bytes 2097152 | tf_op jit(solution)/shard_map/all_to_all | solution.py:315
  182.5 1.0 copy-done.10
  183.4 0.7 fusion
  (76 shorter events, 1.5 us)
Async XLA Ops:
  6.5 106.8 %all-gather.2.cloned.1.call-start = ((), (), s32[]{:S(2)}) async-start(), calls=%async_computation.3 | async-start | bytes 8650752 | tf_op jit(solution)/shard_map/all_gather | solution.py:284
  7.1 21.9 %copy-start.11 = (s32[4,3]{1,0:T(4,128)S(1)}, s32[4,3]{1,0:T(4,128)}, u32[]{:S(2)}) copy-start(s32[4,3]{1,0:T(4,128)} %param.14) | copy-start | bytes 148
  7.1 21.9 %copy-start.12 = (s32[4,16,1]{1,2,0:T(1,128)S(1)}, s32[4,16,1]{1,2,0:T(1,128)}, u32[]{:S(2)}) copy-start(s32[4,16,1]{1,2,0:T(1,128)} %param.13) | copy-start | bytes 772
  7.1 28.5 %copy-start.13 = (s32[4]{0:T(128)S(1)}, s32[4]{0:T(128)}, u32[]{:S(2)}) copy-start(s32[4]{0:T(128)} %constant.95.clone) | copy-start | bytes 52
  29.1 6.5 %collective-permute-start.2 = (s32[4,19]{1,0:T(4,128)S(1)}, s32[4,19]{1,0:T(4,128)S(1)}, u32[]{:S(2)}, u32[]{:S(2)}) collective-permute-start(s32[4,19]{1,0:T(4,128)S(1)} %pad_add_fusion.3), channel_id=1, source_target_pairs={{0,2},{1,3},{2,0},{3,1},{4,6},{5,7},{6,4},{7,5},{8,10},{9,11},{10,... | collective-permute-start | bytes 920 | tf_op jit(solution)/shard_map/ppermute | solution.py:25
  32.3 4.8 %collective-permute-start = (s32[4,19]{1,0:T(4,128)S(1)}, s32[4,19]{1,0:T(4,128)S(1)}, u32[]{:S(2)}, u32[]{:S(2)}) collective-permute-start(s32[4,19]{1,0:T(4,128)S(1)} %pad_add_fusion.3), channel_id=1, source_target_pairs={{0,1},{1,2},{2,3},{3,0},{4,5},{5,6},{6,7},{7,4},{8,9},{9,10},{10,1... | collective-permute-start | bytes 920 | tf_op jit(solution)/shard_map/ppermute | solution.py:25
  33.0 4.1 %collective-permute-start.1 = (s32[4,19]{1,0:T(4,128)S(1)}, s32[4,19]{1,0:T(4,128)S(1)}, u32[]{:S(2)}, u32[]{:S(2)}) collective-permute-start(s32[4,19]{1,0:T(4,128)S(1)} %pad_add_fusion.3), channel_id=1, source_target_pairs={{0,3},{1,0},{2,1},{3,2},{4,7},{5,4},{6,5},{7,6},{8,11},{9,8},{10,9... | collective-permute-start | bytes 920 | tf_op jit(solution)/shard_map/ppermute | solution.py:25
  35.6 5.2 %collective-permute-start.3 = (bf16[2,256,128]{2,1,0:T(8,128)(2,1)}, bf16[2,256,128]{2,1,0:T(8,128)(2,1)S(1)}, u32[]{:S(2)}, u32[]{:S(2)}) collective-permute-start(bf16[2,256,128]{2,1,0:T(8,128)(2,1)} %get-tuple-element.13), channel_id=1, source_target_pairs={{0,32},{32,0},{1,33},{33,1},{2,34},{34,2},{3,35},{35,3},{4,36},{36... | collective-permute-start | bytes 393224 | tf_op jit(solution)/shard_map/ppermute | solution.py:25
  40.8 0.7 copy-start.2
  43.1 8.3 %collective-permute-start.4 = (bf16[2,256,128]{2,1,0:T(8,128)(2,1)}, bf16[2,256,128]{2,1,0:T(8,128)(2,1)S(1)}, u32[]{:S(2)}, u32[]{:S(2)}) collective-permute-start(bf16[2,256,128]{2,1,0:T(8,128)(2,1)} %get-tuple-element.14.refs_0_), channel_id=1, source_target_pairs={{0,64},{64,128},{128,192},{192,0},{1,65},{65,129},{129,193},{193,1... | collective-permute-start | bytes 393224 | tf_op jit(solution)/shard_map/ppermute | solution.py:25
  44.6 7.1 %collective-permute-start.5 = (bf16[2,256,128]{2,1,0:T(8,128)(2,1)}, bf16[2,256,128]{2,1,0:T(8,128)(2,1)S(1)}, u32[]{:S(2)}, u32[]{:S(2)}) collective-permute-start(bf16[2,256,128]{2,1,0:T(8,128)(2,1)} %get-tuple-element.14.refs_0_), channel_id=1, source_target_pairs={{0,192},{64,0},{128,64},{192,128},{1,193},{65,1},{129,65},{193,129... | collective-permute-start | bytes 393224 | tf_op jit(solution)/shard_map/ppermute | solution.py:25
  46.4 7.4 %collective-permute-start.6 = (bf16[2,256,128]{2,1,0:T(8,128)(2,1)}, bf16[2,256,128]{2,1,0:T(8,128)(2,1)S(1)}, u32[]{:S(2)}, u32[]{:S(2)}) collective-permute-start(bf16[2,256,128]{2,1,0:T(8,128)(2,1)} %get-tuple-element.14.refs_0_), channel_id=1, source_target_pairs={{0,128},{64,192},{128,0},{192,64},{1,129},{65,193},{129,1},{193,65... | collective-permute-start | bytes 393224 | tf_op jit(solution)/shard_map/ppermute | solution.py:25
  48.2 7.0 %collective-permute-start.7 = (bf16[2,256,128]{2,1,0:T(8,128)(2,1)}, bf16[2,256,128]{2,1,0:T(8,128)(2,1)S(1)}, u32[]{:S(2)}, u32[]{:S(2)}) collective-permute-start(bf16[2,256,128]{2,1,0:T(8,128)(2,1)} %get-tuple-element.15.refs_4_), channel_id=1, source_target_pairs={{0,1},{1,2},{2,3},{3,0},{4,5},{5,6},{6,7},{7,4},{8,9},{9,10},{10,1... | collective-permute-start | bytes 393224 | tf_op jit(solution)/shard_map/ppermute | solution.py:25
  48.2 7.0 %collective-permute-start.8 = (bf16[2,256,128]{2,1,0:T(8,128)(2,1)}, bf16[2,256,128]{2,1,0:T(8,128)(2,1)S(1)}, u32[]{:S(2)}, u32[]{:S(2)}) collective-permute-start(bf16[2,256,128]{2,1,0:T(8,128)(2,1)} %get-tuple-element.15.refs_4_), channel_id=1, source_target_pairs={{0,3},{1,0},{2,1},{3,2},{4,7},{5,4},{6,5},{7,6},{8,11},{9,8},{10,9... | collective-permute-start | bytes 393224 | tf_op jit(solution)/shard_map/ppermute | solution.py:25
  51.4 6.7 %copy-start.3 = (bf16[2,256,128]{2,1,0:T(8,128)(2,1)}, bf16[2,256,128]{2,1,0:T(8,128)(2,1)S(1)}, u32[]{:S(2)}) copy-start(bf16[2,256,128]{2,1,0:T(8,128)(2,1)S(1)} %collective-permute-done.4.refs_1_) | copy-start | bytes 393220
  51.4 6.7 %collective-permute-start.9 = (bf16[2,256,128]{2,1,0:T(8,128)(2,1)}, bf16[2,256,128]{2,1,0:T(8,128)(2,1)S(1)}, u32[]{:S(2)}, u32[]{:S(2)}) collective-permute-start(bf16[2,256,128]{2,1,0:T(8,128)(2,1)} %get-tuple-element.15.refs_4_), channel_id=1, source_target_pairs={{0,2},{1,3},{2,0},{3,1},{4,6},{5,7},{6,4},{7,5},{8,10},{9,11},{10,... | collective-permute-start | bytes 393224 | tf_op jit(solution)/shard_map/ppermute | solution.py:25
  51.7 6.4 %copy-start.4 = (bf16[2,256,128]{2,1,0:T(8,128)(2,1)}, bf16[2,256,128]{2,1,0:T(8,128)(2,1)S(1)}, u32[]{:S(2)}) copy-start(bf16[2,256,128]{2,1,0:T(8,128)(2,1)S(1)} %collective-permute-done.5.refs_2_) | copy-start | bytes 393220
  53.8 4.4 %copy-start.5 = (bf16[2,256,128]{2,1,0:T(8,128)(2,1)}, bf16[2,256,128]{2,1,0:T(8,128)(2,1)S(1)}, u32[]{:S(2)}) copy-start(bf16[2,256,128]{2,1,0:T(8,128)(2,1)S(1)} %collective-permute-done.6.refs_3_) | copy-start | bytes 393220
  55.2 2.9 %copy-start.6 = (bf16[2,256,128]{2,1,0:T(8,128)(2,1)}, bf16[2,256,128]{2,1,0:T(8,128)(2,1)S(1)}, u32[]{:S(2)}) copy-start(bf16[2,256,128]{2,1,0:T(8,128)(2,1)S(1)} %collective-permute-done.7.refs_5_) | copy-start | bytes 393220
  55.2 2.9 %copy-start.7 = (bf16[2,256,128]{2,1,0:T(8,128)(2,1)}, bf16[2,256,128]{2,1,0:T(8,128)(2,1)S(1)}, u32[]{:S(2)}) copy-start(bf16[2,256,128]{2,1,0:T(8,128)(2,1)S(1)} %collective-permute-done.8.refs_6_) | copy-start | bytes 393220
  58.1 0.7 copy-start.8
  61.1 6.8 %copy-start = (bf16[4,2,256,128]{3,2,1,0:T(8,128)(2,1)S(1)}, bf16[4,2,256,128]{3,2,1,0:T(8,128)(2,1)}, u32[]{:S(2)}) copy-start(bf16[4,2,256,128]{3,2,1,0:T(8,128)(2,1)} %get-tuple-element.16.refs_0_) | copy-start | bytes 1572868
  61.1 10.8 %copy-start.9 = (s32[8,19]{1,0:T(8,128)S(1)}, s32[8,19]{1,0:T(8,128)}, u32[]{:S(2)}) copy-start(s32[8,19]{1,0:T(8,128)} %pad_add_fusion.2.refs_0_) | copy-start | bytes 1828
  61.1 52.2 %copy-start.1 = (s32[6]{0:T(128)S(1)}, s32[6]{0:T(128)}, u32[]{:S(2)}) copy-start(s32[6]{0:T(128)} %stack.43.place) | copy-start | bytes 76
  63.4 49.9 %all-to-all-start = ((bf16[8,64,1024]{2,1,0:T(8,128)(2,1)}), bf16[8,64,1024]{2,1,0:T(8,128)(2,1)}, u32[]{:S(2)}, u32[]{:S(2)}) async-start(bf16[8,64,1024]{2,1,0:T(8,128)(2,1)} %by_plane.1), calls=%async_computation | async-start | bytes 2097152 | tf_op jit(solution)/shard_map/all_to_all | solution.py:293
  67.9 29.0 %collective-permute-start.11 = (bf16[4,2,256,128]{3,2,1,0:T(8,128)(2,1)S(1)}, bf16[4,2,256,128]{3,2,1,0:T(8,128)(2,1)S(1)}, u32[]{:S(2)}, u32[]{:S(2)}) collective-permute-start(bf16[4,2,256,128]{3,2,1,0:T(8,128)(2,1)S(1)} %copy-done), channel_id=1, source_target_pairs={{0,1},{1,2},{2,3},{3,0},{4,5},{5,6},{6,7},{7,4},{8,9},{9,10},{10,1... | collective-permute-start | bytes 1572872 | tf_op jit(solution)/shard_map/ppermute | solution.py:25
  69.0 29.5 %collective-permute-start.13 = (bf16[4,2,256,128]{3,2,1,0:T(8,128)(2,1)S(1)}, bf16[4,2,256,128]{3,2,1,0:T(8,128)(2,1)S(1)}, u32[]{:S(2)}, u32[]{:S(2)}) collective-permute-start(bf16[4,2,256,128]{3,2,1,0:T(8,128)(2,1)S(1)} %copy-done), channel_id=1, source_target_pairs={{0,3},{1,0},{2,1},{3,2},{4,7},{5,4},{6,5},{7,6},{8,11},{9,8},{10,9... | collective-permute-start | bytes 1572872 | tf_op jit(solution)/shard_map/ppermute | solution.py:25
  71.2 35.0 %collective-permute-start.15 = (bf16[4,2,256,128]{3,2,1,0:T(8,128)(2,1)S(1)}, bf16[4,2,256,128]{3,2,1,0:T(8,128)(2,1)S(1)}, u32[]{:S(2)}, u32[]{:S(2)}) collective-permute-start(bf16[4,2,256,128]{3,2,1,0:T(8,128)(2,1)S(1)} %copy-done), channel_id=1, source_target_pairs={{0,2},{1,3},{2,0},{3,1},{4,6},{5,7},{6,4},{7,5},{8,10},{9,11},{10,... | collective-permute-start | bytes 1572872 | tf_op jit(solution)/shard_map/ppermute | solution.py:25
  71.3 35.0 %collective-permute-start.18 = (bf16[4,2,256,128]{3,2,1,0:T(8,128)(2,1)}, bf16[4,2,256,128]{3,2,1,0:T(8,128)(2,1)}, u32[]{:S(2)}, u32[]{:S(2)}) collective-permute-start(bf16[4,2,256,128]{3,2,1,0:T(8,128)(2,1)} %get-tuple-element.18), channel_id=1, source_target_pairs={{0,64},{64,128},{128,192},{192,0},{1,65},{65,129},{129,193},{193,1... | collective-permute-start | bytes 1572872 | tf_op jit(solution)/shard_map/ppermute | solution.py:25
  72.2 35.3 %collective-permute-start.20 = (bf16[4,2,256,128]{3,2,1,0:T(8,128)(2,1)}, bf16[4,2,256,128]{3,2,1,0:T(8,128)(2,1)}, u32[]{:S(2)}, u32[]{:S(2)}) collective-permute-start(bf16[4,2,256,128]{3,2,1,0:T(8,128)(2,1)} %get-tuple-element.18), channel_id=1, source_target_pairs={{0,192},{64,0},{128,64},{192,128},{1,193},{65,1},{129,65},{193,129... | collective-permute-start | bytes 1572872 | tf_op jit(solution)/shard_map/ppermute | solution.py:25
  96.9 11.0 %collective-permute-start.22 = (bf16[4,2,256,128]{3,2,1,0:T(8,128)(2,1)}, bf16[4,2,256,128]{3,2,1,0:T(8,128)(2,1)}, u32[]{:S(2)}, u32[]{:S(2)}) collective-permute-start(bf16[4,2,256,128]{3,2,1,0:T(8,128)(2,1)} %get-tuple-element.18), channel_id=1, source_target_pairs={{0,128},{64,192},{128,0},{192,64},{1,129},{65,193},{129,1},{193,65... | collective-permute-start | bytes 1572872 | tf_op jit(solution)/shard_map/ppermute | solution.py:25
  98.5 9.7 %collective-permute-start.10 = (bf16[4,2,256,128]{3,2,1,0:T(8,128)(2,1)S(1)}, bf16[4,2,256,128]{3,2,1,0:T(8,128)(2,1)S(1)}, u32[]{:S(2)}, u32[]{:S(2)}) collective-permute-start(bf16[4,2,256,128]{3,2,1,0:T(8,128)(2,1)S(1)} %copy-done), channel_id=1, source_target_pairs={{0,16},{16,0},{1,17},{17,1},{2,18},{18,2},{3,19},{19,3},{4,20},{20... | collective-permute-start | bytes 1572872 | tf_op jit(solution)/shard_map/ppermute | solution.py:25
  106.2 2.9 %collective-permute-start.17 = (bf16[4,2,256,128]{3,2,1,0:T(8,128)(2,1)}, bf16[4,2,256,128]{3,2,1,0:T(8,128)(2,1)}, u32[]{:S(2)}, u32[]{:S(2)}) collective-permute-start(bf16[4,2,256,128]{3,2,1,0:T(8,128)(2,1)} %get-tuple-element.18), channel_id=1, source_target_pairs={{0,16},{16,0},{1,17},{17,1},{2,18},{18,2},{3,19},{19,3},{4,20},{20... | collective-permute-start | bytes 1572872 | tf_op jit(solution)/shard_map/ppermute | solution.py:25
  106.2 3.1 %collective-permute-start.12 = (bf16[4,2,256,128]{3,2,1,0:T(8,128)(2,1)S(1)}, bf16[4,2,256,128]{3,2,1,0:T(8,128)(2,1)S(1)}, u32[]{:S(2)}, u32[]{:S(2)}) collective-permute-start(bf16[4,2,256,128]{3,2,1,0:T(8,128)(2,1)S(1)} %collective-permute-done.11), channel_id=1, source_target_pairs={{0,16},{16,0},{1,17},{17,1},{2,18},{18,2},{3,19},{19,3},{4,20},{20... | collective-permute-start | bytes 1572872 | tf_op jit(solution)/shard_map/ppermute | solution.py:25
  107.5 3.1 %collective-permute-start.14 = (bf16[4,2,256,128]{3,2,1,0:T(8,128)(2,1)S(1)}, bf16[4,2,256,128]{3,2,1,0:T(8,128)(2,1)}, u32[]{:S(2)}, u32[]{:S(2)}) collective-permute-start(bf16[4,2,256,128]{3,2,1,0:T(8,128)(2,1)S(1)} %collective-permute-done.13), channel_id=1, source_target_pairs={{0,16},{16,0},{1,17},{17,1},{2,18},{18,2},{3,19},{19,3},{4,20},{20... | collective-permute-start | bytes 1572872 | tf_op jit(solution)/shard_map/ppermute | solution.py:25
  107.9 4.2 %collective-permute-start.16 = (bf16[4,2,256,128]{3,2,1,0:T(8,128)(2,1)S(1)}, bf16[4,2,256,128]{3,2,1,0:T(8,128)(2,1)}, u32[]{:S(2)}, u32[]{:S(2)}) collective-permute-start(bf16[4,2,256,128]{3,2,1,0:T(8,128)(2,1)S(1)} %collective-permute-done.15), channel_id=1, source_target_pairs={{0,16},{16,0},{1,17},{17,1},{2,18},{18,2},{3,19},{19,3},{4,20},{20... | collective-permute-start | bytes 1572872 | tf_op jit(solution)/shard_map/ppermute | solution.py:25
  108.1 4.0 %collective-permute-start.19 = (bf16[4,2,256,128]{3,2,1,0:T(8,128)(2,1)}, bf16[4,2,256,128]{3,2,1,0:T(8,128)(2,1)}, u32[]{:S(2)}, u32[]{:S(2)}) collective-permute-start(bf16[4,2,256,128]{3,2,1,0:T(8,128)(2,1)} %collective-permute-done.18), channel_id=1, source_target_pairs={{0,16},{16,0},{1,17},{17,1},{2,18},{18,2},{3,19},{19,3},{4,20},{20... | collective-permute-start | bytes 1572872 | tf_op jit(solution)/shard_map/ppermute | solution.py:25
  109.1 3.5 %collective-permute-start.21 = (bf16[4,2,256,128]{3,2,1,0:T(8,128)(2,1)}, bf16[4,2,256,128]{3,2,1,0:T(8,128)(2,1)}, u32[]{:S(2)}, u32[]{:S(2)}) collective-permute-start(bf16[4,2,256,128]{3,2,1,0:T(8,128)(2,1)} %collective-permute-done.20), channel_id=1, source_target_pairs={{0,16},{16,0},{1,17},{17,1},{2,18},{18,2},{3,19},{19,3},{4,20},{20... | collective-permute-start | bytes 1572872 | tf_op jit(solution)/shard_map/ppermute | solution.py:25
  109.3 4.1 %collective-permute-start.23 = (bf16[4,2,256,128]{3,2,1,0:T(8,128)(2,1)}, bf16[4,2,256,128]{3,2,1,0:T(8,128)(2,1)}, u32[]{:S(2)}, u32[]{:S(2)}) collective-permute-start(bf16[4,2,256,128]{3,2,1,0:T(8,128)(2,1)} %collective-permute-done.22), channel_id=1, source_target_pairs={{0,16},{16,0},{1,17},{17,1},{2,18},{18,2},{3,19},{19,3},{4,20},{20... | collective-permute-start | bytes 1572872 | tf_op jit(solution)/shard_map/ppermute | solution.py:25
  182.5 1.0 copy-start.10
Sparse Core Ops, SparseCore 0:
  29.1 80.7 all-gather.1

commit v2 on v1

v2 whole, which is shorter than its diff:
```python
import functools

import jax
import jax.numpy as jnp
import numpy as np
from jax import lax
from jax.experimental import pallas as pl
from jax.experimental.pallas import tpu as pltpu
from jax.sharding import Mesh
from jax.sharding import PartitionSpec as P

H = 64
KVH = 8
DH = 128
BLK = 128
GROUP = H // KVH
HALF = 64
NLIST = 20
LARGEST = 2.0**90
masked_score = -1e30
SCALE = DH ** (-0.5) * 1.4426950408889634


def shift(value, axis, size, step):
    return lax.ppermute(value, axis, [(i, (i + step) % size) for i in range(size)])


def ring_direct(value, axis):
    return [value, shift(value, axis, 4, 1), shift(value, axis, 4, -1), shift(value, axis, 4, 2)]


ORIGINS = (0, -1, 1, 2)
PLANES = (0, 2, 4, 6, 1, 3, 5, 7)


HBM = pl.BlockSpec(memory_space=pltpu.HBM)
SMEM = pl.BlockSpec(memory_space=pltpu.SMEM)
VMEM = pl.BlockSpec(memory_space=pltpu.VMEM)


def shaped(shape, dtype=jnp.bfloat16):
    return jax.ShapeDtypeStruct(shape, dtype)


def payload_kernel(place, cache_keys, cache_values, span_keys, span_values, own, other, span, sems):
    start = pl.multiple_of(place[1] * 256, 256)
    copies = []
    for i, cache in enumerate((cache_keys, cache_values)):
        for j, (target, column) in enumerate(((own, place[3]), (other, place[4]))):
            lanes = pl.ds(pl.multiple_of(column * DH, DH), DH)
            copies.append(
                pltpu.make_async_copy(cache.at[pl.ds(start, 256), lanes], target.at[i], sems.at[2 * i + j])
            )
    for copy in copies:
        copy.start()
    for i, source in enumerate((span_keys, span_values)):
        for slot, p in enumerate(PLANES):
            span[slot, i] = source[:, p * DH : (p + 1) * DH]
    for copy in copies:
        copy.wait()


def payload(place, cache_keys, cache_values, span_keys, span_values):
    return pl.pallas_call(
        payload_kernel,
        out_shape=[shaped((2, 256, DH)), shaped((2, 256, DH)), shaped((8, 2, HALF, DH))],
        in_specs=[SMEM, HBM, HBM, VMEM, VMEM],
        out_specs=[VMEM, VMEM, VMEM],
        scratch_shapes=[pltpu.SemaphoreType.DMA((4,))],
        compiler_params=pltpu.CompilerParams(vmem_limit_bytes=56 * 1024 * 1024),
        name="payload",
    )(place, cache_keys, cache_values, span_keys, span_values)


def pack_kernel(own, swapped, span, out):
    for i in range(2):
        out[0, i] = own[i]
        out[1, i] = swapped[i]
        for zl in range(2):
            for zh in range(4):
                out[2 + zl, i, zh * HALF : (zh + 1) * HALF] = span[zl * 4 + zh, i]


def pack(own, swapped, span):
    return pl.pallas_call(
        pack_kernel,
        out_shape=shaped((4, 2, 256, DH)),
        in_specs=[VMEM] * 3,
        out_specs=VMEM,
        name="pack",
    )(own, swapped, span)


def plane_kernel(extra, source, *refs):
    target = refs[extra]
    width = GROUP * DH
    for slot, plane in enumerate(PLANES):
        target[slot] = source[:, plane * width : (plane + 1) * width]


def by_plane(queries, after=()):
    return pl.pallas_call(
        functools.partial(plane_kernel, len(after)),
        out_shape=shaped((8, HALF, GROUP * DH)),
        in_specs=[VMEM] + [HBM] * len(after),
        out_specs=VMEM,
        name="by_plane",
    )(queries, *after)


BUFFER = (2, 4, 2, 2, 4, 2, BLK, DH)


def attend(exact, place, picks, biases, q_ref, keys, values, out_ref):
    group = 4 if exact else 8
    half = lax.rem(place[1], 2) * HALF
    rows = lax.broadcasted_iota(jnp.int32, (HALF, BLK), 0) + half
    cols = lax.broadcasted_iota(jnp.int32, (HALF, BLK), 1)
    triangle = cols <= rows
    dims = (((1,), (1,)), ((), ()))

    def step(item, largest):
        head = lax.div(item, 8 // group)
        part = lax.rem(item, 8 // group)
        lane = pl.ds(pl.multiple_of(head * DH, DH), DH)
        base = [(head * 8 + part * group + r) * NLIST for r in range(group)]
        q = [q_ref[part * group + r, :, lane] for r in range(group)]
        q_all = jnp.concatenate(q, axis=0)
        scores = [[] for _ in range(group)]

        def pick(ref, start, e):
            return jnp.concatenate([ref[picks[start + e]], ref[picks[start + e + 1]]], axis=0)

        def put(r, e, s):
            for d in range(2):
                block = s[:, d * BLK : (d + 1) * BLK]
                if e + d == 0:
                    block = jnp.where(triangle, block, masked_score)
                else:
                    block = block + biases[base[r] + e + d]
                scores[r].append(block)

        for e in range(0, 4, 2):
            for r in range(group):
                s = lax.dot_general(q[r], pick(keys, base[r], e), dims, preferred_element_type=jnp.float32)
                put(r, e, s)
        for e in range(4, NLIST, 2):
            s = lax.dot_general(q_all, pick(keys, base[0], e), dims, preferred_element_type=jnp.float32)
            for r in range(group):
                put(r, e, s[r * HALF : (r + 1) * HALF])
        weights = []
        inverse = []
        for r in range(group):
            top = functools.reduce(jnp.maximum, scores[r] if exact else scores[r][:4])
            top = jnp.max(top, axis=1, keepdims=True) * SCALE
            w = [jnp.exp2(s * SCALE - top) for s in scores[r]]
            total = functools.reduce(jnp.add, w)
            largest = jnp.maximum(largest, total)
            inverse.append(1.0 / jnp.sum(total, axis=1, keepdims=True))
            weights.append([a.astype(jnp.bfloat16) for a in w])
        summed = []
        for r in range(group):
            acc = jnp.zeros((HALF, DH), jnp.float32)
            for e in range(0, 4, 2):
                pair = jnp.concatenate(weights[r][e : e + 2], axis=1)
                acc = acc + jnp.dot(pair, pick(values, base[r], e), preferred_element_type=jnp.float32)
            summed.append(acc)
        acc = jnp.concatenate(summed, axis=0)
        for e in range(4, NLIST, 2):
            pair = jnp.concatenate(
                [jnp.concatenate(weights[r][e : e + 2], axis=1) for r in range(group)], axis=0
            )
            acc = acc + jnp.dot(pair, pick(values, base[0], e), preferred_element_type=jnp.float32)
        for r in range(group):
            result = acc[r * HALF : (r + 1) * HALF] * inverse[r]
            out_ref[part * group + r, :, lane] = result.astype(jnp.bfloat16)
        return largest

    return lax.fori_loop(0, GROUP * 8 // group, step, jnp.zeros((HALF, BLK), jnp.float32))


def attention_kernel(place, picks, biases, q_ref, cached, span, out_ref, kbuf, vbuf, sems):
    zl = place[5]
    copies = []

    def copy(source, target):
        copies.append(pltpu.make_async_copy(source, target, sems.at[len(copies)]))

    for i, buffer in enumerate((kbuf, vbuf)):
        for slot in range(32):
            x, k, y = slot // 8, slot // 4 % 2, slot % 4
            copy(cached.at[slot, 0, i], buffer.at[0, x, zl, k, y])
            copy(cached.at[slot, 1, i], buffer.at[0, x, 1 - zl, k, y])
            rows = pl.ds(y % 2 * HALF, HALF)
            copy(span.at[slot, 2:, i], buffer.at[1, x, :, k, :, y // 2, rows, :])
    for entry in copies:
        entry.start()
    for entry in copies:
        entry.wait()

    keys = kbuf.reshape(256, BLK, DH)
    values = vbuf.reshape(256, BLK, DH)
    largest = attend(False, place, picks, biases, q_ref, keys, values, out_ref)

    @pl.when(jnp.logical_not(jnp.max(largest) < LARGEST))
    def _():
        attend(True, place, picks, biases, q_ref, keys, values, out_ref)


def attention(place, picks, biases, queries, gathered):
    return pl.pallas_call(
        attention_kernel,
        out_shape=shaped((8, HALF, GROUP * DH)),
        in_specs=[SMEM, SMEM, SMEM, VMEM, HBM, HBM],
        out_specs=VMEM,
        scratch_shapes=[
            pltpu.VMEM(BUFFER, jnp.bfloat16),
            pltpu.VMEM(BUFFER, jnp.bfloat16),
            pltpu.SemaphoreType.DMA((192,)),
        ],
        compiler_params=pltpu.CompilerParams(vmem_limit_bytes=56 * 1024 * 1024),
        cost_estimate=pl.CostEstimate(
            flops=2 * 2 * GROUP * 512 * 2560 * 128,
            bytes_accessed=18 << 20,
            transcendentals=GROUP * 512 * 2560,
        ),
        name="attention",
    )(
        place,
        picks,
        biases,
        queries,
        gathered.reshape(32, 4, 2, 2, BLK, DH),
        gathered.reshape(32, 4, 2, 4, HALF, DH),
    )


def head_table(around, my_y, zl):
    origins = (my_y + jnp.array([0, 3, 1, 2], jnp.int32)) % 4

    def of(wanted):
        return jnp.sum(jnp.where((origins == wanted)[:, None, None], around, 0), axis=0)

    return jnp.concatenate([of(2 * zl), of(2 * zl + 1)], axis=0)


def listed_blocks(table, my_x, my_y, my_k):
    verticals, slashes = table[:, :16], table[:, 16:]
    shard = jnp.arange(16, dtype=jnp.int32)
    vertical = shard * 8 + verticals + jnp.where(verticals >= 8, 120, 0)
    zl = jnp.arange(8, dtype=jnp.int32) // 4
    zh = jnp.arange(8, dtype=jnp.int32) % 4
    own = 128 + (my_x * 4 + zl * 2 + my_k) * 8 + zh * 2 + my_y // 2
    target = own[None, :, None] - slashes[:, None, :]
    before = jnp.arange(3)[None, :] < jnp.arange(3)[:, None]
    repeated = jnp.any((slashes[:, :, None] == slashes[:, None, :]) & before, axis=-1)
    listed = jnp.any(target[..., None] == vertical[:, None, None, :], axis=-1)
    slash_ok = (target >= 0) & jnp.logical_not(repeated[:, None, :]) & jnp.logical_not(listed)
    vertical_ok = vertical[:, None, :] < own[None, :, None]
    shape = (GROUP, 8, 1)
    picks = jnp.concatenate(
        [
            jnp.broadcast_to(own[None, :, None], shape),
            jnp.maximum(target, 0),
            jnp.broadcast_to(vertical[:, None, :], (GROUP, 8, 16)),
        ],
        axis=2,
    )
    usable = jnp.concatenate([jnp.ones(shape, bool), slash_ok, vertical_ok], axis=2)
    biases = jnp.where(usable, 0.0, masked_score).astype(jnp.float32)
    return picks.reshape(-1), biases.reshape(-1)


def per_device(queries, span_keys, span_values, cache_keys, cache_values, verticals, slashes):
    my_x, my_y, my_k = lax.axis_index("x"), lax.axis_index("y"), lax.axis_index("k")
    zh, zl = lax.axis_index("zh"), lax.axis_index("zl")
    plane = zh * 2 + zl
    zaxes = ("zl", "zh")

    table = jnp.concatenate([verticals[:, :, 0], slashes], axis=1)
    table = head_table(jnp.stack(ring_direct(table, "y")), my_y, zl)
    place = jnp.stack([my_x, my_y, my_k, plane, plane + 1 - 2 * zl, zl]).astype(jnp.int32)

    own, other, span = payload(place, cache_keys, cache_values, span_keys, span_values)
    swapped = shift(other, "zl", 2, 1)
    span = lax.all_to_all(span, zaxes, split_axis=0, concat_axis=0, tiled=True)
    packed = pack(own, swapped, span)
    gathered = lax.all_gather(packed, ("x", "k", "y"), axis=0, tiled=False)
    slab_queries = lax.all_to_all(
        by_plane(queries, (packed,)), zaxes, split_axis=0, concat_axis=0, tiled=True
    )
    picks, biases = listed_blocks(table, my_x, my_y, my_k)

    attended = attention(place, picks, biases, slab_queries, gathered)
    result = lax.all_to_all(attended, zaxes, split_axis=0, concat_axis=0, tiled=True)
    return jnp.concatenate([result[PLANES.index(p)] for p in range(8)], axis=1)


def solution(mesh):
    axes = ("x", "zl", "k", "zh", "y")
    fine = Mesh(np.asarray(mesh.devices).reshape(4, 2, 2, 4, 4), axes)
    rows = P(axes, None)
    return jax.shard_map(
        per_device,
        mesh=fine,
        in_specs=(
            rows,
            rows,
            rows,
            P(("x", "zl", "k"), None),
            P(("x", "zl", "k"), None),
            P(("zh", "y"), None, None),
            P(("zh", "y"), None),
        ),
        out_specs=rows,
        check_vma=False,
    )
```

time: 191 us -> 180 us (0.942)
  waiting for transfers between devices: 44.6 us -> 70.4 us
  blocking collectives: 53.9 us -> 35.2 us
  Pallas kernels: 43.3 us -> 33 us
  starting transfers between devices: 29.3 us -> 21.1 us
    all_gather x1, waiting for transfers between devices: 0.01 us -> 37.1 us  [per_device(): gathered = lax.all_gather(packed, ('x', 'k', 'y'), axis=0, tiled=False)]
    ppermute x24 -> x4, waiting for transfers between devices: 44.6 us -> 8.72 us  [shift(): lax.ppermute(value, axis, [(i, (i + step) % size) for i in range(size)])]
    all_to_all x1 -> x2, waiting for transfers between devices: 0.01 us -> 24.5 us  [the longest x1 22.5 us: per_device(): lax.all_to_all(by_plane(queries, (packed,)), zaxes, split_axis=0, concat_...]
    all_to_all x1 -> x0, blocking collectives: 19.1 us -> none  [per_device(): span = lax.all_to_all(span, zaxes, split_axis=0, concat_axis=0, tiled=True)]
    ppermute x24 -> x4, starting transfers between devices: 24.8 us -> 6.59 us  [shift(): lax.ppermute(value, axis, [(i, (i + step) % size) for i in range(size)])]
    pallas_call x3 -> x2, Pallas kernels: 38.2 us -> 28 us  [the longest x1 26.1 us: attention(): pl.pallas_call(attention_kernel, out_shape=shaped((8, HALF, GROUP * DH)),...]
    all_to_all x1 -> x2, starting transfers between devices: 4.47 us -> 14.5 us  [the longest x1 8.71 us: per_device(): span = lax.all_to_all(span, zaxes, split_axis=0, concat_axis=0, tiled=True)]
  transfers between devices with their start and end apart: 26 -> 7, of which waited for: 13 -> 4; matrix products, arithmetic and copies ran while one was open for 1% -> 2% of each run, Pallas kernels for 3% -> 1%
where the time goes in v2:
time: 180 us; the launch traced here: 179 us
  waiting for transfers between devices  70.4 us (39%)
  blocking collectives  35.2 us (20%)
  Pallas kernels  33 us (18%)
  starting transfers between devices  21.1 us (12%)
  between operations  13.6 us (8%)
  local copies, waits for them, and re-layouts  4.96 us (3%)
    all_gather x1, waiting for transfers between devices, per_device(): gathered = lax.all_gather(packed, ('x', 'k', 'y'), axis=0, tiled=False)  37.1 us
    all_to_all x1, blocking collectives, per_device(): lax.all_to_all(attended, zaxes, split_axis=0, concat_axis=0, tiled=True)  35.2 us
    pallas_call x1, Pallas kernels, attention(): pl.pallas_call(attention_kernel, out_shape=shaped((8, HALF, GROUP * DH)),...  26.1 us
    all_to_all x1, waiting for transfers between devices, per_device(): lax.all_to_all(by_plane(queries, (packed,)), zaxes, split_axis=0, concat_...  22.5 us
    ppermute x4, waiting for transfers between devices, shift(): lax.ppermute(value, axis, [(i, (i + step) % size) for i in range(size)])  8.72 us
    all_to_all x1, starting transfers between devices, per_device(): span = lax.all_to_all(span, zaxes, split_axis=0, concat_axis=0, tiled=True)  8.71 us
    ppermute x4, starting transfers between devices, shift(): lax.ppermute(value, axis, [(i, (i + step) % size) for i in range(size)])  6.59 us
    all_to_all x1, starting transfers between devices, per_device(): lax.all_to_all(by_plane(queries, (packed,)), zaxes, split_axis=0, concat_...  5.75 us
  transfers between devices with their start and end apart: 7, of which 4 were waited for; matrix products, arithmetic and copies ran while one was open for 2% of the time, Pallas kernels for 1%

profile of v2, /device:TPU:32, one launch (start us, length us, event | category | flops | bytes accessed | tf_op | source)
XLA Modules:
  0.0 179.5 jit_solution(7825325869175369321)
XLA Ops:
  6.5 0.6 stack.42.place
  7.1 2.7 %payload.1 = (bf16[2,256,128]{2,1,0:T(8,128)(2,1)}, bf16[2,256,128]{2,1,0:T(8,128)(2,1)}, bf16[8,2,64,128]{3,2,1,0:T(8,128)(2,1)}) custom-call(s32[6]{0:T(128)} %stack.42.place, bf16[1024,1024]{1,0:T(8,128)(2,1)} %cache_keys.1, bf16[1024,1024]{1,0:T(8,128)(2,1)} %cache_values.1, bf16[64,1024]{1,0:T(8,128)(2,1)} %span_keys.1, bf16[64,1024]{1,0:T(8,128)(2,1)} %span_values.1), custom_call_target="tpu_custom_call" | custom-call | tf_op jit(solution)/shard_map/payload/pallas_call | solution.py:64
  9.9 0.0 copy-start.4
  9.9 0.0 copy-start.5
  9.9 0.0 copy-start.6
  9.9 8.7 %all-to-all-start = ((bf16[8,2,64,128]{3,2,1,0:T(8,128)(2,1)}), bf16[8,2,64,128]{3,2,1,0:T(8,128)(2,1)S(1)}, u32[]{:S(2)}, u32[]{:S(2)}) async-start(bf16[8,2,64,128]{3,2,1,0:T(8,128)(2,1)} %get-tuple-element.10), calls=%async_computation | async-start | bytes 524288 | tf_op jit(solution)/shard_map/all_to_all | solution.py:286
  18.7 0.0 all-gather.3.cloned.1.call-start
  18.7 0.1 collective-permute-start.3
  18.8 8.7 %collective-permute-done.3.swapped = bf16[2,256,128]{2,1,0:T(8,128)(2,1)S(1)} collective-permute-done((bf16[2,256,128]{2,1,0:T(8,128)(2,1)}, bf16[2,256,128]{2,1,0:T(8,128)(2,1)S(1)}, u32[]{:S(2)}, u32[]{:S(2)}) %collective-permute-start.3) | collective-permute-done | bytes 131104 | tf_op jit(solution)/shard_map/ppermute | solution.py:25
  27.5 2.0 %all-to-all-done.span = bf16[8,2,64,128]{3,2,1,0:T(8,128)(2,1)S(1)} async-done(((bf16[8,2,64,128]{3,2,1,0:T(8,128)(2,1)}), bf16[8,2,64,128]{3,2,1,0:T(8,128)(2,1)S(1)}, u32[]{:S(2)}, u32[]{:S(2)}) %all-to-all-start) | async-done | bytes 262176 | tf_op jit(solution)/shard_map/all_to_all | solution.py:286
  29.5 0.0 copy-done.2
  29.5 0.7 copy-done.1
  30.2 1.9 %pack.1.refs_0_ = bf16[4,2,256,128]{3,2,1,0:T(8,128)(2,1)} custom-call(bf16[2,256,128]{2,1,0:T(8,128)(2,1)} %get-tuple-element.8.own, bf16[2,256,128]{2,1,0:T(8,128)(2,1)} %copy-done.2, bf16[8,2,64,128]{3,2,1,0:T(8,128)(2,1)} %copy-done.1), custom_call_target="tpu_custom_call" | custom-call | tf_op jit(solution)/shard_map/pack/pallas_call | solution.py:85
  32.1 0.0 all-gather.3.cloned.1.call-update
  32.1 0.0 copy-done.4
  32.1 0.0 copy-done.5
  32.1 0.1 pad_add_fusion.3
  32.2 3.2 %collective-permute-start.2 = (s32[4,19]{1,0:T(4,128)S(1)}, s32[4,19]{1,0:T(4,128)S(1)}, u32[]{:S(2)}, u32[]{:S(2)}) collective-permute-start(s32[4,19]{1,0:T(4,128)S(1)} %pad_add_fusion.3), channel_id=1, source_target_pairs={{0,2},{1,3},{2,0},{3,1},{4,6},{5,7},{6,4},{7,5},{8,10},{9,11},{10,... | collective-permute-start | bytes 920 | tf_op jit(solution)/shard_map/ppermute | solution.py:25
  35.4 0.7 collective-permute-start
  36.1 2.6 %collective-permute-start.1 = (s32[4,19]{1,0:T(4,128)S(1)}, s32[4,19]{1,0:T(4,128)S(1)}, u32[]{:S(2)}, u32[]{:S(2)}) collective-permute-start(s32[4,19]{1,0:T(4,128)S(1)} %pad_add_fusion.3), channel_id=1, source_target_pairs={{0,3},{1,0},{2,1},{3,2},{4,7},{5,4},{6,5},{7,6},{8,11},{9,8},{10,9... | collective-permute-start | bytes 920 | tf_op jit(solution)/shard_map/ppermute | solution.py:25
  38.7 0.0 copy-done.6
  38.7 2.3 %by_plane.1 = bf16[8,64,1024]{2,1,0:T(8,128)(2,1)} custom-call(bf16[64,8192]{1,0:T(8,128)(2,1)} %source.1, bf16[4,2,256,128]{3,2,1,0:T(8,128)(2,1)} %pack.1.refs_0_), custom_call_target="tpu_custom_call" | custom-call | tf_op jit(solution)/shard_map/by_plane/pallas_call | solution.py:102
  41.0 5.7 %all-to-all-start.1 = ((bf16[8,64,1024]{2,1,0:T(8,128)(2,1)}), bf16[8,64,1024]{2,1,0:T(8,128)(2,1)S(1)}, u32[]{:S(2)}, u32[]{:S(2)}) async-start(bf16[8,64,1024]{2,1,0:T(8,128)(2,1)} %by_plane.1), calls=%async_computation.1 | async-start | bytes 2097152 | tf_op jit(solution)/shard_map/all_to_all | solution.py:289
  46.8 0.0 collective-permute-done.2
  46.8 0.0 collective-permute-done
  46.8 0.0 collective-permute-done.1
  46.8 0.1 select_reduce_fusion.1
  46.9 0.1 slice.30
  47.0 0.1 copy.20
  47.0 0.1 broadcast_subtract_fusion
  47.1 0.1 and_reduce_fusion
  47.2 0.6 compare_reduce_fusion
  47.8 0.1 fusion.8
  47.9 0.1 copy.26
  48.0 0.1 broadcast_compare_fusion
  48.1 0.1 add_select_fusion
  48.2 0.7 select_n.55.biases
  48.9 0.1 copy.21
  49.0 0.1 broadcast_in_dim.64
  49.1 0.1 pad_add_fusion
  49.2 0.7 reshape.47.picks
  49.9 22.5 %all-to-all-done.1.q_ref = bf16[8,64,1024]{2,1,0:T(8,128)(2,1)S(1)} async-done(((bf16[8,64,1024]{2,1,0:T(8,128)(2,1)}), bf16[8,64,1024]{2,1,0:T(8,128)(2,1)S(1)}, u32[]{:S(2)}, u32[]{:S(2)}) %all-to-all-start.1) | async-done | bytes 1048608 | tf_op jit(solution)/shard_map/all_to_all | solution.py:289
  72.4 37.1 %all-gather.3.cloned.1.call-done = bf16[128,2,256,128]{3,2,1,0:T(8,128)(2,1)} async-done(((bf16[4,2,256,128]{3,2,1,0:T(8,128)(2,1)}), bf16[128,2,256,128]{3,2,1,0:T(8,128)(2,1)}) %all-gather.3.cloned.1.call-update) | async-done | bytes 16777232 | tf_op jit(solution)/shard_map/all_gather | solution.py:288
  109.6 26.1 %attention.1 = bf16[8,64,1024]{2,1,0:T(8,128)(2,1)} custom-call(s32[6]{0:T(128)} %stack.42.place, s32[1280]{0:T(1024)} %reshape.47.picks, f32[1280]{0:T(1024)} %select_n.55.biases, bf16[8,64,1024]{2,1,0:T(8,128)(2,1)} %copy-done, bf16[32,4,2,2,128,128]{5,4,3,2,1,0:T(8,128)(2,1)} %bitcast.46, bf16[32,4,2,4,64,128]{5,4,3,2,1,0:T(8,128)(2,1)} %bitcast.47), custom_call_target="tpu_custom_call" | custom-call | flops 5368709120 | bytes 18874368 | tf_op jit(solution)/shard_map/attention/pallas_call | solution.py:211
  135.7 35.2 %all_to_all.15 = bf16[8,64,1024]{2,1,0:T(8,128)(2,1)S(1)} all-to-all(bf16[8,64,1024]{2,1,0:T(8,128)(2,1)} %attention.1), channel_id=1, replica_groups=mesh['x'=4,'zl'=2,'k'=2,'zh'=4,'y'=4] {'zl','zh'}, dimensions={0} | all-to-all | bytes 2097152 | tf_op jit(solution)/shard_map/all_to_all | solution.py:295
  171.0 0.0 copy-start.3
  171.0 1.0 copy-done.3
  172.0 0.7 fusion
  (22 shorter events, 0.2 us)
Async XLA Ops:
  9.9 22.2 %copy-start.4 = (s32[4,3]{1,0:T(4,128)S(1)}, s32[4,3]{1,0:T(4,128)}, u32[]{:S(2)}) copy-start(s32[4,3]{1,0:T(4,128)} %param.14) | copy-start | bytes 148
  9.9 22.2 %copy-start.5 = (s32[4,16,1]{1,2,0:T(1,128)S(1)}, s32[4,16,1]{1,2,0:T(1,128)}, u32[]{:S(2)}) copy-start(s32[4,16,1]{1,2,0:T(1,128)} %param.13) | copy-start | bytes 772
  9.9 28.8 %copy-start.6 = (s32[4]{0:T(128)S(1)}, s32[4]{0:T(128)}, u32[]{:S(2)}) copy-start(s32[4]{0:T(128)} %constant.95.clone) | copy-start | bytes 52
  9.9 19.5 %all-to-all-start = ((bf16[8,2,64,128]{3,2,1,0:T(8,128)(2,1)}), bf16[8,2,64,128]{3,2,1,0:T(8,128)(2,1)S(1)}, u32[]{:S(2)}, u32[]{:S(2)}) async-start(bf16[8,2,64,128]{3,2,1,0:T(8,128)(2,1)} %get-tuple-element.10), calls=%async_computation | async-start | bytes 524288 | tf_op jit(solution)/shard_map/all_to_all | solution.py:286
  18.7 90.9 %all-gather.3.cloned.1.call-start = ((), (), s32[]{:S(2)}) async-start(), calls=%async_computation.3 | async-start | bytes 17301504 | tf_op jit(solution)/shard_map/all_gather | solution.py:288
  18.7 8.8 %collective-permute-start.3 = (bf16[2,256,128]{2,1,0:T(8,128)(2,1)}, bf16[2,256,128]{2,1,0:T(8,128)(2,1)S(1)}, u32[]{:S(2)}, u32[]{:S(2)}) collective-permute-start(bf16[2,256,128]{2,1,0:T(8,128)(2,1)} %get-tuple-element.9), channel_id=1, source_target_pairs={{0,32},{32,0},{1,33},{33,1},{2,34},{34,2},{3,35},{35,3},{4,36},{36... | collective-permute-start | bytes 393224 | tf_op jit(solution)/shard_map/ppermute | solution.py:25
  27.5 2.0 %copy-start.2 = (bf16[2,256,128]{2,1,0:T(8,128)(2,1)}, bf16[2,256,128]{2,1,0:T(8,128)(2,1)S(1)}, u32[]{:S(2)}) copy-start(bf16[2,256,128]{2,1,0:T(8,128)(2,1)S(1)} %collective-permute-done.3.swapped) | copy-start | bytes 393220
  29.5 0.7 copy-start.1
  32.2 14.5 %collective-permute-start.2 = (s32[4,19]{1,0:T(4,128)S(1)}, s32[4,19]{1,0:T(4,128)S(1)}, u32[]{:S(2)}, u32[]{:S(2)}) collective-permute-start(s32[4,19]{1,0:T(4,128)S(1)} %pad_add_fusion.3), channel_id=1, source_target_pairs={{0,2},{1,3},{2,0},{3,1},{4,6},{5,7},{6,4},{7,5},{8,10},{9,11},{10,... | collective-permute-start | bytes 920 | tf_op jit(solution)/shard_map/ppermute | solution.py:25
  35.4 11.3 %collective-permute-start = (s32[4,19]{1,0:T(4,128)S(1)}, s32[4,19]{1,0:T(4,128)S(1)}, u32[]{:S(2)}, u32[]{:S(2)}) collective-permute-start(s32[4,19]{1,0:T(4,128)S(1)} %pad_add_fusion.3), channel_id=1, source_target_pairs={{0,1},{1,2},{2,3},{3,0},{4,5},{5,6},{6,7},{7,4},{8,9},{9,10},{10,1... | collective-permute-start | bytes 920 | tf_op jit(solution)/shard_map/ppermute | solution.py:25
  36.1 10.7 %collective-permute-start.1 = (s32[4,19]{1,0:T(4,128)S(1)}, s32[4,19]{1,0:T(4,128)S(1)}, u32[]{:S(2)}, u32[]{:S(2)}) collective-permute-start(s32[4,19]{1,0:T(4,128)S(1)} %pad_add_fusion.3), channel_id=1, source_target_pairs={{0,3},{1,0},{2,1},{3,2},{4,7},{5,4},{6,5},{7,6},{8,11},{9,8},{10,9... | collective-permute-start | bytes 920 | tf_op jit(solution)/shard_map/ppermute | solution.py:25
  41.0 31.4 %all-to-all-start.1 = ((bf16[8,64,1024]{2,1,0:T(8,128)(2,1)}), bf16[8,64,1024]{2,1,0:T(8,128)(2,1)S(1)}, u32[]{:S(2)}, u32[]{:S(2)}) async-start(bf16[8,64,1024]{2,1,0:T(8,128)(2,1)} %by_plane.1), calls=%async_computation.1 | async-start | bytes 2097152 | tf_op jit(solution)/shard_map/all_to_all | solution.py:289
  72.4 37.1 %copy-start = (bf16[8,64,1024]{2,1,0:T(8,128)(2,1)}, bf16[8,64,1024]{2,1,0:T(8,128)(2,1)S(1)}, u32[]{:S(2)}) copy-start(bf16[8,64,1024]{2,1,0:T(8,128)(2,1)S(1)} %all-to-all-done.1.q_ref) | copy-start | bytes 3145732
  171.0 1.0 copy-start.3
Sparse Core Ops, SparseCore 0:
  32.2 77.2 all-gather.2

commit v3 on v2

--- a/solution.py
+++ b/solution.py
@@ -16,7 +16,6 @@
 GROUP = H // KVH
 HALF = 64
 NLIST = 20
-LARGEST = 2.0**90
 masked_score = -1e30
 SCALE = DH ** (-0.5) * 1.4426950408889634
 
@@ -42,15 +41,16 @@
     return jax.ShapeDtypeStruct(shape, dtype)
 
 
-def payload_kernel(place, cache_keys, cache_values, span_keys, span_values, own, other, span, sems):
-    start = pl.multiple_of(place[1] * 256, 256)
-    copies = []
-    for i, cache in enumerate((cache_keys, cache_values)):
-        for j, (target, column) in enumerate(((own, place[3]), (other, place[4]))):
-            lanes = pl.ds(pl.multiple_of(column * DH, DH), DH)
-            copies.append(
-                pltpu.make_async_copy(cache.at[pl.ds(start, 256), lanes], target.at[i], sems.at[2 * i + j])
-            )
+def slab_copies(cache_keys, cache_values, plane, target, sems):
+    lanes = pl.ds(pl.multiple_of(plane * DH, DH), DH)
+    return [
+        pltpu.make_async_copy(cache.at[:, lanes], target.at[i], sems.at[i])
+        for i, cache in enumerate((cache_keys, cache_values))
+    ]
+
+
+def payload_kernel(place, cache_keys, cache_values, span_keys, span_values, own, span, sems):
+    copies = slab_copies(cache_keys, cache_values, place[3], own, sems)
     for copy in copies:
         copy.start()
     for i, source in enumerate((span_keys, span_values)):
@@ -63,32 +63,68 @@
 def payload(place, cache_keys, cache_values, span_keys, span_values):
     return pl.pallas_call(
         payload_kernel,
-        out_shape=[shaped((2, 256, DH)), shaped((2, 256, DH)), shaped((8, 2, HALF, DH))],
+        out_shape=[shaped((2, cache_keys.shape[0], DH)), shaped((8, 2, HALF, DH))],
         in_specs=[SMEM, HBM, HBM, VMEM, VMEM],
-        out_specs=[VMEM, VMEM, VMEM],
-        scratch_shapes=[pltpu.SemaphoreType.DMA((4,))],
+        out_specs=[VMEM, VMEM],
+        scratch_shapes=[pltpu.SemaphoreType.DMA((2,))],
         compiler_params=pltpu.CompilerParams(vmem_limit_bytes=56 * 1024 * 1024),
         name="payload",
     )(place, cache_keys, cache_values, span_keys, span_values)
 
 
-def pack_kernel(own, swapped, span, out):
-    for i in range(2):
-        out[0, i] = own[i]
-        out[1, i] = swapped[i]
-        for zl in range(2):
-            for zh in range(4):
-                out[2 + zl, i, zh * HALF : (zh + 1) * HALF] = span[zl * 4 + zh, i]
-
-
-def pack(own, swapped, span):
-    return pl.pallas_call(
-        pack_kernel,
-        out_shape=shaped((4, 2, 256, DH)),
-        in_specs=[VMEM] * 3,
+def neighbour_kernel(place, cache_keys, cache_values, after, other, sems):
+    copies = slab_copies(cache_keys, cache_values, place[4], other, sems)
+    for copy in copies:
+        copy.start()
+    for copy in copies:
+        copy.wait()
+
+
+def neighbour(place, cache_keys, cache_values, after):
+    return pl.pallas_call(
+        neighbour_kernel,
+        out_shape=shaped((2, cache_keys.shape[0], DH)),
+        in_specs=[SMEM, HBM, HBM, HBM],
         out_specs=VMEM,
-        name="pack",
-    )(own, swapped, span)
+        scratch_shapes=[pltpu.SemaphoreType.DMA((2,))],
+        compiler_params=pltpu.CompilerParams(vmem_limit_bytes=56 * 1024 * 1024),
+        name="neighbour",
+    )(place, cache_keys, cache_values, after)
+
+
+def split_kernel(span, table, keys, values):
+    for slot in range(8):
+        keys[slot * HALF : (slot + 1) * HALF] = span[slot, 0]
+        values[slot * HALF : (slot + 1) * HALF] = span[slot, 1]
+    values[8 * HALF :] = table[...]
+
+
+def split(span, table):
+    return pl.pallas_call(
+        split_kernel,
+        out_shape=[shaped((8 * HALF, DH)), shaped((8 * HALF + 16, DH))],
+        in_specs=[VMEM, VMEM],
+        out_specs=[VMEM, VMEM],
+        name="split",
+    )(span, table)
+
+
+def stack_kernel(*refs):
+    keys, values, tables = refs[8:]
+    for slot in range(4):
+        keys[slot] = refs[slot][...]
+        values[slot] = refs[4 + slot][: 8 * HALF]
+        tables[slot] = refs[4 + slot][8 * HALF :]
+
+
+def stack(keys, values):
+    return pl.pallas_call(
+        stack_kernel,
+        out_shape=[shaped((4, 8 * HALF, DH))] * 2 + [shaped((4, 16, DH))],
+        in_specs=[VMEM] * 8,
+        out_specs=[VMEM] * 3,
+        name="stack",
+    )(*keys, *values)
 
 
 def plane_kernel(extra, source, *refs):
@@ -108,7 +144,21 @@
     )(queries, *after)
 
 
+def second_stage(plan, arrays, slots, is_value):
+    x_first = not is_value
+    axis = "y" if x_first else "x"
+    left, right = shift(slots, axis, 4, 1), shift(slots, axis, 4, -1)
+    pieces = [slots, left, right, shift(left, axis, 4, 1)]
+    for array, origin in zip(pieces, ORIGINS):
+        for other in range(2):
+            plan.append((is_value, x_first, origin, other))
+            arrays.append((shift(array, "k", 2, 1) if other else array).reshape(4, 2, 4, HALF, DH))
+
+
 BUFFER = (2, 4, 2, 2, 4, 2, BLK, DH)
+
+
+LARGEST = 2.0**90
 
 
 def attend(exact, place, picks, biases, q_ref, keys, values, out_ref):
@@ -179,20 +229,28 @@
     return lax.fori_loop(0, GROUP * 8 // group, step, jnp.zeros((HALF, BLK), jnp.float32))
 
 
-def attention_kernel(place, picks, biases, q_ref, cached, span, out_ref, kbuf, vbuf, sems):
-    zl = place[5]
+def attention_kernel(plan, place, picks, biases, q_ref, own, other, *refs):
+    pieces = refs[: len(plan)]
+    out_ref, kbuf, vbuf, sems = refs[len(plan) :]
+    my_x, my_y, my_k, zl = place[0], place[1], place[2], place[5]
     copies = []
 
     def copy(source, target):
         copies.append(pltpu.make_async_copy(source, target, sems.at[len(copies)]))
 
-    for i, buffer in enumerate((kbuf, vbuf)):
-        for slot in range(32):
-            x, k, y = slot // 8, slot // 4 % 2, slot % 4
-            copy(cached.at[slot, 0, i], buffer.at[0, x, zl, k, y])
-            copy(cached.at[slot, 1, i], buffer.at[0, x, 1 - zl, k, y])
-            rows = pl.ds(y % 2 * HALF, HALF)
-            copy(span.at[slot, 2:, i], buffer.at[1, x, :, k, :, y // 2, rows, :])
+    for slot in range(8):
+        for i, buffer in enumerate((kbuf, vbuf)):
+            copy(own.at[slot, i], buffer.at[0, slot // 2, zl, slot % 2])
+            copy(other.at[slot, i], buffer.at[0, slot // 2, 1 - zl, slot % 2])
+    for piece, (is_value, x_first, origin, other_k) in zip(pieces, plan):
+        buffer = vbuf if is_value else kbuf
+        for slot, near in enumerate(ORIGINS):
+            dx, dy = (near, origin) if x_first else (origin, near)
+            from_x = lax.rem(my_x + (dx + 4), 4)
+            from_y = lax.rem(my_y + (dy + 4), 4)
+            from_k = 1 - my_k if other_k else my_k
+            rows = pl.ds(pl.multiple_of(lax.rem(from_y, 2) * HALF, HALF), HALF)
+            copy(piece.at[slot], buffer.at[1, from_x, :, from_k, :, lax.div(from_y, 2), rows, :])
     for entry in copies:
         entry.start()
     for entry in copies:
@@ -207,16 +265,16 @@
         attend(True, place, picks, biases, q_ref, keys, values, out_ref)
 
 
-def attention(place, picks, biases, queries, gathered):
-    return pl.pallas_call(
-        attention_kernel,
+def attention(plan, place, picks, biases, queries, own, other, pieces):
+    return pl.pallas_call(
+        functools.partial(attention_kernel, tuple(plan)),
         out_shape=shaped((8, HALF, GROUP * DH)),
-        in_specs=[SMEM, SMEM, SMEM, VMEM, HBM, HBM],
+        in_specs=[SMEM, SMEM, SMEM, VMEM] + [HBM] * (2 + len(pieces)),
         out_specs=VMEM,
         scratch_shapes=[
             pltpu.VMEM(BUFFER, jnp.bfloat16),
             pltpu.VMEM(BUFFER, jnp.bfloat16),
-            pltpu.SemaphoreType.DMA((192,)),
+            pltpu.SemaphoreType.DMA((32 + 4 * len(pieces),)),
         ],
         compiler_params=pltpu.CompilerParams(vmem_limit_bytes=56 * 1024 * 1024),
         cost_estimate=pl.CostEstimate(
@@ -225,14 +283,7 @@
             transcendentals=GROUP * 512 * 2560,
         ),
         name="attention",
-    )(
-        place,
-        picks,
-        biases,
-        queries,
-        gathered.reshape(32, 4, 2, 2, BLK, DH),
-        gathered.reshape(32, 4, 2, 4, HALF, DH),
-    )
+    )(place, picks, biases, queries, own, other, *pieces)
 
 
 def head_table(around, my_y, zl):
@@ -277,21 +328,32 @@
     plane = zh * 2 + zl
     zaxes = ("zl", "zh")
 
-    table = jnp.concatenate([verticals[:, :, 0], slashes], axis=1)
-    table = head_table(jnp.stack(ring_direct(table, "y")), my_y, zl)
+    table = jnp.concatenate([verticals[:, :, 0], slashes], axis=1).astype(jnp.bfloat16)
+    table = jnp.pad(table, ((0, 12), (0, DH - 19)))
     place = jnp.stack([my_x, my_y, my_k, plane, plane + 1 - 2 * zl, zl]).astype(jnp.int32)
 
-    own, other, span = payload(place, cache_keys, cache_values, span_keys, span_values)
-    swapped = shift(other, "zl", 2, 1)
+    own, span = payload(place, cache_keys, cache_values, span_keys, span_values)
     span = lax.all_to_all(span, zaxes, split_axis=0, concat_axis=0, tiled=True)
-    packed = pack(own, swapped, span)
-    gathered = lax.all_gather(packed, ("x", "k", "y"), axis=0, tiled=False)
+
+    def slabs(slab):
+        held = lax.all_gather(slab, ("x", "k"), axis=0, tiled=False)
+        return held.reshape(8, 2, 4, 2, BLK, DH)
+
+    span_k, span_v = split(span, table)
+    span_k, span_v = ring_direct(span_k, "x"), ring_direct(span_v, "y")
+    swapped = shift(neighbour(place, cache_keys, cache_values, span_k[1]), "zl", 2, 1)
+    own, swapped = slabs(own), slabs(swapped)
     slab_queries = lax.all_to_all(
-        by_plane(queries, (packed,)), zaxes, split_axis=0, concat_axis=0, tiled=True
+        by_plane(queries, (span_k[1],)), zaxes, split_axis=0, concat_axis=0, tiled=True
     )
+    span_k, span_v, tables = stack(span_k, span_v)
+    table = head_table(tables[:, :4, :19].astype(jnp.int32), my_y, zl)
+    plan = []
+    pieces = []
+    second_stage(plan, pieces, span_k, False)
+    second_stage(plan, pieces, span_v, True)
     picks, biases = listed_blocks(table, my_x, my_y, my_k)
-
-    attended = attention(place, picks, biases, slab_queries, gathered)
+    attended = attention(plan, place, picks, biases, slab_queries, own, swapped, pieces)
     result = lax.all_to_all(attended, zaxes, split_axis=0, concat_axis=0, tiled=True)
     return jnp.concatenate([result[PLANES.index(p)] for p in range(8)], axis=1)
 

time: 180 us -> 189 us (1.050)
  starting transfers between devices: 21.1 us -> 31.8 us
  waiting for transfers between devices: 70.4 us -> 59.9 us
  Pallas kernels: 33 us -> 36.8 us
  local copies, waits for them, and re-layouts: 4.96 us -> 8.69 us
    ppermute x4 -> x21, waiting for transfers between devices: 8.72 us -> 50.1 us  [shift(): lax.ppermute(value, axis, [(i, (i + step) % size) for i in range(size)])]
    all_gather x1 -> x2, waiting for transfers between devices: 37.1 us -> 0.02 us  [slabs(): held = lax.all_gather(slab, ('x', 'k'), axis=0, tiled=False)]
    all_to_all x1, waiting for transfers between devices: 22.5 us -> 0.01 us  [per_device(): lax.all_to_all(by_plane(queries, (span_k[1],)), zaxes, split_axis=0, conc...]
    ppermute x4 -> x21, starting transfers between devices: 6.59 us -> 18.4 us  [shift(): lax.ppermute(value, axis, [(i, (i + step) % size) for i in range(size)])]
    all_to_all x1, waiting for transfers between devices: 1.97 us -> 9.71 us  [per_device(): span = lax.all_to_all(span, zaxes, split_axis=0, concat_axis=0, tiled=True)]
    pallas_call x3 -> x5, Pallas kernels: 30.8 us -> 34.5 us  [the longest x1 25.1 us: attention(): pl.pallas_call(functools.partial(attention_kernel, tuple(plan)), out_shap...]
    unnamed x21 -> x44, local copies, waits for them, and re-layouts: 1.77 us -> 5.53 us
  transfers between devices with their start and end apart: 7 -> 25, of which waited for: 4 -> 8; matrix products, arithmetic and copies ran while one was open for 2% -> 2% of each run, Pallas kernels for 1% -> 5%
where the time goes in v3:
time: 189 us
  waiting for transfers between devices  59.9 us (32%)
  Pallas kernels  36.8 us (19%)
  blocking collectives  35.1 us (19%)
  starting transfers between devices  31.8 us (17%)
  between operations  13.8 us (7%)
  local copies, waits for them, and re-layouts  8.69 us (5%)
  other arithmetic  2.6 us (1%)
    ppermute x21, waiting for transfers between devices, shift(): lax.ppermute(value, axis, [(i, (i + step) % size) for i in range(size)])  50.1 us
    all_to_all x1, blocking collectives, per_device(): lax.all_to_all(attended, zaxes, split_axis=0, concat_axis=0, tiled=True)  35.1 us
    pallas_call x1, Pallas kernels, attention(): pl.pallas_call(functools.partial(attention_kernel, tuple(plan)), out_shap...  25.1 us
    ppermute x21, starting transfers between devices, shift(): lax.ppermute(value, axis, [(i, (i + step) % size) for i in range(size)])  18.4 us
    all_to_all x1, waiting for transfers between devices, per_device(): span = lax.all_to_all(span, zaxes, split_axis=0, concat_axis=0, tiled=True)  9.71 us
    all_to_all x1, starting transfers between devices, per_device(): span = lax.all_to_all(span, zaxes, split_axis=0, concat_axis=0, tiled=True)  8.58 us
    unnamed x44, local copies, waits for them, and re-layouts  5.53 us
    all_to_all x1, starting transfers between devices, per_device(): lax.all_to_all(by_plane(queries, (span_k[1],)), zaxes, split_axis=0, conc...  4.75 us
  transfers between devices with their start and end apart: 25, of which 8 were waited for; matrix products, arithmetic and copies ran while one was open for 2% of the time, Pallas kernels for 5%

profile of v3, /device:TPU:32, one launch (start us, length us, event | category | flops | bytes accessed | tf_op | source)
XLA Modules:
  0.0 188.6 jit_solution(9253027333956112611)
XLA Ops:
  6.5 0.6 stack.28.place
  7.1 2.9 %payload.1 = (bf16[2,1024,128]{2,1,0:T(8,128)(2,1)}, bf16[8,2,64,128]{3,2,1,0:T(8,128)(2,1)}) custom-call(s32[6]{0:T(128)} %stack.28.place, bf16[1024,1024]{1,0:T(8,128)(2,1)} %cache_keys.3, bf16[1024,1024]{1,0:T(8,128)(2,1)} %cache_values.3, bf16[64,1024]{1,0:T(8,128)(2,1)} %span_keys.1, bf16[64,1024]{1,0:T(8,128)(2,1)} %span_values.1), custom_call_target="tpu_custom_call" | custom-call | tf_op jit(solution)/shard_map/payload/pallas_call | solution.py:64
  10.1 8.6 %all-to-all-start = ((bf16[8,2,64,128]{3,2,1,0:T(8,128)(2,1)}), bf16[8,2,64,128]{3,2,1,0:T(8,128)(2,1)S(1)}, u32[]{:S(2)}, u32[]{:S(2)}) async-start(bf16[8,2,64,128]{3,2,1,0:T(8,128)(2,1)} %get-tuple-element.12), calls=%async_computation | async-start | bytes 524288 | tf_op jit(solution)/shard_map/all_to_all | solution.py:336
  18.7 0.7 fusion.16.table
  19.4 9.7 %all-to-all-done.span = bf16[8,2,64,128]{3,2,1,0:T(8,128)(2,1)S(1)} async-done(((bf16[8,2,64,128]{3,2,1,0:T(8,128)(2,1)}), bf16[8,2,64,128]{3,2,1,0:T(8,128)(2,1)S(1)}, u32[]{:S(2)}, u32[]{:S(2)}) %all-to-all-start) | async-done | bytes 262176 | tf_op jit(solution)/shard_map/all_to_all | solution.py:336
  29.1 0.7 copy-done.2
  29.8 1.7 split.1
  31.5 1.5 collective-permute-start
  33.0 8.2 %collective-permute-done.refs_1_.refs_0_.after = bf16[512,128]{1,0:T(8,128)(2,1)S(1)} collective-permute-done((bf16[512,128]{1,0:T(8,128)(2,1)}, bf16[512,128]{1,0:T(8,128)(2,1)S(1)}, u32[]{:S(2)}, u32[]{:S(2)}) %collective-permute-start) | collective-permute-done | bytes 131104 | tf_op jit(solution)/shard_map/ppermute | solution.py:24
  41.2 0.6 copy-done
  41.8 2.5 %neighbour.1 = bf16[2,1024,128]{2,1,0:T(8,128)(2,1)} custom-call(s32[6]{0:T(128)} %stack.28.place, bf16[1024,1024]{1,0:T(8,128)(2,1)} %cache_keys.3, bf16[1024,1024]{1,0:T(8,128)(2,1)} %cache_values.3, bf16[512,128]{1,0:T(8,128)(2,1)} %copy-done), custom_call_target="tpu_custom_call" | custom-call | tf_op jit(solution)/shard_map/neighbour/pallas_call | solution.py:84
  44.5 11.6 %collective-permute-done.6 = bf16[2,1024,128]{2,1,0:T(8,128)(2,1)S(1)} collective-permute-done((bf16[2,1024,128]{2,1,0:T(8,128)(2,1)}, bf16[2,1024,128]{2,1,0:T(8,128)(2,1)S(1)}, u32[]{:S(2)}, u32[]{:S(2)}) %collective-permute-start.6) | collective-permute-done | bytes 524320 | tf_op jit(solution)/shard_map/ppermute | solution.py:24
  56.0 0.8 copy-done.3
  56.9 1.6 collective-permute-start.3
  58.6 1.7 collective-permute-start.4
  60.2 2.0 %collective-permute-start.5 = (bf16[528,128]{1,0:T(8,128)(2,1)S(1)}, bf16[528,128]{1,0:T(8,128)(2,1)S(1)}, u32[]{:S(2)}, u32[]{:S(2)}) collective-permute-start(bf16[528,128]{1,0:T(8,128)(2,1)S(1)} %copy-done.4), channel_id=1, source_target_pairs={{0,2},{1,3},{2,0},{3,1},{4,6},{5,7},{6,4},{7,5},{8,10},{9,11},{10,... | collective-permute-start | bytes 405512 | tf_op jit(solution)/shard_map/ppermute | solution.py:24
  62.2 1.5 collective-permute-start.1
  63.8 0.7 collective-permute-start.2
  64.5 2.3 %by_plane.1 = bf16[8,64,1024]{2,1,0:T(8,128)(2,1)} custom-call(bf16[64,8192]{1,0:T(8,128)(2,1)} %source.1, bf16[512,128]{1,0:T(8,128)(2,1)} %copy-done), custom_call_target="tpu_custom_call" | custom-call | tf_op jit(solution)/shard_map/by_plane/pallas_call | solution.py:138
  66.7 4.8 %all-to-all-start.1 = ((bf16[8,64,1024]{2,1,0:T(8,128)(2,1)}), bf16[8,64,1024]{2,1,0:T(8,128)(2,1)S(1)}, u32[]{:S(2)}, u32[]{:S(2)}) async-start(bf16[8,64,1024]{2,1,0:T(8,128)(2,1)} %by_plane.1), calls=%async_computation.1 | async-start | bytes 2097152 | tf_op jit(solution)/shard_map/all_to_all | solution.py:346
  71.6 0.6 copy-done.9
  72.3 0.7 copy-done.7
  73.0 2.3 %stack.29 = (bf16[4,512,128]{2,1,0:T(8,128)(2,1)}, bf16[4,512,128]{2,1,0:T(8,128)(2,1)}, bf16[4,16,128]{2,1,0:T(8,128)(2,1)}) custom-call(bf16[512,128]{1,0:T(8,128)(2,1)} %get-tuple-element.13.refs_0_, bf16[512,128]{1,0:T(8,128)(2,1)} %copy-done, bf16[512,128]{1,0:T(8,128)(2,1)} %copy-done.9, bf16[512,128]{1,0:T(8,128)(2,1)} %copy-done.10, ...), custom_call_target="tpu_custom_call" | custom-call | tf_op jit(solution)/shard_map/stack/pallas_call | solution.py:121
  75.3 0.6 collective-permute-start.8
  75.9 2.6 %collective-permute-start.10 = (bf16[4,512,128]{2,1,0:T(8,128)(2,1)}, bf16[4,512,128]{2,1,0:T(8,128)(2,1)S(1)}, u32[]{:S(2)}, u32[]{:S(2)}) collective-permute-start(bf16[4,512,128]{2,1,0:T(8,128)(2,1)} %get-tuple-element.17), channel_id=1, source_target_pairs={{0,3},{1,0},{2,1},{3,2},{4,7},{5,4},{6,5},{7,6},{8,11},{9,8},{10,9... | collective-permute-start | bytes 1572872 | tf_op jit(solution)/shard_map/ppermute | solution.py:24
  78.6 0.9 collective-permute-start.15
  79.4 2.4 %collective-permute-start.17 = (bf16[4,512,128]{2,1,0:T(8,128)(2,1)}, bf16[4,512,128]{2,1,0:T(8,128)(2,1)}, u32[]{:S(2)}, u32[]{:S(2)}) collective-permute-start(bf16[4,512,128]{2,1,0:T(8,128)(2,1)} %get-tuple-element.18), channel_id=1, source_target_pairs={{0,192},{64,0},{128,64},{192,128},{1,193},{65,1},{129,65},{193,129... | collective-permute-start | bytes 1572872 | tf_op jit(solution)/shard_map/ppermute | solution.py:24
  81.8 0.8 fusion.9
  82.9 3.3 %collective-permute-done.8 = bf16[4,512,128]{2,1,0:T(8,128)(2,1)S(1)} collective-permute-done((bf16[4,512,128]{2,1,0:T(8,128)(2,1)}, bf16[4,512,128]{2,1,0:T(8,128)(2,1)S(1)}, u32[]{:S(2)}, u32[]{:S(2)}) %collective-permute-start.8) | collective-permute-done | bytes 524320 | tf_op jit(solution)/shard_map/ppermute | solution.py:24
  86.3 12.4 %collective-permute-done.15 = bf16[4,512,128]{2,1,0:T(8,128)(2,1)S(1)} collective-permute-done((bf16[4,512,128]{2,1,0:T(8,128)(2,1)}, bf16[4,512,128]{2,1,0:T(8,128)(2,1)S(1)}, u32[]{:S(2)}, u32[]{:S(2)}) %collective-permute-start.15) | collective-permute-done | bytes 524320 | tf_op jit(solution)/shard_map/ppermute | solution.py:24
  98.7 1.5 collective-permute-start.12
  100.2 0.3 collective-permute-start.19
  100.5 0.6 compare_reduce_fusion
  101.2 0.1 copy.26
  101.3 0.3 collective-permute-start.16
  101.6 0.3 collective-permute-start.11
  101.9 10.1 %collective-permute-done.12 = bf16[4,512,128]{2,1,0:T(8,128)(2,1)} collective-permute-done((bf16[4,512,128]{2,1,0:T(8,128)(2,1)S(1)}, bf16[4,512,128]{2,1,0:T(8,128)(2,1)}, u32[]{:S(2)}, u32[]{:S(2)}) %collective-permute-start.12) | collective-permute-done | bytes 524320 | tf_op jit(solution)/shard_map/ppermute | solution.py:24
  112.0 3.8 %collective-permute-done.19 = bf16[4,512,128]{2,1,0:T(8,128)(2,1)} collective-permute-done((bf16[4,512,128]{2,1,0:T(8,128)(2,1)S(1)}, bf16[4,512,128]{2,1,0:T(8,128)(2,1)}, u32[]{:S(2)}, u32[]{:S(2)}) %collective-permute-start.19) | collective-permute-done | bytes 524320 | tf_op jit(solution)/shard_map/ppermute | solution.py:24
  115.9 0.5 collective-permute-start.20
  116.5 0.7 select_n.55.biases
  117.2 0.1 copy.21
  117.5 0.7 reshape.95.picks
  118.2 0.6 collective-permute-done.20
  118.9 0.9 copy-done.1
  119.8 25.1 %attention.1 = bf16[8,64,1024]{2,1,0:T(8,128)(2,1)} custom-call(s32[6]{0:T(128)} %stack.28.place, s32[1280]{0:T(1024)} %reshape.95.picks, f32[1280]{0:T(1024)} %select_n.55.biases, bf16[8,64,1024]{2,1,0:T(8,128)(2,1)} %copy-done.1, bf16[8,2,4,2,128,128]{5,4,3,2,1,0:T(8,128)(2,1)} %bitcast.61, bf16[8,2,4,2,128,128]{5,4,3,2,1,0:T(8,128)(2,1)} %bitcast.62, ...), custom_call_target="tpu_custom_call" | custom-call | flops 5368709120 | bytes 18874368 | tf_op jit(solution)/shard_map/attention/pallas_call | solution.py:269
  144.9 35.1 %all_to_all.15 = bf16[8,64,1024]{2,1,0:T(8,128)(2,1)S(1)} all-to-all(bf16[8,64,1024]{2,1,0:T(8,128)(2,1)} %attention.1), channel_id=1, replica_groups=mesh['x'=4,'zl'=2,'k'=2,'zh'=4,'y'=4] {'zl','zh'}, dimensions={0} | all-to-all | bytes 2097152 | tf_op jit(solution)/shard_map/all_to_all | solution.py:357
  180.1 1.0 copy-done.11
  181.1 0.7 fusion
  (86 shorter events, 1.3 us)
Async XLA Ops:
  6.5 12.2 %copy-start.13 = (s32[4,16,1]{1,2,0:T(1,128)S(1)}, s32[4,16,1]{1,2,0:T(1,128)}, u32[]{:S(2)}) copy-start(s32[4,16,1]{1,2,0:T(1,128)} %param.13) | copy-start | bytes 772
  6.5 12.2 %copy-start.12 = (s32[4,3]{1,0:T(4,128)S(1)}, s32[4,3]{1,0:T(4,128)}, u32[]{:S(2)}) copy-start(s32[4,3]{1,0:T(4,128)} %param.14) | copy-start | bytes 148
  6.5 112.3 %all-gather.5.cloned.1.call-start = ((), (), s32[]{:S(2)}) async-start(), calls=%async_computation.3 | async-start | bytes 4718592 | tf_op jit(solution)/shard_map/all_gather | solution.py:339
  10.1 46.8 %copy-start.14 = (s32[4]{0:T(128)S(1)}, s32[4]{0:T(128)}, u32[]{:S(2)}) copy-start(s32[4]{0:T(128)} %constant.97.clone) | copy-start | bytes 52
  10.1 19.0 %all-to-all-start = ((bf16[8,2,64,128]{3,2,1,0:T(8,128)(2,1)}), bf16[8,2,64,128]{3,2,1,0:T(8,128)(2,1)S(1)}, u32[]{:S(2)}, u32[]{:S(2)}) async-start(bf16[8,2,64,128]{3,2,1,0:T(8,128)(2,1)} %get-tuple-element.12), calls=%async_computation | async-start | bytes 524288 | tf_op jit(solution)/shard_map/all_to_all | solution.py:336
  18.7 100.2 %all-gather.7.cloned.1.call-start = ((), (), s32[]{:S(2)}) async-start(), calls=%async_computation.4 | async-start | bytes 4718592 | tf_op jit(solution)/shard_map/all_gather | solution.py:339
  29.1 0.7 copy-start.2
  31.5 25.4 %copy-start.4 = (bf16[528,128]{1,0:T(8,128)(2,1)S(1)}, bf16[528,128]{1,0:T(8,128)(2,1)}, u32[]{:S(2)}) copy-start(bf16[528,128]{1,0:T(8,128)(2,1)} %get-tuple-element.14.refs_4_) | copy-start | bytes 405508
  31.5 30.7 %copy-start.8 = (bf16[512,128]{1,0:T(8,128)(2,1)S(1)}, bf16[512,128]{1,0:T(8,128)(2,1)}, u32[]{:S(2)}) copy-start(bf16[512,128]{1,0:T(8,128)(2,1)} %get-tuple-element.13.refs_0_) | copy-start | bytes 393220
  31.5 9.7 %collective-permute-start = (bf16[512,128]{1,0:T(8,128)(2,1)}, bf16[512,128]{1,0:T(8,128)(2,1)S(1)}, u32[]{:S(2)}, u32[]{:S(2)}) collective-permute-start(bf16[512,128]{1,0:T(8,128)(2,1)} %get-tuple-element.13.refs_0_), channel_id=1, source_target_pairs={{0,64},{64,128},{128,192},{192,0},{1,65},{65,129},{129,193},{193,1... | collective-permute-start | bytes 393224 | tf_op jit(solution)/shard_map/ppermute | solution.py:24
  41.2 0.6 copy-start
  44.4 11.7 %collective-permute-start.6 = (bf16[2,1024,128]{2,1,0:T(8,128)(2,1)}, bf16[2,1024,128]{2,1,0:T(8,128)(2,1)S(1)}, u32[]{:S(2)}, u32[]{:S(2)}) collective-permute-start(bf16[2,1024,128]{2,1,0:T(8,128)(2,1)} %neighbour.1), channel_id=1, source_target_pairs={{0,32},{32,0},{1,33},{33,1},{2,34},{34,2},{3,35},{35,3},{4,36},{36... | collective-permute-start | bytes 1572872 | tf_op jit(solution)/shard_map/ppermute | solution.py:24
  56.0 0.8 copy-start.3
  56.9 14.6 %collective-permute-start.3 = (bf16[528,128]{1,0:T(8,128)(2,1)S(1)}, bf16[528,128]{1,0:T(8,128)(2,1)S(1)}, u32[]{:S(2)}, u32[]{:S(2)}) collective-permute-start(bf16[528,128]{1,0:T(8,128)(2,1)S(1)} %copy-done.4), channel_id=1, source_target_pairs={{0,1},{1,2},{2,3},{3,0},{4,5},{5,6},{6,7},{7,4},{8,9},{9,10},{10,1... | collective-permute-start | bytes 405512 | tf_op jit(solution)/shard_map/ppermute | solution.py:24
  58.6 13.0 %collective-permute-start.4 = (bf16[528,128]{1,0:T(8,128)(2,1)S(1)}, bf16[528,128]{1,0:T(8,128)(2,1)S(1)}, u32[]{:S(2)}, u32[]{:S(2)}) collective-permute-start(bf16[528,128]{1,0:T(8,128)(2,1)S(1)} %copy-done.4), channel_id=1, source_target_pairs={{0,3},{1,0},{2,1},{3,2},{4,7},{5,4},{6,5},{7,6},{8,11},{9,8},{10,9... | collective-permute-start | bytes 405512 | tf_op jit(solution)/shard_map/ppermute | solution.py:24
  60.2 11.4 %collective-permute-start.5 = (bf16[528,128]{1,0:T(8,128)(2,1)S(1)}, bf16[528,128]{1,0:T(8,128)(2,1)S(1)}, u32[]{:S(2)}, u32[]{:S(2)}) collective-permute-start(bf16[528,128]{1,0:T(8,128)(2,1)S(1)} %copy-done.4), channel_id=1, source_target_pairs={{0,2},{1,3},{2,0},{3,1},{4,6},{5,7},{6,4},{7,5},{8,10},{9,11},{10,... | collective-permute-start | bytes 405512 | tf_op jit(solution)/shard_map/ppermute | solution.py:24
  62.2 9.3 %collective-permute-start.1 = (bf16[512,128]{1,0:T(8,128)(2,1)S(1)}, bf16[512,128]{1,0:T(8,128)(2,1)S(1)}, u32[]{:S(2)}, u32[]{:S(2)}) collective-permute-start(bf16[512,128]{1,0:T(8,128)(2,1)S(1)} %copy-done.8), channel_id=1, source_target_pairs={{0,192},{64,0},{128,64},{192,128},{1,193},{65,1},{129,65},{193,129... | collective-permute-start | bytes 393224 | tf_op jit(solution)/shard_map/ppermute | solution.py:24
  63.8 7.8 %collective-permute-start.2 = (bf16[512,128]{1,0:T(8,128)(2,1)S(1)}, bf16[512,128]{1,0:T(8,128)(2,1)S(1)}, u32[]{:S(2)}, u32[]{:S(2)}) collective-permute-start(bf16[512,128]{1,0:T(8,128)(2,1)S(1)} %copy-done.8), channel_id=1, source_target_pairs={{0,128},{64,192},{128,0},{192,64},{1,129},{65,193},{129,1},{193,65... | collective-permute-start | bytes 393224 | tf_op jit(solution)/shard_map/ppermute | solution.py:24
  66.7 52.1 %all-to-all-start.1 = ((bf16[8,64,1024]{2,1,0:T(8,128)(2,1)}), bf16[8,64,1024]{2,1,0:T(8,128)(2,1)S(1)}, u32[]{:S(2)}, u32[]{:S(2)}) async-start(bf16[8,64,1024]{2,1,0:T(8,128)(2,1)} %by_plane.1), calls=%async_computation.1 | async-start | bytes 2097152 | tf_op jit(solution)/shard_map/all_to_all | solution.py:346
  71.5 0.6 copy-start.9
  71.6 0.7 copy-start.10
  71.6 0.7 copy-start.5
  71.6 0.7 copy-start.6
  72.3 0.7 copy-start.7
  75.3 10.9 %collective-permute-start.8 = (bf16[4,512,128]{2,1,0:T(8,128)(2,1)}, bf16[4,512,128]{2,1,0:T(8,128)(2,1)S(1)}, u32[]{:S(2)}, u32[]{:S(2)}) collective-permute-start(bf16[4,512,128]{2,1,0:T(8,128)(2,1)} %get-tuple-element.17), channel_id=1, source_target_pairs={{0,1},{1,2},{2,3},{3,0},{4,5},{5,6},{6,7},{7,4},{8,9},{9,10},{10,1... | collective-permute-start | bytes 1572872 | tf_op jit(solution)/shard_map/ppermute | solution.py:24
  75.9 24.3 %collective-permute-start.10 = (bf16[4,512,128]{2,1,0:T(8,128)(2,1)}, bf16[4,512,128]{2,1,0:T(8,128)(2,1)S(1)}, u32[]{:S(2)}, u32[]{:S(2)}) collective-permute-start(bf16[4,512,128]{2,1,0:T(8,128)(2,1)} %get-tuple-element.17), channel_id=1, source_target_pairs={{0,3},{1,0},{2,1},{3,2},{4,7},{5,4},{6,5},{7,6},{8,11},{9,8},{10,9... | collective-permute-start | bytes 1572872 | tf_op jit(solution)/shard_map/ppermute | solution.py:24
  78.6 20.1 %collective-permute-start.15 = (bf16[4,512,128]{2,1,0:T(8,128)(2,1)}, bf16[4,512,128]{2,1,0:T(8,128)(2,1)S(1)}, u32[]{:S(2)}, u32[]{:S(2)}) collective-permute-start(bf16[4,512,128]{2,1,0:T(8,128)(2,1)} %get-tuple-element.18), channel_id=1, source_target_pairs={{0,64},{64,128},{128,192},{192,0},{1,65},{65,129},{129,193},{193,1... | collective-permute-start | bytes 1572872 | tf_op jit(solution)/shard_map/ppermute | solution.py:24
  79.4 20.8 %collective-permute-start.17 = (bf16[4,512,128]{2,1,0:T(8,128)(2,1)}, bf16[4,512,128]{2,1,0:T(8,128)(2,1)}, u32[]{:S(2)}, u32[]{:S(2)}) collective-permute-start(bf16[4,512,128]{2,1,0:T(8,128)(2,1)} %get-tuple-element.18), channel_id=1, source_target_pairs={{0,192},{64,0},{128,64},{192,128},{1,193},{65,1},{129,65},{193,129... | collective-permute-start | bytes 1572872 | tf_op jit(solution)/shard_map/ppermute | solution.py:24
  81.8 19.5 %collective-permute-start.14 = (bf16[4,512,128]{2,1,0:T(8,128)(2,1)}, bf16[4,512,128]{2,1,0:T(8,128)(2,1)}, u32[]{:S(2)}, u32[]{:S(2)}) collective-permute-start(bf16[4,512,128]{2,1,0:T(8,128)(2,1)} %get-tuple-element.18), channel_id=1, source_target_pairs={{0,16},{16,0},{1,17},{17,1},{2,18},{18,2},{3,19},{19,3},{4,20},{20... | collective-permute-start | bytes 1572872 | tf_op jit(solution)/shard_map/ppermute | solution.py:24
  86.2 32.6 %copy-start.15 = (bf16[4,512,128]{2,1,0:T(8,128)(2,1)}, bf16[4,512,128]{2,1,0:T(8,128)(2,1)S(1)}, u32[]{:S(2)}) copy-start(bf16[4,512,128]{2,1,0:T(8,128)(2,1)S(1)} %collective-permute-done.8) | copy-start | bytes 1572868
  86.2 15.4 %collective-permute-start.7 = (bf16[4,512,128]{2,1,0:T(8,128)(2,1)}, bf16[4,512,128]{2,1,0:T(8,128)(2,1)}, u32[]{:S(2)}, u32[]{:S(2)}) collective-permute-start(bf16[4,512,128]{2,1,0:T(8,128)(2,1)} %get-tuple-element.17), channel_id=1, source_target_pairs={{0,16},{16,0},{1,17},{17,1},{2,18},{18,2},{3,19},{19,3},{4,20},{20... | collective-permute-start | bytes 1572872 | tf_op jit(solution)/shard_map/ppermute | solution.py:24
  98.7 20.2 %copy-start.17 = (bf16[4,512,128]{2,1,0:T(8,128)(2,1)}, bf16[4,512,128]{2,1,0:T(8,128)(2,1)S(1)}, u32[]{:S(2)}) copy-start(bf16[4,512,128]{2,1,0:T(8,128)(2,1)S(1)} %collective-permute-done.15) | copy-start | bytes 1572868
  98.7 13.3 %collective-permute-start.12 = (bf16[4,512,128]{2,1,0:T(8,128)(2,1)S(1)}, bf16[4,512,128]{2,1,0:T(8,128)(2,1)}, u32[]{:S(2)}, u32[]{:S(2)}) collective-permute-start(bf16[4,512,128]{2,1,0:T(8,128)(2,1)S(1)} %collective-permute-done.8), channel_id=1, source_target_pairs={{0,1},{1,2},{2,3},{3,0},{4,5},{5,6},{6,7},{7,4},{8,9},{9,10},{10,1... | collective-permute-start | bytes 1572872 | tf_op jit(solution)/shard_map/ppermute | solution.py:24
  100.2 18.7 %copy-start.16 = (bf16[4,512,128]{2,1,0:T(8,128)(2,1)}, bf16[4,512,128]{2,1,0:T(8,128)(2,1)S(1)}, u32[]{:S(2)}) copy-start(bf16[4,512,128]{2,1,0:T(8,128)(2,1)S(1)} %collective-permute-done.10) | copy-start | bytes 1572868
  100.2 15.7 %collective-permute-start.9 = (bf16[4,512,128]{2,1,0:T(8,128)(2,1)S(1)}, bf16[4,512,128]{2,1,0:T(8,128)(2,1)}, u32[]{:S(2)}, u32[]{:S(2)}) collective-permute-start(bf16[4,512,128]{2,1,0:T(8,128)(2,1)S(1)} %collective-permute-done.8), channel_id=1, source_target_pairs={{0,16},{16,0},{1,17},{17,1},{2,18},{18,2},{3,19},{19,3},{4,20},{20... | collective-permute-start | bytes 1572872 | tf_op jit(solution)/shard_map/ppermute | solution.py:24
  100.2 15.6 %collective-permute-start.19 = (bf16[4,512,128]{2,1,0:T(8,128)(2,1)S(1)}, bf16[4,512,128]{2,1,0:T(8,128)(2,1)}, u32[]{:S(2)}, u32[]{:S(2)}) collective-permute-start(bf16[4,512,128]{2,1,0:T(8,128)(2,1)S(1)} %collective-permute-done.15), channel_id=1, source_target_pairs={{0,64},{64,128},{128,192},{192,0},{1,65},{65,129},{129,193},{193,1... | collective-permute-start | bytes 1572872 | tf_op jit(solution)/shard_map/ppermute | solution.py:24
  101.3 16.9 %collective-permute-start.16 = (bf16[4,512,128]{2,1,0:T(8,128)(2,1)S(1)}, bf16[4,512,128]{2,1,0:T(8,128)(2,1)}, u32[]{:S(2)}, u32[]{:S(2)}) collective-permute-start(bf16[4,512,128]{2,1,0:T(8,128)(2,1)S(1)} %collective-permute-done.15), channel_id=1, source_target_pairs={{0,16},{16,0},{1,17},{17,1},{2,18},{18,2},{3,19},{19,3},{4,20},{20... | collective-permute-start | bytes 1572872 | tf_op jit(solution)/shard_map/ppermute | solution.py:24
  101.6 16.6 %collective-permute-start.11 = (bf16[4,512,128]{2,1,0:T(8,128)(2,1)S(1)}, bf16[4,512,128]{2,1,0:T(8,128)(2,1)}, u32[]{:S(2)}, u32[]{:S(2)}) collective-permute-start(bf16[4,512,128]{2,1,0:T(8,128)(2,1)S(1)} %collective-permute-done.10), channel_id=1, source_target_pairs={{0,16},{16,0},{1,17},{17,1},{2,18},{18,2},{3,19},{19,3},{4,20},{20... | collective-permute-start | bytes 1572872 | tf_op jit(solution)/shard_map/ppermute | solution.py:24
  112.0 6.2 %collective-permute-start.18 = (bf16[4,512,128]{2,1,0:T(8,128)(2,1)}, bf16[4,512,128]{2,1,0:T(8,128)(2,1)}, u32[]{:S(2)}, u32[]{:S(2)}) collective-permute-start(bf16[4,512,128]{2,1,0:T(8,128)(2,1)} %collective-permute-done.17), channel_id=1, source_target_pairs={{0,16},{16,0},{1,17},{17,1},{2,18},{18,2},{3,19},{19,3},{4,20},{20... | collective-permute-start | bytes 1572872 | tf_op jit(solution)/shard_map/ppermute | solution.py:24
  115.9 2.4 %collective-permute-start.13 = (bf16[4,512,128]{2,1,0:T(8,128)(2,1)}, bf16[4,512,128]{2,1,0:T(8,128)(2,1)}, u32[]{:S(2)}, u32[]{:S(2)}) collective-permute-start(bf16[4,512,128]{2,1,0:T(8,128)(2,1)} %collective-permute-done.12), channel_id=1, source_target_pairs={{0,16},{16,0},{1,17},{17,1},{2,18},{18,2},{3,19},{19,3},{4,20},{20... | collective-permute-start | bytes 1572872 | tf_op jit(solution)/shard_map/ppermute | solution.py:24
  115.9 3.0 %collective-permute-start.20 = (bf16[4,512,128]{2,1,0:T(8,128)(2,1)}, bf16[4,512,128]{2,1,0:T(8,128)(2,1)}, u32[]{:S(2)}, u32[]{:S(2)}) collective-permute-start(bf16[4,512,128]{2,1,0:T(8,128)(2,1)} %collective-permute-done.19), channel_id=1, source_target_pairs={{0,16},{16,0},{1,17},{17,1},{2,18},{18,2},{3,19},{19,3},{4,20},{20... | collective-permute-start | bytes 1572872 | tf_op jit(solution)/shard_map/ppermute | solution.py:24
  118.9 1.0 copy-start.1
  180.1 1.0 copy-start.11
Sparse Core Ops, SparseCore 0:
  10.2 40.0 all-gather.4
  57.0 40.1 all-gather.6

commit v4 on v2

--- a/solution.py
+++ b/solution.py
@@ -72,23 +72,49 @@
     )(place, cache_keys, cache_values, span_keys, span_values)
 
 
-def pack_kernel(own, swapped, span, out):
+def pack_kernel(own, swapped, span, out, low, high):
     for i in range(2):
-        out[0, i] = own[i]
-        out[1, i] = swapped[i]
-        for zl in range(2):
-            for zh in range(4):
-                out[2 + zl, i, zh * HALF : (zh + 1) * HALF] = span[zl * 4 + zh, i]
+        out[i] = own[i]
+        out[2 + i] = swapped[i]
+        for zh in range(4):
+            rows = slice(zh * HALF, (zh + 1) * HALF)
+            out[4 + i, rows] = span[i * 4 + zh, 1]
+            (low, high)[i][rows] = span[i * 4 + zh, 0]
 
 
 def pack(own, swapped, span):
     return pl.pallas_call(
         pack_kernel,
-        out_shape=shaped((4, 2, 256, DH)),
+        out_shape=[shaped((6, 256, DH)), shaped((256, DH)), shaped((256, DH))],
         in_specs=[VMEM] * 3,
-        out_specs=VMEM,
+        out_specs=[VMEM] * 3,
         name="pack",
     )(own, swapped, span)
+
+
+def stack_kernel(*refs):
+    for i, source in enumerate(refs[:8]):
+        refs[8 + i // 4][i % 4] = source[...]
+
+
+def stack(low, high):
+    return pl.pallas_call(
+        stack_kernel,
+        out_shape=[shaped((4, 256, DH))] * 2,
+        in_specs=[VMEM] * 8,
+        out_specs=[VMEM] * 2,
+        name="stack",
+    )(*low, *high)
+
+
+def second_stage(plan, arrays, slots, from_zl):
+    axis = "x" if from_zl else "y"
+    left, right = shift(slots, axis, 4, 1), shift(slots, axis, 4, -1)
+    pieces = [slots, left, right, shift(left, axis, 4, 1)]
+    for array, origin in zip(pieces, ORIGINS):
+        for other in range(2):
+            plan.append((from_zl, origin, other))
+            arrays.append((shift(array, "k", 2, 1) if other else array).reshape(4, 4, HALF, DH))
 
 
 def plane_kernel(extra, source, *refs):
@@ -179,20 +205,29 @@
     return lax.fori_loop(0, GROUP * 8 // group, step, jnp.zeros((HALF, BLK), jnp.float32))
 
 
-def attention_kernel(place, picks, biases, q_ref, cached, span, out_ref, kbuf, vbuf, sems):
-    zl = place[5]
+def attention_kernel(plan, place, picks, biases, q_ref, cached, span, *refs):
+    pieces = refs[: len(plan)]
+    out_ref, kbuf, vbuf, sems = refs[len(plan) :]
+    my_x, my_y, my_k, zl = place[0], place[1], place[2], place[5]
     copies = []
 
     def copy(source, target):
         copies.append(pltpu.make_async_copy(source, target, sems.at[len(copies)]))
 
-    for i, buffer in enumerate((kbuf, vbuf)):
-        for slot in range(32):
-            x, k, y = slot // 8, slot // 4 % 2, slot % 4
-            copy(cached.at[slot, 0, i], buffer.at[0, x, zl, k, y])
-            copy(cached.at[slot, 1, i], buffer.at[0, x, 1 - zl, k, y])
-            rows = pl.ds(y % 2 * HALF, HALF)
-            copy(span.at[slot, 2:, i], buffer.at[1, x, :, k, :, y // 2, rows, :])
+    for piece, (from_zl, origin, other) in zip(pieces, plan):
+        for slot, near in enumerate(ORIGINS):
+            dx, dy = (origin, near) if from_zl else (near, origin)
+            from_x = lax.rem(my_x + (dx + 4), 4)
+            from_y = lax.rem(my_y + (dy + 4), 4)
+            from_k = 1 - my_k if other else my_k
+            rows = pl.ds(pl.multiple_of(lax.rem(from_y, 2) * HALF, HALF), HALF)
+            copy(piece.at[slot], kbuf.at[1, from_x, from_zl, from_k, :, lax.div(from_y, 2), rows, :])
+    for slot in range(32):
+        x, k, y = slot // 8, slot // 4 % 2, slot % 4
+        for i, buffer in enumerate((kbuf, vbuf)):
+            copy(cached.at[slot, i], buffer.at[0, x, zl, k, y])
+            copy(cached.at[slot, 2 + i], buffer.at[0, x, 1 - zl, k, y])
+        copy(span.at[slot, 4:], vbuf.at[1, x, :, k, :, y // 2, pl.ds(y % 2 * HALF, HALF), :])
     for entry in copies:
         entry.start()
     for entry in copies:
@@ -207,16 +242,16 @@
         attend(True, place, picks, biases, q_ref, keys, values, out_ref)
 
 
-def attention(place, picks, biases, queries, gathered):
-    return pl.pallas_call(
-        attention_kernel,
+def attention(plan, place, picks, biases, queries, gathered, pieces):
+    return pl.pallas_call(
+        functools.partial(attention_kernel, tuple(plan)),
         out_shape=shaped((8, HALF, GROUP * DH)),
-        in_specs=[SMEM, SMEM, SMEM, VMEM, HBM, HBM],
+        in_specs=[SMEM, SMEM, SMEM, VMEM, HBM, HBM] + [HBM] * len(pieces),
         out_specs=VMEM,
         scratch_shapes=[
             pltpu.VMEM(BUFFER, jnp.bfloat16),
             pltpu.VMEM(BUFFER, jnp.bfloat16),
-            pltpu.SemaphoreType.DMA((192,)),
+            pltpu.SemaphoreType.DMA((160 + 4 * len(pieces),)),
         ],
         compiler_params=pltpu.CompilerParams(vmem_limit_bytes=56 * 1024 * 1024),
         cost_estimate=pl.CostEstimate(
@@ -230,8 +265,9 @@
         picks,
         biases,
         queries,
-        gathered.reshape(32, 4, 2, 2, BLK, DH),
-        gathered.reshape(32, 4, 2, 4, HALF, DH),
+        gathered.reshape(32, 6, 2, BLK, DH),
+        gathered.reshape(32, 6, 4, HALF, DH),
+        *pieces,
     )
 
 
@@ -284,14 +320,19 @@
     own, other, span = payload(place, cache_keys, cache_values, span_keys, span_values)
     swapped = shift(other, "zl", 2, 1)
     span = lax.all_to_all(span, zaxes, split_axis=0, concat_axis=0, tiled=True)
-    packed = pack(own, swapped, span)
+    packed, low, high = pack(own, swapped, span)
     gathered = lax.all_gather(packed, ("x", "k", "y"), axis=0, tiled=False)
     slab_queries = lax.all_to_all(
-        by_plane(queries, (packed,)), zaxes, split_axis=0, concat_axis=0, tiled=True
+        by_plane(queries, (low,)), zaxes, split_axis=0, concat_axis=0, tiled=True
     )
     picks, biases = listed_blocks(table, my_x, my_y, my_k)
 
-    attended = attention(place, picks, biases, slab_queries, gathered)
+    low, high = stack(ring_direct(low, "x"), ring_direct(high, "y"))
+    plan = []
+    pieces = []
+    second_stage(plan, pieces, low, 0)
+    second_stage(plan, pieces, high, 1)
+    attended = attention(plan, place, picks, biases, slab_queries, gathered, pieces)
     result = lax.all_to_all(attended, zaxes, split_axis=0, concat_axis=0, tiled=True)
     return jnp.concatenate([result[PLANES.index(p)] for p in range(8)], axis=1)
 

time: 180 us -> 178 us (0.989)
  waiting for transfers between devices: 70.4 us -> 49.6 us
  starting transfers between devices: 21.1 us -> 37 us
  Pallas kernels: 33 us -> 35.2 us
    ppermute x4 -> x24, waiting for transfers between devices: 8.72 us -> 37.2 us  [shift(): lax.ppermute(value, axis, [(i, (i + step) % size) for i in range(size)])]
    all_gather x1, waiting for transfers between devices: 37.1 us -> 10.4 us  [per_device(): gathered = lax.all_gather(packed, ('x', 'k', 'y'), axis=0, tiled=False)]
    all_to_all x1, waiting for transfers between devices: 22.5 us -> 0.01 us  [per_device(): lax.all_to_all(by_plane(queries, (low,)), zaxes, split_axis=0, concat_axi...]
    ppermute x4 -> x24, starting transfers between devices: 6.59 us -> 22.7 us  [shift(): lax.ppermute(value, axis, [(i, (i + step) % size) for i in range(size)])]
    pallas_call x2 -> x3, Pallas kernels: 28 us -> 30.2 us  [the longest x1 26.4 us: attention(): pl.pallas_call(functools.partial(attention_kernel, tuple(plan)), out_shap...]
  transfers between devices with their start and end apart: 7 -> 27, of which waited for: 4 -> 11; matrix products, arithmetic and copies ran while one was open for 2% -> 2% of each run, Pallas kernels for 1% -> 2%
where the time goes in v4:
time: 178 us
  waiting for transfers between devices  49.6 us (28%)
  starting transfers between devices  37 us (21%)
  Pallas kernels  35.2 us (20%)
  blocking collectives  35.1 us (20%)
  between operations  13.8 us (8%)
  local copies, waits for them, and re-layouts  5.59 us (3%)
    ppermute x24, waiting for transfers between devices, shift(): lax.ppermute(value, axis, [(i, (i + step) % size) for i in range(size)])  37.2 us
    all_to_all x1, blocking collectives, per_device(): lax.all_to_all(attended, zaxes, split_axis=0, concat_axis=0, tiled=True)  35.1 us
    pallas_call x1, Pallas kernels, attention(): pl.pallas_call(functools.partial(attention_kernel, tuple(plan)), out_shap...  26.4 us
    ppermute x24, starting transfers between devices, shift(): lax.ppermute(value, axis, [(i, (i + step) % size) for i in range(size)])  22.7 us
    all_gather x1, waiting for transfers between devices, per_device(): gathered = lax.all_gather(packed, ('x', 'k', 'y'), axis=0, tiled=False)  10.4 us
    all_to_all x1, starting transfers between devices, per_device(): span = lax.all_to_all(span, zaxes, split_axis=0, concat_axis=0, tiled=True)  8.58 us
    all_to_all x1, starting transfers between devices, per_device(): lax.all_to_all(by_plane(queries, (low,)), zaxes, split_axis=0, concat_axi...  5.75 us
  transfers between devices with their start and end apart: 27, of which 11 were waited for; matrix products, arithmetic and copies ran while one was open for 2% of the time, Pallas kernels for 2%

profile of v4, /device:TPU:32, one launch (start us, length us, event | category | flops | bytes accessed | tf_op | source)
XLA Modules:
  0.0 177.6 jit_solution(15516903127456926775)
XLA Ops:
  6.5 0.6 stack.43.place
  7.1 2.8 %payload.1 = (bf16[2,256,128]{2,1,0:T(8,128)(2,1)}, bf16[2,256,128]{2,1,0:T(8,128)(2,1)}, bf16[8,2,64,128]{3,2,1,0:T(8,128)(2,1)}) custom-call(s32[6]{0:T(128)} %stack.43.place, bf16[1024,1024]{1,0:T(8,128)(2,1)} %cache_keys.1, bf16[1024,1024]{1,0:T(8,128)(2,1)} %cache_values.1, bf16[64,1024]{1,0:T(8,128)(2,1)} %span_keys.1, bf16[64,1024]{1,0:T(8,128)(2,1)} %span_values.1), custom_call_target="tpu_custom_call" | custom-call | tf_op jit(solution)/shard_map/payload/pallas_call | solution.py:64
  9.9 8.6 %all-to-all-start = ((bf16[8,2,64,128]{3,2,1,0:T(8,128)(2,1)}), bf16[8,2,64,128]{3,2,1,0:T(8,128)(2,1)S(1)}, u32[]{:S(2)}, u32[]{:S(2)}) async-start(bf16[8,2,64,128]{3,2,1,0:T(8,128)(2,1)} %get-tuple-element.15), calls=%async_computation | async-start | bytes 524288 | tf_op jit(solution)/shard_map/all_to_all | solution.py:322
  18.5 0.1 collective-permute-start.3
  18.6 8.7 %collective-permute-done.3.swapped = bf16[2,256,128]{2,1,0:T(8,128)(2,1)S(1)} collective-permute-done((bf16[2,256,128]{2,1,0:T(8,128)(2,1)}, bf16[2,256,128]{2,1,0:T(8,128)(2,1)S(1)}, u32[]{:S(2)}, u32[]{:S(2)}) %collective-permute-start.3) | collective-permute-done | bytes 131104 | tf_op jit(solution)/shard_map/ppermute | solution.py:25
  27.3 2.0 %all-to-all-done.span = bf16[8,2,64,128]{3,2,1,0:T(8,128)(2,1)S(1)} async-done(((bf16[8,2,64,128]{3,2,1,0:T(8,128)(2,1)}), bf16[8,2,64,128]{3,2,1,0:T(8,128)(2,1)S(1)}, u32[]{:S(2)}, u32[]{:S(2)}) %all-to-all-start) | async-done | bytes 262176 | tf_op jit(solution)/shard_map/all_to_all | solution.py:322
  29.3 0.7 copy-done.1
  30.0 1.9 %pack.1 = (bf16[6,256,128]{2,1,0:T(8,128)(2,1)}, bf16[256,128]{1,0:T(8,128)(2,1)}, bf16[256,128]{1,0:T(8,128)(2,1)}) custom-call(bf16[2,256,128]{2,1,0:T(8,128)(2,1)} %get-tuple-element.13.own, bf16[2,256,128]{2,1,0:T(8,128)(2,1)} %copy-done.12, bf16[8,2,64,128]{3,2,1,0:T(8,128)(2,1)} %copy-done.1), custom_call_target="tpu_custom_call" | custom-call | tf_op jit(solution)/shard_map/pack/pallas_call | solution.py:86
  32.0 3.2 %collective-permute-start.2 = (s32[4,19]{1,0:T(4,128)S(1)}, s32[4,19]{1,0:T(4,128)S(1)}, u32[]{:S(2)}, u32[]{:S(2)}) collective-permute-start(s32[4,19]{1,0:T(4,128)S(1)} %pad_add_fusion.3), channel_id=1, source_target_pairs={{0,2},{1,3},{2,0},{3,1},{4,6},{5,7},{6,4},{7,5},{8,10},{9,11},{10,... | collective-permute-start | bytes 920 | tf_op jit(solution)/shard_map/ppermute | solution.py:25
  35.2 0.7 collective-permute-start
  35.9 2.6 %collective-permute-start.1 = (s32[4,19]{1,0:T(4,128)S(1)}, s32[4,19]{1,0:T(4,128)S(1)}, u32[]{:S(2)}, u32[]{:S(2)}) collective-permute-start(s32[4,19]{1,0:T(4,128)S(1)} %pad_add_fusion.3), channel_id=1, source_target_pairs={{0,3},{1,0},{2,1},{3,2},{4,7},{5,4},{6,5},{7,6},{8,11},{9,8},{10,9... | collective-permute-start | bytes 920 | tf_op jit(solution)/shard_map/ppermute | solution.py:25
  38.5 2.3 %by_plane.1 = bf16[8,64,1024]{2,1,0:T(8,128)(2,1)} custom-call(bf16[64,8192]{1,0:T(8,128)(2,1)} %source.1, bf16[256,128]{1,0:T(8,128)(2,1)} %get-tuple-element.16.refs_0_), custom_call_target="tpu_custom_call" | custom-call | tf_op jit(solution)/shard_map/by_plane/pallas_call | solution.py:128
  40.8 5.7 %all-to-all-start.1 = ((bf16[8,64,1024]{2,1,0:T(8,128)(2,1)}), bf16[8,64,1024]{2,1,0:T(8,128)(2,1)S(1)}, u32[]{:S(2)}, u32[]{:S(2)}) async-start(bf16[8,64,1024]{2,1,0:T(8,128)(2,1)} %by_plane.1), calls=%async_computation.1 | async-start | bytes 2097152 | tf_op jit(solution)/shard_map/all_to_all | solution.py:325
  46.6 0.1 select_reduce_fusion.1
  46.8 0.1 copy.20
  46.9 1.5 collective-permute-start.4
  48.5 1.8 %collective-permute-start.5 = (bf16[256,128]{1,0:T(8,128)(2,1)S(1)}, bf16[256,128]{1,0:T(8,128)(2,1)S(1)}, u32[]{:S(2)}, u32[]{:S(2)}) collective-permute-start(bf16[256,128]{1,0:T(8,128)(2,1)S(1)} %copy-done.11), channel_id=1, source_target_pairs={{0,192},{64,0},{128,64},{192,128},{1,193},{65,1},{129,65},{193,129... | collective-permute-start | bytes 196616 | tf_op jit(solution)/shard_map/ppermute | solution.py:25
  50.3 1.8 %collective-permute-start.6 = (bf16[256,128]{1,0:T(8,128)(2,1)S(1)}, bf16[256,128]{1,0:T(8,128)(2,1)S(1)}, u32[]{:S(2)}, u32[]{:S(2)}) collective-permute-start(bf16[256,128]{1,0:T(8,128)(2,1)S(1)} %copy-done.11), channel_id=1, source_target_pairs={{0,128},{64,192},{128,0},{192,64},{1,129},{65,193},{129,1},{193,65... | collective-permute-start | bytes 196616 | tf_op jit(solution)/shard_map/ppermute | solution.py:25
  52.1 3.2 %collective-permute-start.8 = (bf16[256,128]{1,0:T(8,128)(2,1)S(1)}, bf16[256,128]{1,0:T(8,128)(2,1)S(1)}, u32[]{:S(2)}, u32[]{:S(2)}) collective-permute-start(bf16[256,128]{1,0:T(8,128)(2,1)S(1)} %copy-done.13), channel_id=1, source_target_pairs={{0,3},{1,0},{2,1},{3,2},{4,7},{5,4},{6,5},{7,6},{8,11},{9,8},{10,9... | collective-permute-start | bytes 196616 | tf_op jit(solution)/shard_map/ppermute | solution.py:25
  55.4 0.1 and_reduce_fusion
  55.5 1.3 collective-permute-done.6.refs_3_
  56.8 2.3 %collective-permute-done.7.refs_5_ = bf16[256,128]{1,0:T(8,128)(2,1)S(1)} collective-permute-done((bf16[256,128]{1,0:T(8,128)(2,1)S(1)}, bf16[256,128]{1,0:T(8,128)(2,1)S(1)}, u32[]{:S(2)}, u32[]{:S(2)}) %collective-permute-start.7) | collective-permute-done | bytes 65568 | tf_op jit(solution)/shard_map/ppermute | solution.py:25
  59.0 2.2 %collective-permute-done.9.refs_7_ = bf16[256,128]{1,0:T(8,128)(2,1)S(1)} collective-permute-done((bf16[256,128]{1,0:T(8,128)(2,1)S(1)}, bf16[256,128]{1,0:T(8,128)(2,1)S(1)}, u32[]{:S(2)}, u32[]{:S(2)}) %collective-permute-start.9) | collective-permute-done | bytes 65568 | tf_op jit(solution)/shard_map/ppermute | solution.py:25
  61.2 0.6 copy-done.19
  61.8 1.9 %stack.49 = (bf16[4,256,128]{2,1,0:T(8,128)(2,1)}, bf16[4,256,128]{2,1,0:T(8,128)(2,1)}) custom-call(bf16[256,128]{1,0:T(8,128)(2,1)} %get-tuple-element.16.refs_0_, bf16[256,128]{1,0:T(8,128)(2,1)} %copy-done.14, bf16[256,128]{1,0:T(8,128)(2,1)} %copy-done.15, bf16[256,128]{1,0:T(8,128)(2,1)} %copy-done.16, bf16[256,128]{1,0:T(8,128)(2,1)} %get-tuple-element.18.refs_4_, ...), custom_call_target="tpu_custom_call" | custom-call | tf_op jit(solution)/shard_map/stack/pallas_call | solution.py:101
  63.7 3.2 %collective-permute-start.13 = (bf16[4,256,128]{2,1,0:T(8,128)(2,1)}, bf16[4,256,128]{2,1,0:T(8,128)(2,1)S(1)}, u32[]{:S(2)}, u32[]{:S(2)}) collective-permute-start(bf16[4,256,128]{2,1,0:T(8,128)(2,1)} %get-tuple-element.19), channel_id=1, source_target_pairs={{0,3},{1,0},{2,1},{3,2},{4,7},{5,4},{6,5},{7,6},{8,11},{9,8},{10,9... | collective-permute-start | bytes 786440 | tf_op jit(solution)/shard_map/ppermute | solution.py:25
  67.0 0.7 collective-permute-start.18
  67.7 2.5 %collective-permute-start.20 = (bf16[4,256,128]{2,1,0:T(8,128)(2,1)}, bf16[4,256,128]{2,1,0:T(8,128)(2,1)S(1)}, u32[]{:S(2)}, u32[]{:S(2)}) collective-permute-start(bf16[4,256,128]{2,1,0:T(8,128)(2,1)} %get-tuple-element.20), channel_id=1, source_target_pairs={{0,192},{64,0},{128,64},{192,128},{1,193},{65,1},{129,65},{193,129... | collective-permute-start | bytes 786440 | tf_op jit(solution)/shard_map/ppermute | solution.py:25
  70.2 0.6 compare_reduce_fusion
  70.8 0.1 collective-permute-start.10
  70.9 0.6 collective-permute-done.11
  71.5 5.0 %collective-permute-done.18 = bf16[4,256,128]{2,1,0:T(8,128)(2,1)S(1)} collective-permute-done((bf16[4,256,128]{2,1,0:T(8,128)(2,1)}, bf16[4,256,128]{2,1,0:T(8,128)(2,1)S(1)}, u32[]{:S(2)}, u32[]{:S(2)}) %collective-permute-start.18) | collective-permute-done | bytes 262176 | tf_op jit(solution)/shard_map/ppermute | solution.py:25
  76.5 0.1 collective-permute-start.12
  76.6 3.0 %collective-permute-done.20 = bf16[4,256,128]{2,1,0:T(8,128)(2,1)S(1)} collective-permute-done((bf16[4,256,128]{2,1,0:T(8,128)(2,1)}, bf16[4,256,128]{2,1,0:T(8,128)(2,1)S(1)}, u32[]{:S(2)}, u32[]{:S(2)}) %collective-permute-start.20) | collective-permute-done | bytes 262176 | tf_op jit(solution)/shard_map/ppermute | solution.py:25
  79.7 0.1 copy.26
  80.0 0.1 collective-permute-start.19
  80.1 0.5 collective-permute-start.14
  80.6 10.1 %collective-permute-done.15 = bf16[4,256,128]{2,1,0:T(8,128)(2,1)S(1)} collective-permute-done((bf16[4,256,128]{2,1,0:T(8,128)(2,1)S(1)}, bf16[4,256,128]{2,1,0:T(8,128)(2,1)S(1)}, u32[]{:S(2)}, u32[]{:S(2)}) %collective-permute-start.15) | collective-permute-done | bytes 262176 | tf_op jit(solution)/shard_map/ppermute | solution.py:25
  90.7 4.0 %collective-permute-done.22 = bf16[4,256,128]{2,1,0:T(8,128)(2,1)S(1)} collective-permute-done((bf16[4,256,128]{2,1,0:T(8,128)(2,1)S(1)}, bf16[4,256,128]{2,1,0:T(8,128)(2,1)S(1)}, u32[]{:S(2)}, u32[]{:S(2)}) %collective-permute-start.22) | collective-permute-done | bytes 262176 | tf_op jit(solution)/shard_map/ppermute | solution.py:25
  94.7 0.5 collective-permute-start.23
  95.3 0.7 select_n.55.biases
  96.0 0.1 copy.21
  96.3 0.7 reshape.95.picks
  97.0 10.4 %all-gather.3.cloned.1.call-done = bf16[192,256,128]{2,1,0:T(8,128)(2,1)} async-done(((bf16[6,256,128]{2,1,0:T(8,128)(2,1)}), bf16[192,256,128]{2,1,0:T(8,128)(2,1)}) %all-gather.3.cloned.1.call-update) | async-done | bytes 12582928 | tf_op jit(solution)/shard_map/all_gather | solution.py:324
  107.5 26.4 %attention.1 = bf16[8,64,1024]{2,1,0:T(8,128)(2,1)} custom-call(s32[6]{0:T(128)} %stack.43.place, s32[1280]{0:T(1024)} %reshape.95.picks, f32[1280]{0:T(1024)} %select_n.55.biases, bf16[8,64,1024]{2,1,0:T(8,128)(2,1)} %copy-done, bf16[32,6,2,128,128]{4,3,2,1,0:T(8,128)(2,1)} %bitcast.62, bf16[32,6,4,64,128]{4,3,2,1,0:T(8,128)(2,1)} %bitcast.63, ...), custom_call_target="tpu_custom_call" | custom-call | flops 5368709120 | bytes 18874368 | tf_op jit(solution)/shard_map/attention/pallas_call | solution.py:246
  133.9 35.1 %all_to_all.15 = bf16[8,64,1024]{2,1,0:T(8,128)(2,1)S(1)} all-to-all(bf16[8,64,1024]{2,1,0:T(8,128)(2,1)} %attention.1), channel_id=1, replica_groups=mesh['x'=4,'zl'=2,'k'=2,'zh'=4,'y'=4] {'zl','zh'}, dimensions={0} | all-to-all | bytes 2097152 | tf_op jit(solution)/shard_map/all_to_all | solution.py:336
  169.1 1.0 copy-done.20
  170.1 0.7 fusion
  (97 shorter events, 0.9 us)
Async XLA Ops:
  7.1 24.8 %copy-start.21 = (s32[4,3]{1,0:T(4,128)S(1)}, s32[4,3]{1,0:T(4,128)}, u32[]{:S(2)}) copy-start(s32[4,3]{1,0:T(4,128)} %param.14) | copy-start | bytes 148
  7.1 24.8 %copy-start.22 = (s32[4,16,1]{1,2,0:T(1,128)S(1)}, s32[4,16,1]{1,2,0:T(1,128)}, u32[]{:S(2)}) copy-start(s32[4,16,1]{1,2,0:T(1,128)} %param.13) | copy-start | bytes 772
  7.1 31.4 %copy-start.23 = (s32[4]{0:T(128)S(1)}, s32[4]{0:T(128)}, u32[]{:S(2)}) copy-start(s32[4]{0:T(128)} %constant.95.clone) | copy-start | bytes 52
  9.9 19.4 %all-to-all-start = ((bf16[8,2,64,128]{3,2,1,0:T(8,128)(2,1)}), bf16[8,2,64,128]{3,2,1,0:T(8,128)(2,1)S(1)}, u32[]{:S(2)}, u32[]{:S(2)}) async-start(bf16[8,2,64,128]{3,2,1,0:T(8,128)(2,1)} %get-tuple-element.15), calls=%async_computation | async-start | bytes 524288 | tf_op jit(solution)/shard_map/all_to_all | solution.py:322
  18.5 88.9 %all-gather.3.cloned.1.call-start = ((), (), s32[]{:S(2)}) async-start(), calls=%async_computation.3 | async-start | bytes 12976128 | tf_op jit(solution)/shard_map/all_gather | solution.py:324
  18.5 8.8 %collective-permute-start.3 = (bf16[2,256,128]{2,1,0:T(8,128)(2,1)}, bf16[2,256,128]{2,1,0:T(8,128)(2,1)S(1)}, u32[]{:S(2)}, u32[]{:S(2)}) collective-permute-start(bf16[2,256,128]{2,1,0:T(8,128)(2,1)} %get-tuple-element.14), channel_id=1, source_target_pairs={{0,32},{32,0},{1,33},{33,1},{2,34},{34,2},{3,35},{35,3},{4,36},{36... | collective-permute-start | bytes 393224 | tf_op jit(solution)/shard_map/ppermute | solution.py:25
  27.3 2.0 %copy-start.12 = (bf16[2,256,128]{2,1,0:T(8,128)(2,1)}, bf16[2,256,128]{2,1,0:T(8,128)(2,1)S(1)}, u32[]{:S(2)}) copy-start(bf16[2,256,128]{2,1,0:T(8,128)(2,1)S(1)} %collective-permute-done.3.swapped) | copy-start | bytes 393220
  32.0 14.6 %collective-permute-start.2 = (s32[4,19]{1,0:T(4,128)S(1)}, s32[4,19]{1,0:T(4,128)S(1)}, u32[]{:S(2)}, u32[]{:S(2)}) collective-permute-start(s32[4,19]{1,0:T(4,128)S(1)} %pad_add_fusion.3), channel_id=1, source_target_pairs={{0,2},{1,3},{2,0},{3,1},{4,6},{5,7},{6,4},{7,5},{8,10},{9,11},{10,... | collective-permute-start | bytes 920 | tf_op jit(solution)/shard_map/ppermute | solution.py:25
  35.2 11.4 %collective-permute-start = (s32[4,19]{1,0:T(4,128)S(1)}, s32[4,19]{1,0:T(4,128)S(1)}, u32[]{:S(2)}, u32[]{:S(2)}) collective-permute-start(s32[4,19]{1,0:T(4,128)S(1)} %pad_add_fusion.3), channel_id=1, source_target_pairs={{0,1},{1,2},{2,3},{3,0},{4,5},{5,6},{6,7},{7,4},{8,9},{9,10},{10,1... | collective-permute-start | bytes 920 | tf_op jit(solution)/shard_map/ppermute | solution.py:25
  35.9 10.7 %collective-permute-start.1 = (s32[4,19]{1,0:T(4,128)S(1)}, s32[4,19]{1,0:T(4,128)S(1)}, u32[]{:S(2)}, u32[]{:S(2)}) collective-permute-start(s32[4,19]{1,0:T(4,128)S(1)} %pad_add_fusion.3), channel_id=1, source_target_pairs={{0,3},{1,0},{2,1},{3,2},{4,7},{5,4},{6,5},{7,6},{8,11},{9,8},{10,9... | collective-permute-start | bytes 920 | tf_op jit(solution)/shard_map/ppermute | solution.py:25
  38.5 8.4 %copy-start.11 = (bf16[256,128]{1,0:T(8,128)(2,1)S(1)}, bf16[256,128]{1,0:T(8,128)(2,1)}, u32[]{:S(2)}) copy-start(bf16[256,128]{1,0:T(8,128)(2,1)} %get-tuple-element.16.refs_0_) | copy-start | bytes 196612
  38.5 13.6 %copy-start.13 = (bf16[256,128]{1,0:T(8,128)(2,1)S(1)}, bf16[256,128]{1,0:T(8,128)(2,1)}, u32[]{:S(2)}) copy-start(bf16[256,128]{1,0:T(8,128)(2,1)} %get-tuple-element.18.refs_4_) | copy-start | bytes 196612
  40.8 56.2 %all-to-all-start.1 = ((bf16[8,64,1024]{2,1,0:T(8,128)(2,1)}), bf16[8,64,1024]{2,1,0:T(8,128)(2,1)S(1)}, u32[]{:S(2)}, u32[]{:S(2)}) async-start(bf16[8,64,1024]{2,1,0:T(8,128)(2,1)} %by_plane.1), calls=%async_computation.1 | async-start | bytes 2097152 | tf_op jit(solution)/shard_map/all_to_all | solution.py:325
  46.9 8.4 %collective-permute-start.4 = (bf16[256,128]{1,0:T(8,128)(2,1)S(1)}, bf16[256,128]{1,0:T(8,128)(2,1)S(1)}, u32[]{:S(2)}, u32[]{:S(2)}) collective-permute-start(bf16[256,128]{1,0:T(8,128)(2,1)S(1)} %copy-done.11), channel_id=1, source_target_pairs={{0,64},{64,128},{128,192},{192,0},{1,65},{65,129},{129,193},{193,1... | collective-permute-start | bytes 196616 | tf_op jit(solution)/shard_map/ppermute | solution.py:25
  48.5 7.0 %collective-permute-start.5 = (bf16[256,128]{1,0:T(8,128)(2,1)S(1)}, bf16[256,128]{1,0:T(8,128)(2,1)S(1)}, u32[]{:S(2)}, u32[]{:S(2)}) collective-permute-start(bf16[256,128]{1,0:T(8,128)(2,1)S(1)} %copy-done.11), channel_id=1, source_target_pairs={{0,192},{64,0},{128,64},{192,128},{1,193},{65,1},{129,65},{193,129... | collective-permute-start | bytes 196616 | tf_op jit(solution)/shard_map/ppermute | solution.py:25
  50.3 6.5 %collective-permute-start.6 = (bf16[256,128]{1,0:T(8,128)(2,1)S(1)}, bf16[256,128]{1,0:T(8,128)(2,1)S(1)}, u32[]{:S(2)}, u32[]{:S(2)}) collective-permute-start(bf16[256,128]{1,0:T(8,128)(2,1)S(1)} %copy-done.11), channel_id=1, source_target_pairs={{0,128},{64,192},{128,0},{192,64},{1,129},{65,193},{129,1},{193,65... | collective-permute-start | bytes 196616 | tf_op jit(solution)/shard_map/ppermute | solution.py:25
  52.1 6.9 %collective-permute-start.7 = (bf16[256,128]{1,0:T(8,128)(2,1)S(1)}, bf16[256,128]{1,0:T(8,128)(2,1)S(1)}, u32[]{:S(2)}, u32[]{:S(2)}) collective-permute-start(bf16[256,128]{1,0:T(8,128)(2,1)S(1)} %copy-done.13), channel_id=1, source_target_pairs={{0,1},{1,2},{2,3},{3,0},{4,5},{5,6},{6,7},{7,4},{8,9},{9,10},{10,1... | collective-permute-start | bytes 196616 | tf_op jit(solution)/shard_map/ppermute | solution.py:25
  52.1 6.9 %collective-permute-start.8 = (bf16[256,128]{1,0:T(8,128)(2,1)S(1)}, bf16[256,128]{1,0:T(8,128)(2,1)S(1)}, u32[]{:S(2)}, u32[]{:S(2)}) collective-permute-start(bf16[256,128]{1,0:T(8,128)(2,1)S(1)} %copy-done.13), channel_id=1, source_target_pairs={{0,3},{1,0},{2,1},{3,2},{4,7},{5,4},{6,5},{7,6},{8,11},{9,8},{10,9... | collective-permute-start | bytes 196616 | tf_op jit(solution)/shard_map/ppermute | solution.py:25
  55.3 5.8 %copy-start.14 = (bf16[256,128]{1,0:T(8,128)(2,1)}, bf16[256,128]{1,0:T(8,128)(2,1)S(1)}, u32[]{:S(2)}) copy-start(bf16[256,128]{1,0:T(8,128)(2,1)S(1)} %collective-permute-done.4.refs_1_) | copy-start | bytes 196612
  55.3 5.8 %collective-permute-start.9 = (bf16[256,128]{1,0:T(8,128)(2,1)S(1)}, bf16[256,128]{1,0:T(8,128)(2,1)S(1)}, u32[]{:S(2)}, u32[]{:S(2)}) collective-permute-start(bf16[256,128]{1,0:T(8,128)(2,1)S(1)} %copy-done.13), channel_id=1, source_target_pairs={{0,2},{1,3},{2,0},{3,1},{4,6},{5,7},{6,4},{7,5},{8,10},{9,11},{10,... | collective-permute-start | bytes 196616 | tf_op jit(solution)/shard_map/ppermute | solution.py:25
  55.5 5.7 %copy-start.15 = (bf16[256,128]{1,0:T(8,128)(2,1)}, bf16[256,128]{1,0:T(8,128)(2,1)S(1)}, u32[]{:S(2)}) copy-start(bf16[256,128]{1,0:T(8,128)(2,1)S(1)} %collective-permute-done.5.refs_2_) | copy-start | bytes 196612
  56.8 4.4 %copy-start.16 = (bf16[256,128]{1,0:T(8,128)(2,1)}, bf16[256,128]{1,0:T(8,128)(2,1)S(1)}, u32[]{:S(2)}) copy-start(bf16[256,128]{1,0:T(8,128)(2,1)S(1)} %collective-permute-done.6.refs_3_) | copy-start | bytes 196612
  59.0 2.2 %copy-start.17 = (bf16[256,128]{1,0:T(8,128)(2,1)}, bf16[256,128]{1,0:T(8,128)(2,1)S(1)}, u32[]{:S(2)}) copy-start(bf16[256,128]{1,0:T(8,128)(2,1)S(1)} %collective-permute-done.7.refs_5_) | copy-start | bytes 196612
  59.0 2.2 %copy-start.18 = (bf16[256,128]{1,0:T(8,128)(2,1)}, bf16[256,128]{1,0:T(8,128)(2,1)S(1)}, u32[]{:S(2)}) copy-start(bf16[256,128]{1,0:T(8,128)(2,1)S(1)} %collective-permute-done.8.refs_6_) | copy-start | bytes 196612
  63.7 7.8 %collective-permute-start.11 = (bf16[4,256,128]{2,1,0:T(8,128)(2,1)}, bf16[4,256,128]{2,1,0:T(8,128)(2,1)S(1)}, u32[]{:S(2)}, u32[]{:S(2)}) collective-permute-start(bf16[4,256,128]{2,1,0:T(8,128)(2,1)} %get-tuple-element.19), channel_id=1, source_target_pairs={{0,1},{1,2},{2,3},{3,0},{4,5},{5,6},{6,7},{7,4},{8,9},{9,10},{10,1... | collective-permute-start | bytes 786440 | tf_op jit(solution)/shard_map/ppermute | solution.py:25
  63.7 12.8 %collective-permute-start.13 = (bf16[4,256,128]{2,1,0:T(8,128)(2,1)}, bf16[4,256,128]{2,1,0:T(8,128)(2,1)S(1)}, u32[]{:S(2)}, u32[]{:S(2)}) collective-permute-start(bf16[4,256,128]{2,1,0:T(8,128)(2,1)} %get-tuple-element.19), channel_id=1, source_target_pairs={{0,3},{1,0},{2,1},{3,2},{4,7},{5,4},{6,5},{7,6},{8,11},{9,8},{10,9... | collective-permute-start | bytes 786440 | tf_op jit(solution)/shard_map/ppermute | solution.py:25
  67.0 9.6 %collective-permute-start.18 = (bf16[4,256,128]{2,1,0:T(8,128)(2,1)}, bf16[4,256,128]{2,1,0:T(8,128)(2,1)S(1)}, u32[]{:S(2)}, u32[]{:S(2)}) collective-permute-start(bf16[4,256,128]{2,1,0:T(8,128)(2,1)} %get-tuple-element.20), channel_id=1, source_target_pairs={{0,64},{64,128},{128,192},{192,0},{1,65},{65,129},{129,193},{193,1... | collective-permute-start | bytes 786440 | tf_op jit(solution)/shard_map/ppermute | solution.py:25
  67.7 12.0 %collective-permute-start.20 = (bf16[4,256,128]{2,1,0:T(8,128)(2,1)}, bf16[4,256,128]{2,1,0:T(8,128)(2,1)S(1)}, u32[]{:S(2)}, u32[]{:S(2)}) collective-permute-start(bf16[4,256,128]{2,1,0:T(8,128)(2,1)} %get-tuple-element.20), channel_id=1, source_target_pairs={{0,192},{64,0},{128,64},{192,128},{1,193},{65,1},{129,65},{193,129... | collective-permute-start | bytes 786440 | tf_op jit(solution)/shard_map/ppermute | solution.py:25
  70.8 9.2 %collective-permute-start.10 = (bf16[4,256,128]{2,1,0:T(8,128)(2,1)}, bf16[4,256,128]{2,1,0:T(8,128)(2,1)S(1)}, u32[]{:S(2)}, u32[]{:S(2)}) collective-permute-start(bf16[4,256,128]{2,1,0:T(8,128)(2,1)} %get-tuple-element.19), channel_id=1, source_target_pairs={{0,16},{16,0},{1,17},{17,1},{2,18},{18,2},{3,19},{19,3},{4,20},{20... | collective-permute-start | bytes 786440 | tf_op jit(solution)/shard_map/ppermute | solution.py:25
  71.5 35.9 %copy-start.2 = (bf16[4,256,128]{2,1,0:T(8,128)(2,1)}, bf16[4,256,128]{2,1,0:T(8,128)(2,1)S(1)}, u32[]{:S(2)}) copy-start(bf16[4,256,128]{2,1,0:T(8,128)(2,1)S(1)} %collective-permute-done.11) | copy-start | bytes 786436
  71.5 8.6 %collective-permute-start.17 = (bf16[4,256,128]{2,1,0:T(8,128)(2,1)}, bf16[4,256,128]{2,1,0:T(8,128)(2,1)S(1)}, u32[]{:S(2)}, u32[]{:S(2)}) collective-permute-start(bf16[4,256,128]{2,1,0:T(8,128)(2,1)} %get-tuple-element.20), channel_id=1, source_target_pairs={{0,16},{16,0},{1,17},{17,1},{2,18},{18,2},{3,19},{19,3},{4,20},{20... | collective-permute-start | bytes 786440 | tf_op jit(solution)/shard_map/ppermute | solution.py:25
  76.5 30.9 %copy-start.4 = (bf16[4,256,128]{2,1,0:T(8,128)(2,1)}, bf16[4,256,128]{2,1,0:T(8,128)(2,1)S(1)}, u32[]{:S(2)}) copy-start(bf16[4,256,128]{2,1,0:T(8,128)(2,1)S(1)} %collective-permute-done.18) | copy-start | bytes 786436
  76.5 14.1 %collective-permute-start.15 = (bf16[4,256,128]{2,1,0:T(8,128)(2,1)S(1)}, bf16[4,256,128]{2,1,0:T(8,128)(2,1)S(1)}, u32[]{:S(2)}, u32[]{:S(2)}) collective-permute-start(bf16[4,256,128]{2,1,0:T(8,128)(2,1)S(1)} %collective-permute-done.11), channel_id=1, source_target_pairs={{0,1},{1,2},{2,3},{3,0},{4,5},{5,6},{6,7},{7,4},{8,9},{9,10},{10,1... | collective-permute-start | bytes 786440 | tf_op jit(solution)/shard_map/ppermute | solution.py:25
  76.5 30.9 %copy-start.3 = (bf16[4,256,128]{2,1,0:T(8,128)(2,1)}, bf16[4,256,128]{2,1,0:T(8,128)(2,1)S(1)}, u32[]{:S(2)}) copy-start(bf16[4,256,128]{2,1,0:T(8,128)(2,1)S(1)} %collective-permute-done.13) | copy-start | bytes 786436
  76.5 18.2 %collective-permute-start.12 = (bf16[4,256,128]{2,1,0:T(8,128)(2,1)S(1)}, bf16[4,256,128]{2,1,0:T(8,128)(2,1)S(1)}, u32[]{:S(2)}, u32[]{:S(2)}) collective-permute-start(bf16[4,256,128]{2,1,0:T(8,128)(2,1)S(1)} %collective-permute-done.11), channel_id=1, source_target_pairs={{0,16},{16,0},{1,17},{17,1},{2,18},{18,2},{3,19},{19,3},{4,20},{20... | collective-permute-start | bytes 786440 | tf_op jit(solution)/shard_map/ppermute | solution.py:25
  79.7 27.8 %copy-start.5 = (bf16[4,256,128]{2,1,0:T(8,128)(2,1)}, bf16[4,256,128]{2,1,0:T(8,128)(2,1)S(1)}, u32[]{:S(2)}) copy-start(bf16[4,256,128]{2,1,0:T(8,128)(2,1)S(1)} %collective-permute-done.20) | copy-start | bytes 786436
  79.7 15.0 %collective-permute-start.22 = (bf16[4,256,128]{2,1,0:T(8,128)(2,1)S(1)}, bf16[4,256,128]{2,1,0:T(8,128)(2,1)S(1)}, u32[]{:S(2)}, u32[]{:S(2)}) collective-permute-start(bf16[4,256,128]{2,1,0:T(8,128)(2,1)S(1)} %collective-permute-done.18), channel_id=1, source_target_pairs={{0,64},{64,128},{128,192},{192,0},{1,65},{65,129},{129,193},{193,1... | collective-permute-start | bytes 786440 | tf_op jit(solution)/shard_map/ppermute | solution.py:25
  80.0 27.5 %copy-start.6 = (bf16[4,256,128]{2,1,0:T(8,128)(2,1)}, bf16[4,256,128]{2,1,0:T(8,128)(2,1)S(1)}, u32[]{:S(2)}) copy-start(bf16[4,256,128]{2,1,0:T(8,128)(2,1)S(1)} %collective-permute-done.10) | copy-start | bytes 786436
  80.0 17.0 %collective-permute-start.19 = (bf16[4,256,128]{2,1,0:T(8,128)(2,1)S(1)}, bf16[4,256,128]{2,1,0:T(8,128)(2,1)}, u32[]{:S(2)}, u32[]{:S(2)}) collective-permute-start(bf16[4,256,128]{2,1,0:T(8,128)(2,1)S(1)} %collective-permute-done.18), channel_id=1, source_target_pairs={{0,16},{16,0},{1,17},{17,1},{2,18},{18,2},{3,19},{19,3},{4,20},{20... | collective-permute-start | bytes 786440 | tf_op jit(solution)/shard_map/ppermute | solution.py:25
  80.1 27.4 %copy-start.7 = (bf16[4,256,128]{2,1,0:T(8,128)(2,1)}, bf16[4,256,128]{2,1,0:T(8,128)(2,1)S(1)}, u32[]{:S(2)}) copy-start(bf16[4,256,128]{2,1,0:T(8,128)(2,1)S(1)} %collective-permute-done.17) | copy-start | bytes 786436
  80.1 16.9 %collective-permute-start.14 = (bf16[4,256,128]{2,1,0:T(8,128)(2,1)S(1)}, bf16[4,256,128]{2,1,0:T(8,128)(2,1)}, u32[]{:S(2)}, u32[]{:S(2)}) collective-permute-start(bf16[4,256,128]{2,1,0:T(8,128)(2,1)S(1)} %collective-permute-done.13), channel_id=1, source_target_pairs={{0,16},{16,0},{1,17},{17,1},{2,18},{18,2},{3,19},{19,3},{4,20},{20... | collective-permute-start | bytes 786440 | tf_op jit(solution)/shard_map/ppermute | solution.py:25
  90.7 16.8 %copy-start.8 = (bf16[4,256,128]{2,1,0:T(8,128)(2,1)}, bf16[4,256,128]{2,1,0:T(8,128)(2,1)S(1)}, u32[]{:S(2)}) copy-start(bf16[4,256,128]{2,1,0:T(8,128)(2,1)S(1)} %collective-permute-done.15) | copy-start | bytes 786436
  90.7 6.3 %collective-permute-start.21 = (bf16[4,256,128]{2,1,0:T(8,128)(2,1)S(1)}, bf16[4,256,128]{2,1,0:T(8,128)(2,1)}, u32[]{:S(2)}, u32[]{:S(2)}) collective-permute-start(bf16[4,256,128]{2,1,0:T(8,128)(2,1)S(1)} %collective-permute-done.20), channel_id=1, source_target_pairs={{0,16},{16,0},{1,17},{17,1},{2,18},{18,2},{3,19},{19,3},{4,20},{20... | collective-permute-start | bytes 786440 | tf_op jit(solution)/shard_map/ppermute | solution.py:25
  94.7 12.8 %copy-start.10 = (bf16[4,256,128]{2,1,0:T(8,128)(2,1)}, bf16[4,256,128]{2,1,0:T(8,128)(2,1)S(1)}, u32[]{:S(2)}) copy-start(bf16[4,256,128]{2,1,0:T(8,128)(2,1)S(1)} %collective-permute-done.22) | copy-start | bytes 786436
  94.7 2.3 %collective-permute-start.16 = (bf16[4,256,128]{2,1,0:T(8,128)(2,1)S(1)}, bf16[4,256,128]{2,1,0:T(8,128)(2,1)}, u32[]{:S(2)}, u32[]{:S(2)}) collective-permute-start(bf16[4,256,128]{2,1,0:T(8,128)(2,1)S(1)} %collective-permute-done.15), channel_id=1, source_target_pairs={{0,16},{16,0},{1,17},{17,1},{2,18},{18,2},{3,19},{19,3},{4,20},{20... | collective-permute-start | bytes 786440 | tf_op jit(solution)/shard_map/ppermute | solution.py:25
  94.7 12.8 %copy-start.9 = (bf16[4,256,128]{2,1,0:T(8,128)(2,1)}, bf16[4,256,128]{2,1,0:T(8,128)(2,1)S(1)}, u32[]{:S(2)}) copy-start(bf16[4,256,128]{2,1,0:T(8,128)(2,1)S(1)} %collective-permute-done.12) | copy-start | bytes 786436
  94.7 2.3 %collective-permute-start.23 = (bf16[4,256,128]{2,1,0:T(8,128)(2,1)S(1)}, bf16[4,256,128]{2,1,0:T(8,128)(2,1)}, u32[]{:S(2)}, u32[]{:S(2)}) collective-permute-start(bf16[4,256,128]{2,1,0:T(8,128)(2,1)S(1)} %collective-permute-done.22), channel_id=1, source_target_pairs={{0,16},{16,0},{1,17},{17,1},{2,18},{18,2},{3,19},{19,3},{4,20},{20... | collective-permute-start | bytes 786440 | tf_op jit(solution)/shard_map/ppermute | solution.py:25
  97.0 10.5 %copy-start = (bf16[8,64,1024]{2,1,0:T(8,128)(2,1)}, bf16[8,64,1024]{2,1,0:T(8,128)(2,1)S(1)}, u32[]{:S(2)}) copy-start(bf16[8,64,1024]{2,1,0:T(8,128)(2,1)S(1)} %all-to-all-done.1.q_ref) | copy-start | bytes 3145732
  (3 other events, 2.3 us)
Sparse Core Ops, SparseCore 0:
  32.0 75.3 all-gather.2
